TPU v7x, 32 devices: a whole 2x2x4 slice. The times are simulated.
32 devices in a mesh: ctx: 16 (over z, y, x), fsdp: 2 (over core).
Axes of the slice: x: 2, y: 2, z: 4, core: 2. Of those that a mesh axis runs over, the one named last changes fastest.
Arguments:
- hidden_in: bfloat16 [4, 1024, 2048], P('fsdp', 'ctx'), may hold values from -6 to 6
- positions: int32 [1024], replicated, may hold values from 0 to 1023, as said below
- doc_ids: int32 [4, 1024], P('fsdp'), may hold values from 0 to 2, as said below
- norm_attn: bfloat16 [2048], P(('ctx', 'fsdp')), may hold values from 0.25 to 1.75
- w_query: bfloat16 [2048, 2048], P(('ctx', 'fsdp')), may hold values from -0.25 to 0.25
- key_weight: bfloat16 [2048, 256], P(('ctx', 'fsdp')), may hold values from -0.125 to 0.125
- value_weight: bfloat16 [2048, 256], P(('ctx', 'fsdp')), may hold values from -0.125 to 0.125
- w_out: bfloat16 [2048, 2048], P(('ctx', 'fsdp')), may hold values from -0.5 to 0.5
- norm_mlp: bfloat16 [2048], P(('ctx', 'fsdp')), may hold values from 0.25 to 1.75
- w_gate: bfloat16 [2048, 5632], P(('ctx', 'fsdp')), may hold values from -0.125 to 0.125
- w_up: bfloat16 [2048, 5632], P(('ctx', 'fsdp')), may hold values from -0.125 to 0.125
- w_down: bfloat16 [5632, 2048], P(('ctx', 'fsdp')), may hold values from -0.078125 to 0.078125
- cotangent: bfloat16 [4, 1024, 2048], P('fsdp', 'ctx'), may hold values from -6 to 6
Outputs:
- block_out: bfloat16 [4, 1024, 2048], P('fsdp', 'ctx')
- grad_input: float32 [4, 1024, 2048], P('fsdp', 'ctx')
- grad_norm_attn: float32 [2048], P(('ctx', 'fsdp'))
- grad_query: float32 [2048, 2048], P(('ctx', 'fsdp'))
- grad_key: float32 [2048, 256], P(('ctx', 'fsdp'))
- grad_value: float32 [2048, 256], P(('ctx', 'fsdp'))
- grad_out: float32 [2048, 2048], P(('ctx', 'fsdp'))
- grad_norm_mlp: float32 [2048], P(('ctx', 'fsdp'))
- grad_gate: float32 [2048, 5632], P(('ctx', 'fsdp'))
- grad_up: float32 [2048, 5632], P(('ctx', 'fsdp'))
- grad_down: float32 [5632, 2048], P(('ctx', 'fsdp'))
Inputs may be any that keep to these rules, and one draw needn't show every extreme that they name: On each device of ctx the 64 rows hold, in order, the positions b * 32 to (b + 1) * 32 - 1 and then 1024 - (b + 1) * 32 to 1024 - b * 32 - 1, for a b of that device's own; the positions are a permutation of 0 to 1023. `doc_ids`: each sequence holds three documents, numbered 0, 1, 2 in the order of their positions; document 0 holds more than half of the 1024 positions, and each document at least one.
All inputs are finite; a program needn't handle non-finite values.
Results may differ from a plain program's by a relative error of at most 0.015.
The roundings to bfloat16 on the way count: a program that leaves them out, or rounds other values in their place, can miss the bound.
Values may be sent and summed in bfloat16 or wider, within the bound.
No kernel may reach another device: no remote copies, remote signals or barrier semaphores. Data moves between devices by JAX's collectives and lax.ppermute only.
A program may use at most 448 MiB of HBM per device.

v0:
```python
import math

import jax
import jax.numpy as jnp
from jax import lax
from jax.sharding import PartitionSpec as P

QUERY_HEADS = 32
KEY_VALUE_HEADS = 4
HEAD_WIDTH = 64


epsilon = 1e-05


def rope_tables(positions):
    inverse = 10000.0 ** (-jnp.arange(0, HEAD_WIDTH, 2).astype(jnp.float32) / HEAD_WIDTH)
    angles = positions.astype(jnp.float32)[:, None] * inverse[None, :]
    return (jnp.cos(angles)[:, None, :], jnp.sin(angles)[:, None, :])


def apply_rotation(values, cosine_lookup, sine_lookup):
    half_width = values.shape[-1] // 2
    first_half = values[..., :half_width]
    second_half = values[..., half_width:]
    return jnp.concatenate(
        [
            first_half * cosine_lookup - second_half * sine_lookup,
            second_half * cosine_lookup + first_half * sine_lookup,
        ],
        axis=-1,
    )


def inverse_rotation(upstream, cosine_lookup, sine_lookup):
    half_width = upstream.shape[-1] // 2
    first_half = upstream[..., :half_width]
    second_half = upstream[..., half_width:]
    return jnp.concatenate(
        [
            first_half * cosine_lookup + second_half * sine_lookup,
            second_half * cosine_lookup - first_half * sine_lookup,
        ],
        axis=-1,
    )


def contract_rows(left_side, right_side):
    return lax.dot_general(
        left_side, right_side, (((0,), (0,)), ((), ())), preferred_element_type=jnp.float32
    )


def times_transpose(left_side, right_side):
    return lax.dot_general(
        left_side, right_side, (((1,), (1,)), ((), ())), preferred_element_type=jnp.float32
    )


def norm_back(upstream, values, scaling, gain):
    scaled_grad = upstream * gain
    grad_gain = jnp.sum(upstream * values * scaling, axis=0)
    grad_values = scaling * scaled_grad - values * (scaling * scaling * scaling) * jnp.mean(
        scaled_grad * values, axis=-1, keepdims=True
    )
    return (grad_values, grad_gain)


def attend_forward(bundle):
    queries, all_keys, all_values, visible = bundle
    group_width = QUERY_HEADS // KEY_VALUE_HEADS
    factor = 1.0 / math.sqrt(HEAD_WIDTH)
    outputs = []
    logsums = []
    for key_value_head in range(KEY_VALUE_HEADS):
        query_group = queries[
            :, key_value_head * group_width : (key_value_head + 1) * group_width, :
        ]
        key_head = all_keys[:, key_value_head * HEAD_WIDTH : (key_value_head + 1) * HEAD_WIDTH]
        value_head = all_values[:, key_value_head * HEAD_WIDTH : (key_value_head + 1) * HEAD_WIDTH]
        scores = (
            jnp.einsum("qhd,kd->hqk", query_group, key_head, preferred_element_type=jnp.float32)
            * factor
        )
        scores = jnp.where(visible[None], scores, -1e30)
        maxima = jnp.max(scores, axis=-1, keepdims=True)
        powers = jnp.exp(scores - maxima)
        totals = jnp.sum(powers, axis=-1, keepdims=True)
        chances = (powers / totals).astype(jnp.bfloat16)
        outputs.append(
            jnp.einsum("hqk,kd->qhd", chances, value_head, preferred_element_type=jnp.float32)
        )
        logsums.append(maxima + jnp.log(totals))
    return (jnp.concatenate(outputs, axis=1), jnp.concatenate(logsums, axis=0))


def attend_backward(bundle):
    queries, all_keys, all_values, visible, grad_attended, logsums = bundle
    group_width = QUERY_HEADS // KEY_VALUE_HEADS
    factor = 1.0 / math.sqrt(HEAD_WIDTH)
    grad_queries = []
    grad_keys = []
    grad_values = []
    for key_value_head in range(KEY_VALUE_HEADS):
        heads_here = slice(key_value_head * group_width, (key_value_head + 1) * group_width)
        query_group = queries[:, heads_here, :]
        grad_group = grad_attended[:, heads_here, :]
        key_head = all_keys[:, key_value_head * HEAD_WIDTH : (key_value_head + 1) * HEAD_WIDTH]
        value_head = all_values[:, key_value_head * HEAD_WIDTH : (key_value_head + 1) * HEAD_WIDTH]
        scores = (
            jnp.einsum("qhd,kd->hqk", query_group, key_head, preferred_element_type=jnp.float32)
            * factor
        )
        scores = jnp.where(visible[None], scores, -1e30)
        chances = jnp.exp(scores - logsums[heads_here])
        rounded = chances.astype(jnp.bfloat16)
        grad_chances = jnp.einsum(
            "qhd,kd->hqk", grad_group, value_head, preferred_element_type=jnp.float32
        )
        inner_sum = jnp.sum(chances * grad_chances, axis=-1, keepdims=True)
        grad_scores = (chances * (grad_chances - inner_sum)).astype(jnp.bfloat16)
        grad_queries.append(
            jnp.einsum("hqk,kd->qhd", grad_scores, key_head, preferred_element_type=jnp.float32)
            * factor
        )
        grad_keys.append(
            jnp.einsum("hqk,qhd->kd", grad_scores, query_group, preferred_element_type=jnp.float32)
            * factor
        )
        grad_values.append(
            jnp.einsum("hqk,qhd->kd", rounded, grad_group, preferred_element_type=jnp.float32)
        )
    return (
        jnp.concatenate(grad_queries, axis=1),
        jnp.concatenate(grad_keys, axis=-1),
        jnp.concatenate(grad_values, axis=-1),
    )


def shards(
    hidden_in,
    positions,
    doc_ids,
    norm_attn,
    w_query,
    key_weight,
    value_weight,
    w_out,
    norm_mlp,
    w_gate,
    w_up,
    w_down,
    cotangent,
):
    sequence_count, total_rows, width = hidden_in.shape
    token_ids = sequence_count * total_rows
    start_row = lax.axis_index("ctx") * total_rows
    own_positions = lax.dynamic_slice_in_dim(positions, start_row, total_rows, 0)
    own_docs = lax.dynamic_slice_in_dim(doc_ids, start_row, total_rows, 1)
    visible = (positions[None, None, :] <= own_positions[None, :, None]) & (
        doc_ids[:, None, :] == own_docs[:, :, None]
    )
    cosine_lookup, sine_lookup = rope_tables(own_positions)
    attn_full = (
        lax.all_gather(norm_attn, ("ctx", "fsdp"), axis=0, tiled=True),
        lax.all_gather(w_query, ("ctx", "fsdp"), axis=0, tiled=True),
        lax.all_gather(key_weight, ("ctx", "fsdp"), axis=0, tiled=True),
        lax.all_gather(value_weight, ("ctx", "fsdp"), axis=0, tiled=True),
        lax.all_gather(w_out, ("ctx", "fsdp"), axis=0, tiled=True),
    )
    gain_attn, query_full, key_full, value_full, out_full = attn_full
    inputs = hidden_in.astype(jnp.float32).reshape(token_ids, width)
    scale_attn = lax.rsqrt(jnp.mean(inputs * inputs, axis=-1, keepdims=True) + epsilon)
    gain_attn_wide = gain_attn.astype(jnp.float32)
    normed_attn = (inputs * scale_attn * gain_attn_wide).astype(jnp.bfloat16)
    proj_query = jnp.dot(normed_attn, query_full, preferred_element_type=jnp.float32)
    projected_key = jnp.dot(normed_attn, key_full, preferred_element_type=jnp.float32)
    projected_value = jnp.dot(normed_attn, value_full, preferred_element_type=jnp.float32)
    rot_query = apply_rotation(
        proj_query.reshape(sequence_count, total_rows, QUERY_HEADS, HEAD_WIDTH),
        cosine_lookup,
        sine_lookup,
    ).astype(jnp.bfloat16)
    rot_key = (
        apply_rotation(
            projected_key.reshape(sequence_count, total_rows, KEY_VALUE_HEADS, HEAD_WIDTH),
            cosine_lookup,
            sine_lookup,
        )
        .astype(jnp.bfloat16)
        .reshape(sequence_count, total_rows, KEY_VALUE_HEADS * HEAD_WIDTH)
    )
    value_matrix = projected_value.astype(jnp.bfloat16).reshape(
        sequence_count, total_rows, KEY_VALUE_HEADS * HEAD_WIDTH
    )
    all_keys, all_values = (
        lax.all_gather(rot_key, "ctx", axis=1, tiled=True),
        lax.all_gather(value_matrix, "ctx", axis=1, tiled=True),
    )
    attended, logsums = lax.map(attend_forward, (rot_query, all_keys, all_values, visible))
    attn_rows = attended.astype(jnp.bfloat16).reshape(token_ids, QUERY_HEADS * HEAD_WIDTH)
    middle = inputs + jnp.dot(attn_rows, out_full, preferred_element_type=jnp.float32)
    mlp_full = (
        lax.all_gather(norm_mlp, ("ctx", "fsdp"), axis=0, tiled=True),
        lax.all_gather(w_gate, ("ctx", "fsdp"), axis=0, tiled=True),
        lax.all_gather(w_up, ("ctx", "fsdp"), axis=0, tiled=True),
        lax.all_gather(w_down, ("ctx", "fsdp"), axis=0, tiled=True),
    )
    gain_mlp, gate_full, up_full, down_full = mlp_full
    scale_mlp = lax.rsqrt(jnp.mean(middle * middle, axis=-1, keepdims=True) + epsilon)
    normed_mlp = (middle * scale_mlp * gain_mlp.astype(jnp.float32)).astype(jnp.bfloat16)
    gate_proj = jnp.dot(normed_mlp, gate_full, preferred_element_type=jnp.float32)
    up_proj = jnp.dot(normed_mlp, up_full, preferred_element_type=jnp.float32)
    sigmoid_gate = jax.nn.sigmoid(gate_proj)
    activated = (gate_proj * sigmoid_gate * up_proj).astype(jnp.bfloat16)
    final = middle + jnp.dot(activated, down_full, preferred_element_type=jnp.float32)
    block_out = final.astype(jnp.bfloat16).reshape(sequence_count, total_rows, width)
    upstream = cotangent.reshape(token_ids, width)
    mlp_back = (
        lax.all_gather(norm_mlp, ("ctx", "fsdp"), axis=0, tiled=True),
        lax.all_gather(w_gate, ("ctx", "fsdp"), axis=0, tiled=True),
        lax.all_gather(w_up, ("ctx", "fsdp"), axis=0, tiled=True),
        lax.all_gather(w_down, ("ctx", "fsdp"), axis=0, tiled=True),
    )
    gain_mlp_back, gate_back, up_back, down_back = mlp_back
    grad_activated = times_transpose(upstream, down_back)
    grad_gate_in = (
        grad_activated * up_proj * sigmoid_gate * (1.0 + gate_proj * (1.0 - sigmoid_gate))
    ).astype(jnp.bfloat16)
    grad_up_in = (grad_activated * gate_proj * sigmoid_gate).astype(jnp.bfloat16)
    grad_normed_mlp = times_transpose(grad_gate_in, gate_back) + times_transpose(
        grad_up_in, up_back
    )
    grad_middle_norm, grad_gain_mlp = norm_back(
        grad_normed_mlp, middle, scale_mlp, gain_mlp_back.astype(jnp.float32)
    )
    grad_middle = upstream.astype(jnp.float32) + grad_middle_norm
    mlp_grads = (
        lax.psum_scatter(
            contract_rows(normed_mlp, grad_gate_in),
            ("ctx", "fsdp"),
            scatter_dimension=0,
            tiled=True,
        ),
        lax.psum_scatter(
            contract_rows(normed_mlp, grad_up_in), ("ctx", "fsdp"), scatter_dimension=0, tiled=True
        ),
        lax.psum_scatter(
            contract_rows(activated, upstream), ("ctx", "fsdp"), scatter_dimension=0, tiled=True
        ),
    )
    attn_back = (
        lax.all_gather(norm_attn, ("ctx", "fsdp"), axis=0, tiled=True),
        lax.all_gather(w_query, ("ctx", "fsdp"), axis=0, tiled=True),
        lax.all_gather(key_weight, ("ctx", "fsdp"), axis=0, tiled=True),
        lax.all_gather(value_weight, ("ctx", "fsdp"), axis=0, tiled=True),
        lax.all_gather(w_out, ("ctx", "fsdp"), axis=0, tiled=True),
    )
    gain_attn_back, query_back, key_back, value_back, out_back = attn_back
    grad_branch = grad_middle.astype(jnp.bfloat16)
    grad_out = contract_rows(attn_rows, grad_branch)
    grad_attended = (
        times_transpose(grad_branch, out_back)
        .astype(jnp.bfloat16)
        .reshape(sequence_count, total_rows, QUERY_HEADS, HEAD_WIDTH)
    )
    grad_rot_query, grad_all_keys, grad_all_values = lax.map(
        attend_backward, (rot_query, all_keys, all_values, visible, grad_attended, logsums)
    )
    key_row_gradient, value_row_gradient = (
        lax.psum_scatter(grad_all_keys, "ctx", scatter_dimension=1, tiled=True),
        lax.psum_scatter(grad_all_values, "ctx", scatter_dimension=1, tiled=True),
    )
    grad_query_in = (
        inverse_rotation(grad_rot_query, cosine_lookup, sine_lookup)
        .astype(jnp.bfloat16)
        .reshape(token_ids, QUERY_HEADS * HEAD_WIDTH)
    )
    grad_key_in = (
        inverse_rotation(
            key_row_gradient.reshape(sequence_count, total_rows, KEY_VALUE_HEADS, HEAD_WIDTH),
            cosine_lookup,
            sine_lookup,
        )
        .astype(jnp.bfloat16)
        .reshape(token_ids, KEY_VALUE_HEADS * HEAD_WIDTH)
    )
    value_input_gradient = value_row_gradient.astype(jnp.bfloat16).reshape(
        token_ids, KEY_VALUE_HEADS * HEAD_WIDTH
    )
    grad_query = contract_rows(normed_attn, grad_query_in)
    grad_key = contract_rows(normed_attn, grad_key_in)
    grad_value = contract_rows(normed_attn, value_input_gradient)
    grad_normed_attn = (
        times_transpose(grad_query_in, query_back)
        + times_transpose(grad_key_in, key_back)
        + times_transpose(value_input_gradient, value_back)
    )
    grad_input_norm, grad_gain_attn = norm_back(
        grad_normed_attn, inputs, scale_attn, gain_attn_back.astype(jnp.float32)
    )
    grad_input = (grad_middle + grad_input_norm).reshape(sequence_count, total_rows, width)
    attn_grads = (
        lax.psum_scatter(grad_gain_attn, ("ctx", "fsdp"), scatter_dimension=0, tiled=True),
        lax.psum_scatter(grad_query, ("ctx", "fsdp"), scatter_dimension=0, tiled=True),
        lax.psum_scatter(grad_key, ("ctx", "fsdp"), scatter_dimension=0, tiled=True),
        lax.psum_scatter(grad_value, ("ctx", "fsdp"), scatter_dimension=0, tiled=True),
        lax.psum_scatter(grad_out, ("ctx", "fsdp"), scatter_dimension=0, tiled=True),
        lax.psum_scatter(grad_gain_mlp, ("ctx", "fsdp"), scatter_dimension=0, tiled=True),
    )
    return (
        block_out,
        grad_input,
        attn_grads[0],
        attn_grads[1],
        attn_grads[2],
        attn_grads[3],
        attn_grads[4],
        attn_grads[5],
        mlp_grads[0],
        mlp_grads[1],
        mlp_grads[2],
    )


def solution(mesh):
    in_specs = (
        P("fsdp", "ctx", None),
        P(),
        P("fsdp", None),
        P(("ctx", "fsdp")),
        P(("ctx", "fsdp"), None),
        P(("ctx", "fsdp"), None),
        P(("ctx", "fsdp"), None),
        P(("ctx", "fsdp"), None),
        P(("ctx", "fsdp")),
        P(("ctx", "fsdp"), None),
        P(("ctx", "fsdp"), None),
        P(("ctx", "fsdp"), None),
        P("fsdp", "ctx", None),
    )
    out_specs = (
        P("fsdp", "ctx", None),
        P("fsdp", "ctx", None),
        P(("ctx", "fsdp")),
        P(("ctx", "fsdp"), None),
        P(("ctx", "fsdp"), None),
        P(("ctx", "fsdp"), None),
        P(("ctx", "fsdp"), None),
        P(("ctx", "fsdp")),
        P(("ctx", "fsdp"), None),
        P(("ctx", "fsdp"), None),
        P(("ctx", "fsdp"), None),
    )
    return jax.shard_map(shards, mesh=mesh, in_specs=in_specs, out_specs=out_specs, check_vma=False)
```

profile of v0, /device:TPU:0, one launch (start us, length us, event | category | flops | bytes accessed | tf_op | source)
XLA Modules:
  0.0 3326.1 jit_solution(11883057155312186727)
XLA Ops:
  10.4 42.1 %all-reduce.6 = (bf16[2048]{0:T(1024)(128)(2,1)S(1)}, bf16[2048]{0:T(1024)(128)(2,1)S(1)}) all-reduce(bf16[2048]{0:T(1024)(128)(2,1)S(1)} %dynamic-update-slice, bf16[2048]{0:T(1024)(128)(2,1)S(1)} %dynamic-update-slice.1), channel_id=1, replica_groups=mesh['ctx'=16,'fsdp'=2] {'ctx','fsdp'}, use_global_device_ids=true, to_apply=%add | all-reduce | flops 4096 | bytes 16384
  55.1 12.2 all-gather.10.cloned.1.call-done
  70.1 52.7 %all-gather.14.cloned.1.call-done = bf16[2048,256]{1,0:T(8,128)(2,1)} async-done(((bf16[64,256]{1,0:T(8,128)(2,1)}), bf16[2048,256]{1,0:T(8,128)(2,1)}) %all-gather.14.cloned.1.call-update) | async-done | bytes 1048592 | tf_op jit(solution)/shard_map/all_gather | solution.py:167
  130.0 50.4 %all-gather.12.cloned.1.call-done = bf16[2,1024,256]{2,0,1:T(2,128)(2,1)} async-done(((bf16[2,64,256]{2,0,1:T(2,128)(2,1)}), bf16[2,1024,256]{2,0,1:T(2,128)(2,1)}) %all-gather.12.cloned.1.call-update) | async-done | bytes 1048592 | tf_op jit(solution)/shard_map/all_gather | solution.py:198
  180.4 3.7 copy.69
  184.1 53.6 %all-gather.16.cloned.1.call-done = bf16[2,1024,256]{2,0,1:T(2,128)(2,1)} async-done(((bf16[2,64,256]{2,0,1:T(2,128)(2,1)}), bf16[2,1024,256]{2,0,1:T(2,128)(2,1)}) %all-gather.16.cloned.1.call-update) | async-done | bytes 1048592 | tf_op jit(solution)/shard_map/all_gather | solution.py:197
  237.7 3.7 copy.70
  241.4 75.3 %all-gather.18.cloned.1.call-done = bf16[2048,2048]{1,0:T(8,128)(2,1)} async-done(((bf16[64,2048]{1,0:T(8,128)(2,1)}), bf16[2048,2048]{1,0:T(8,128)(2,1)}) %all-gather.18.cloned.1.call-update) | async-done | bytes 8388624 | tf_op jit(solution)/shard_map/all_gather | solution.py:166
  316.7 12.4 copy.68
  329.1 5.0 fusion.75
  336.0 19.6 while.28
  355.6 1.9 copy.72
  358.3 37.2 %all-gather.20.cloned.1.call-done = bf16[2048,2048]{1,0:T(8,128)(2,1)} async-done(((bf16[64,2048]{1,0:T(8,128)(2,1)}), bf16[2048,2048]{1,0:T(8,128)(2,1)}) %all-gather.20.cloned.1.call-update) | async-done | bytes 8388624 | tf_op jit(solution)/shard_map/all_gather | solution.py:169
  395.5 4.8 multiply_reduce_fusion.2
  400.5 141.1 %all-gather.22.cloned.1.call-done = bf16[2048,5632]{1,0:T(8,128)(2,1)} async-done(((bf16[64,5632]{1,0:T(8,128)(2,1)}), bf16[2048,5632]{1,0:T(8,128)(2,1)}) %all-gather.22.cloned.1.call-update) | async-done | bytes 23068688 | tf_op jit(solution)/shard_map/all_gather | solution.py:205
  541.6 12.3 fusion.87
  553.9 133.3 %all-gather.24.cloned.1.call-done = bf16[2048,5632]{1,0:T(8,128)(2,1)} async-done(((bf16[64,5632]{1,0:T(8,128)(2,1)}), bf16[2048,5632]{1,0:T(8,128)(2,1)}) %all-gather.24.cloned.1.call-update) | async-done | bytes 23068688 | tf_op jit(solution)/shard_map/all_gather | solution.py:206
  687.2 12.3 fusion.88
  699.5 133.4 %all-gather.26.cloned.1.call-done = bf16[5632,2048]{1,0:T(8,128)(2,1)} async-done(((bf16[176,2048]{1,0:T(8,128)(2,1)}), bf16[5632,2048]{1,0:T(8,128)(2,1)}) %all-gather.26.cloned.1.call-update) | async-done | bytes 23068688 | tf_op jit(solution)/shard_map/all_gather | solution.py:207
  832.9 14.6 multiply_convert_fusion
  847.5 13.8 fusion.89
  861.3 13.1 multiply_reduce_fusion
  875.8 6.3 convolution_convert_fusion
  882.0 2.1 reshape.366
  884.1 105.5 %while.29 = (s32[]{:T(128)}, f32[2,64,32,64]{1,3,2,0:T(8,128)}, f32[2,1024,256]{2,0,1:T(2,128)}, f32[2,1024,256]{2,1,0:T(8,128)}, bf16[2,1024,256]{1,2,0:T(8,128...) while((s32[]{:T(128)}, f32[2,64,32,64]{1,3,2,0:T(8,128)}, ...), condition=%wide.region_18.19_spmd.clone, body=%wide.region_13.18_spmd.sunk.clone | while | flops 1363408896 | bytes 159302144 | solution.py:267
  889.9 2.5 fusion.287
  906.5 3.6 copy.111
  910.1 21.7 dynamic_update_slice.36
  942.6 2.5 fusion.287
  959.1 3.6 copy.111
  962.7 21.7 dynamic_update_slice.36
  991.7 122.2 %all-reduce.9.cloned.1.call-done = f32[2,1024,256]{2,0,1:T(2,128)} async-done(((f32[2,1024,256]{2,0,1:T(2,128)}), f32[2,1024,256]{2,0,1:T(2,128)}) %all-reduce.9.cloned.1.call-update) | async-done | bytes 2097168
  1117.3 78.9 %reduce-scatter.9.cloned.1.call-done = f32[2,64,256]{2,1,0:T(8,128)} async-done(((f32[2,1024,256]{2,1,0:T(8,128)}), f32[2,64,256]{2,1,0:T(8,128)}) %reduce-scatter.9.cloned.1.call-update) | async-done | bytes 131088 | tf_op jit(solution)/shard_map/reduce_scatter | solution.py:272
  1197.7 1.8 convolution_bitcast_fusion.12
  1202.9 8.2 fusion.91
  1212.4 8.2 fusion.79
  1222.2 17.9 fusion.93
  1241.4 18.1 fusion.94
  1261.0 17.9 fusion.95
  1279.5 6.3 fusion.90
  1285.8 11.7 fusion.63
  1299.6 37.1 %all-reduce.5 = (f32[2048]{0:T(1024)S(1)}, f32[2048]{0:T(1024)S(1)}) all-reduce(f32[2048]{0:T(1024)S(1)} %get-tuple-element.161, f32[2048]{0:T(1024)S(1)} %copy-done.43), channel_id=4, replica_groups=mesh['ctx'=16,'fsdp'=2] {'ctx','fsdp'}, use_global_device_ids=true, to_apply=%region_23.24.clone | all-reduce | flops 4096 | bytes 32768
  1339.2 129.2 %reduce-scatter.15.cloned.1.call-done = f32[64,256]{1,0:T(8,128)} async-done(((f32[2048,256]{1,0:T(8,128)}), f32[64,256]{1,0:T(8,128)}) %reduce-scatter.15.cloned.1.call-update) | async-done | bytes 65552 | tf_op jit(solution)/shard_map/reduce_scatter | solution.py:307
  1468.4 181.7 %reduce-scatter.11.cloned.1.call-done = f32[64,2048]{1,0:T(8,128)} async-done(((f32[2048,2048]{1,0:T(8,128)}), f32[64,2048]{1,0:T(8,128)}) %reduce-scatter.11.cloned.1.call-update) | async-done | bytes 524304 | tf_op jit(solution)/shard_map/reduce_scatter | solution.py:305
  1650.2 187.3 %reduce-scatter.17.cloned.1.call-done = f32[64,2048]{1,0:T(8,128)} async-done(((f32[2048,2048]{1,0:T(8,128)}), f32[64,2048]{1,0:T(8,128)}) %reduce-scatter.17.cloned.1.call-update) | async-done | bytes 524304 | tf_op jit(solution)/shard_map/reduce_scatter | solution.py:308
  1837.5 489.5 %reduce-scatter.19.cloned.1.call-done = f32[64,5632]{1,0:T(8,128)} async-done(((f32[2048,5632]{1,0:T(8,128)}), f32[64,5632]{1,0:T(8,128)}) %reduce-scatter.19.cloned.1.call-update) | async-done | bytes 1441808 | tf_op jit(solution)/shard_map/reduce_scatter | solution.py:239
  2327.0 495.9 %reduce-scatter.21.cloned.1.call-done = f32[64,5632]{1,0:T(8,128)} async-done(((f32[2048,5632]{1,0:T(8,128)}), f32[64,5632]{1,0:T(8,128)}) %reduce-scatter.21.cloned.1.call-update) | async-done | bytes 1441808 | tf_op jit(solution)/shard_map/reduce_scatter | solution.py:245
  2822.9 495.9 %reduce-scatter.23.cloned.1.call-done = f32[176,2048]{1,0:T(8,128)} async-done(((f32[5632,2048]{1,0:T(8,128)}), f32[176,2048]{1,0:T(8,128)}) %reduce-scatter.23.cloned.1.call-update) | async-done | bytes 1441808 | tf_op jit(solution)/shard_map/reduce_scatter | solution.py:248
  (324 shorter events, 108.6 us)
Async XLA Ops:
  7.2 62.7 %copy-start.11 = (bf16[2,64,2048]{2,1,0:T(8,128)(2,1)S(1)}, bf16[2,64,2048]{2,1,0:T(8,128)(2,1)}, u32[]{:S(2)}) copy-start(bf16[2,64,2048]{2,1,0:T(8,128)(2,1)} %param.17) | copy-start | bytes 1572868
  7.2 62.4 %copy-start.45 = (s32[1024]{0:T(1024)S(1)}, s32[1024]{0:T(1024)}, u32[]{:S(2)}) copy-start(s32[1024]{0:T(1024)} %param.18) | copy-start | bytes 12292
  7.2 60.1 %all-gather.10.cloned.1.call-start = ((), (), s32[]{:S(2)}) async-start(), calls=%async_computation.8 | async-start | bytes 1081344 | tf_op jit(solution)/shard_map/all_gather | solution.py:168
  7.9 114.9 %all-gather.14.cloned.1.call-start = ((), (), s32[]{:S(2)}) async-start(), calls=%async_computation.10 | async-start | bytes 1081344 | tf_op jit(solution)/shard_map/all_gather | solution.py:167
  8.7 171.7 %all-gather.12.cloned.1.call-start = ((), (), s32[]{:S(2)}) async-start(), calls=%async_computation.9 | async-start | bytes 1114112 | tf_op jit(solution)/shard_map/all_gather | solution.py:198
  52.6 17.5 copy-start.41
  53.9 70.4 %copy-start.46 = (f32[128]{0:T(128)}, f32[128]{0:T(128)S(1)}, u32[]{:S(2)}) copy-start(f32[128]{0:T(128)S(1)} %rsqrt.27) | copy-start | bytes 1540
  69.6 168.2 %all-gather.16.cloned.1.call-start = ((), (), s32[]{:S(2)}) async-start(), calls=%async_computation.11 | async-start | bytes 1114112 | tf_op jit(solution)/shard_map/all_gather | solution.py:197
  69.9 264.2 %copy-start.37 = (f32[64,32]{0,1:T(8,128)}, f32[64,32]{0,1:T(8,128)S(1)}, u32[]{:S(2)}) copy-start(f32[64,32]{0,1:T(8,128)S(1)} %get-tuple-element.238) | copy-start | bytes 24580
  69.9 264.2 %copy-start.39 = (f32[64,32]{0,1:T(8,128)}, f32[64,32]{0,1:T(8,128)S(1)}, u32[]{:S(2)}) copy-start(f32[64,32]{0,1:T(8,128)S(1)} %get-tuple-element.239) | copy-start | bytes 24580
  70.1 259.0 %copy-start.22 = (bf16[2,64,2048]{2,1,0:T(8,128)(2,1)}, bf16[2,64,2048]{2,1,0:T(8,128)(2,1)S(1)}, u32[]{:S(2)}) copy-start(bf16[2,64,2048]{2,1,0:T(8,128)(2,1)S(1)} %fusion.66) | copy-start | bytes 1572868
  124.8 4.6 copy-start.44
  125.6 191.1 %all-gather.18.cloned.1.call-start = ((), (), s32[]{:S(2)}) async-start(), calls=%async_computation.12 | async-start | bytes 8650752 | tf_op jit(solution)/shard_map/all_gather | solution.py:166
  126.2 269.3 %all-gather.20.cloned.1.call-start = ((), (), s32[]{:S(2)}) async-start(), calls=%async_computation.13 | async-start | bytes 8650752 | tf_op jit(solution)/shard_map/all_gather | solution.py:169
  126.8 414.8 %all-gather.22.cloned.1.call-start = ((), (), s32[]{:S(2)}) async-start(), calls=%async_computation.14 | async-start | bytes 23789568 | tf_op jit(solution)/shard_map/all_gather | solution.py:205
  127.6 559.7 %all-gather.24.cloned.1.call-start = ((), (), s32[]{:S(2)}) async-start(), calls=%async_computation.15 | async-start | bytes 23789568 | tf_op jit(solution)/shard_map/all_gather | solution.py:206
  128.3 704.6 %all-gather.26.cloned.1.call-start = ((), (), s32[]{:S(2)}) async-start(), calls=%async_computation.16 | async-start | bytes 23789568 | tf_op jit(solution)/shard_map/all_gather | solution.py:207
  129.0 984.8 %all-reduce.9.cloned.1.call-start = ((), (), s32[]{:S(2)}) async-start(), calls=%async_computation.25 | async-start | bytes 4194304
  358.3 42.0 %copy-start.24 = (bf16[128,2048]{1,0:T(8,128)(2,1)}, bf16[128,2048]{1,0:T(8,128)(2,1)S(1)}, u32[]{:S(2)}) copy-start(bf16[128,2048]{1,0:T(8,128)(2,1)S(1)} %reshape.363) | copy-start | bytes 1572868
  400.3 474.1 %copy-start.9 = (f32[128,2048]{1,0:T(8,128)}, f32[128,2048]{1,0:T(8,128)S(1)}, u32[]{:S(2)}) copy-start(f32[128,2048]{1,0:T(8,128)S(1)} %get-tuple-element.243) | copy-start | bytes 3145732
  400.5 286.7 %copy-start.15 = (bf16[128,2048]{1,0:T(8,128)(2,1)}, bf16[128,2048]{1,0:T(8,128)(2,1)S(1)}, u32[]{:S(2)}) copy-start(bf16[128,2048]{1,0:T(8,128)(2,1)S(1)} %multiply_convert_fusion.3) | copy-start | bytes 1572868
  553.9 279.0 %copy-start.28 = (bf16[2,64,2048]{2,1,0:T(8,128)(2,1)S(1)}, bf16[2,64,2048]{2,1,0:T(8,128)(2,1)}, u32[]{:S(2)}) copy-start(bf16[2,64,2048]{2,1,0:T(8,128)(2,1)} %param.29) | copy-start | bytes 1572868
  847.5 13.8 copy-start.17
  847.5 13.8 copy-start.19
  885.5 3.3 copy-start.7
  889.9 2.5 copy-start.6
  901.3 2.3 copy-start.30
  931.8 2.2 copy-start.3
  938.2 3.3 copy-start.7
  942.5 2.5 copy-start.6
  953.9 2.3 copy-start.30
  984.4 2.2 copy-start.3
  989.6 125.4 %copy-start.38 = (f32[64,32]{0,1:T(8,128)S(1)}, f32[64,32]{0,1:T(8,128)}, u32[]{:S(2)}) copy-start(f32[64,32]{0,1:T(8,128)} %copy-done.37) | copy-start | bytes 24580
  989.6 125.4 %copy-start.40 = (f32[64,32]{0,1:T(8,128)S(1)}, f32[64,32]{0,1:T(8,128)}, u32[]{:S(2)}) copy-start(f32[64,32]{0,1:T(8,128)} %copy-done.39) | copy-start | bytes 24580
  989.6 125.7 %copy-start.23 = (bf16[2,64,2048]{2,1,0:T(8,128)(2,1)S(1)}, bf16[2,64,2048]{2,1,0:T(8,128)(2,1)}, u32[]{:S(2)}) copy-start(bf16[2,64,2048]{2,1,0:T(8,128)(2,1)} %copy-done.22) | copy-start | bytes 1572868
  989.6 206.6 %reduce-scatter.9.cloned.1.call-start = ((), (), s32[]{:S(2)}) async-start(), calls=%async_computation.17 | async-start | bytes 2228224 | tf_op jit(solution)/shard_map/reduce_scatter | solution.py:272
  990.4 348.9 %reduce-scatter.13.cloned.1.call-start = ((), (), s32[]{:S(2)}) async-start(), calls=%async_computation.19 | async-start | bytes 2162688 | tf_op jit(solution)/shard_map/reduce_scatter | solution.py:306
  1115.3 1.9 copy-start.35
  1117.2 351.2 %reduce-scatter.15.cloned.1.call-start = ((), (), s32[]{:S(2)}) async-start(), calls=%async_computation.20 | async-start | bytes 2162688 | tf_op jit(solution)/shard_map/reduce_scatter | solution.py:307
  1197.7 2.1 copy-start.32
  1199.6 450.6 %reduce-scatter.11.cloned.1.call-start = ((), (), s32[]{:S(2)}) async-start(), calls=%async_computation.18 | async-start | bytes 17301504 | tf_op jit(solution)/shard_map/reduce_scatter | solution.py:305
  1211.1 626.4 %reduce-scatter.17.cloned.1.call-start = ((), (), s32[]{:S(2)}) async-start(), calls=%async_computation.21 | async-start | bytes 17301504 | tf_op jit(solution)/shard_map/reduce_scatter | solution.py:308
  1220.7 1106.3 %reduce-scatter.19.cloned.1.call-start = ((), (), s32[]{:S(2)}) async-start(), calls=%async_computation.22 | async-start | bytes 47579136 | tf_op jit(solution)/shard_map/reduce_scatter | solution.py:239
  1240.1 1582.8 %reduce-scatter.21.cloned.1.call-start = ((), (), s32[]{:S(2)}) async-start(), calls=%async_computation.23 | async-start | bytes 47579136 | tf_op jit(solution)/shard_map/reduce_scatter | solution.py:245
  1259.5 2059.3 %reduce-scatter.23.cloned.1.call-start = ((), (), s32[]{:S(2)}) async-start(), calls=%async_computation.24 | async-start | bytes 47579136 | tf_op jit(solution)/shard_map/reduce_scatter | solution.py:248
  1279.5 6.4 copy-start.10
  1285.8 11.7 copy-start.26
  1285.8 11.7 copy-start.36
  (30 other events, 38.6 us)
Sparse Core Ops, SparseCore 0:
  10.9 56.3 all-gather.9
  70.2 52.6 all-gather.13
  126.2 54.2 all-gather.11
  183.6 54.0 all-gather.15
  240.4 76.2 all-gather.17
  319.4 76.0 all-gather.19
  398.3 143.1 all-gather.21
  544.4 142.7 all-gather.23
  690.1 142.7 all-gather.25
  989.7 124.0 all-reduce.8
  1116.3 79.8 reduce-scatter.8
  1199.0 134.0 reduce-scatter.12
  1335.9 132.4 reduce-scatter.14
  1471.3 178.8 reduce-scatter.10
  1653.0 184.4 reduce-scatter.16
  1840.3 486.6 reduce-scatter.18
  2329.8 493.0 reduce-scatter.20
  2825.7 493.0 reduce-scatter.22
where the time goes:
time: 3340 us; the launch traced here: 3330 us
  waiting for transfers between devices  2880 us (86%)
  matrix products  214 us (6%)
  local copies, waits for them, and re-layouts  123 us (4%)
  blocking collectives  79.2 us (2%)
    reduce_scatter x1, waiting for transfers between devices, shards(): lax.psum_scatter(contract_rows(activated, upstream), ('ctx', 'fsdp'), sca...  496 us
    reduce_scatter x1, waiting for transfers between devices, shards(): lax.psum_scatter(contract_rows(normed_mlp, grad_up_in), ('ctx', 'fsdp'),...  496 us
    reduce_scatter x1, waiting for transfers between devices, shards(): lax.psum_scatter(contract_rows(normed_mlp, grad_gate_in), ('ctx', 'fsdp')...  489 us
    reduce_scatter x1, waiting for transfers between devices, shards(): lax.psum_scatter(grad_out, ('ctx', 'fsdp'), scatter_dimension=0, tiled=True)  187 us
    reduce_scatter x1, waiting for transfers between devices, shards(): lax.psum_scatter(grad_query, ('ctx', 'fsdp'), scatter_dimension=0, tiled=...  182 us
    all_gather x1, waiting for transfers between devices, shards(): lax.all_gather(w_gate, ('ctx', 'fsdp'), axis=0, tiled=True)  141 us
    all_gather x1, waiting for transfers between devices, shards(): lax.all_gather(w_down, ('ctx', 'fsdp'), axis=0, tiled=True)  133 us
    all_gather x1, waiting for transfers between devices, shards(): lax.all_gather(w_up, ('ctx', 'fsdp'), axis=0, tiled=True)  133 us
  transfers between devices with their start and end apart: 18, of which 17 were waited for; matrix products, arithmetic and copies ran while one was open for 6% of the time, Pallas kernels for 0%

commit v1 on v0

v1 whole, which is shorter than its diff:
```python
import functools
import math

import jax
import jax.numpy as jnp
from jax import lax
from jax.experimental import pallas as pl
from jax.experimental.pallas import tpu as pltpu
from jax.sharding import Mesh, PartitionSpec as P

QUERY_HEADS = 32
KEY_VALUE_HEADS = 4
HEAD_WIDTH = 64
GROUP = QUERY_HEADS // KEY_VALUE_HEADS
EPSILON = 1e-05
SCALE = 1.0 / math.sqrt(HEAD_WIDTH)
SWAP = ((0, 1), (1, 0))
CROSS = ((1, 2), (2, 1))
BF16 = jnp.bfloat16
F32 = jnp.float32
VMEM = 56 * 1024 * 1024
COST = pl.CostEstimate(flops=1, bytes_accessed=1, transcendentals=0)

NT = (((1,), (1,)), ((), ()))
TN = (((0,), (0,)), ((), ()))
NN = (((1,), (0,)), ((), ()))


def dot(left, right, dims=NN):
    return lax.dot_general(left, right, dims, preferred_element_type=F32)


def pick(array, index, axis=0):
    return lax.dynamic_index_in_dim(array, index, axis, keepdims=False)


def bit(axis):
    return lax.axis_index(axis)


def swap(array, axis, name="swap"):
    with jax.named_scope(name):
        return lax.ppermute(array, axis, SWAP)


def pair(axis, own, got, at=0):
    first = bit(axis) == 0
    return jnp.stack([jnp.where(first, own, got), jnp.where(first, got, own)], at)


def half_swap(array):
    width = array.shape[-1]
    lane = lax.broadcasted_iota(jnp.int32, array.shape, array.ndim - 1)
    ahead = pltpu.roll(array, width - HEAD_WIDTH // 2, array.ndim - 1)
    behind = pltpu.roll(array, HEAD_WIDTH // 2, array.ndim - 1)
    return jnp.where(lane % HEAD_WIDTH < HEAD_WIDTH // 2, ahead, behind)


def widen(table, width):
    return jnp.concatenate([table] * (width // table.shape[-1]), axis=-1)


def place_of(bits_ref, which):
    high = 1 - bits_ref[0] if which & 1 else bits_ref[0]
    low = 1 - bits_ref[1] if which & 2 else bits_ref[1]
    return high, low


def deal_attn_kernel(queries, kv_of, order, bits_ref, own, far, near, corner, out_ref, scratch):
    rows = own.shape[0]
    columns = out_ref.shape[-1]
    keys = own.shape[1] - 128 - 2 * KEY_VALUE_HEADS * HEAD_WIDTH
    values = keys + KEY_VALUE_HEADS * HEAD_WIDTH
    for which, ref in enumerate((own, far, near, corner)):
        high, low = place_of(bits_ref, which)
        scratch[2 * high + low] = ref[...]
    gains = [scratch[at, :, own.shape[1] - 128 :].astype(F32).T[:16] for at in range(4)]
    gains = jnp.concatenate(gains + [jnp.zeros((16, columns - 4 * rows), F32)], axis=1).astype(BF16)
    for slot, (member, kv) in enumerate(zip(order, kv_of)):
        for at in range(4):
            head = lambda start: scratch[at, :, start + kv * HEAD_WIDTH : start + (kv + 1) * HEAD_WIDTH]
            out_ref[slot, at * rows : (at + 1) * rows, :queries] = scratch[
                at, :, member * queries : (member + 1) * queries
            ]
            if queries < columns - 128:
                out_ref[slot, at * rows : (at + 1) * rows, queries : columns - 128] = jnp.zeros(
                    (rows, columns - 128 - queries), BF16
                )
            both = jnp.concatenate([head(keys), head(values)], axis=1)
            out_ref[slot, at * rows : (at + 1) * rows, columns - 128 :] = both
        out_ref[slot, 4 * rows :] = gains


def deal_attn(bits, order, kv_of, queries, padded, parts):
    rows, width = parts[0].shape
    columns = padded + 128
    shape = (len(order), 4 * rows + 16, columns)
    return pl.pallas_call(
        functools.partial(deal_attn_kernel, queries, kv_of, order),
        in_specs=[pl.BlockSpec(memory_space=pltpu.SMEM)]
        + [pl.BlockSpec(memory_space=pltpu.VMEM)] * 4,
        out_shape=jax.ShapeDtypeStruct(shape, BF16),
        scratch_shapes=[pltpu.VMEM((4, rows, width), BF16)],
        compiler_params=pltpu.CompilerParams(vmem_limit_bytes=VMEM),
        cost_estimate=COST,
        name="deal_attn",
    )(bits, *parts)


def project_kernel(
    x_ref, dealt_ref, cos_ref, sin_ref,
    normed_ref, q_ref, k_ref, v_ref, kt_ref, vt_ref, gains_ref, w_ref,
):
    width = q_ref.shape[-1]
    places, rows = w_ref.shape[1], w_ref.shape[4]

    @pl.when(pl.program_id(0) == 0)
    def _():
        gains = []
        for high in (0, 1):
            for place in range(places):
                for low in (0, 1):
                    for core in (0, 1):
                        at = slice((2 * high + low) * rows, (2 * high + low + 1) * rows)
                        w_ref[high, place, low, core] = dealt_ref[2 * place + core, at, :]
                        both = dealt_ref[2 * place + core, 4 * rows :, at]
                        gains.append(both.astype(F32)[:8])
        gains_ref[...] = jnp.concatenate(gains, axis=1)

    x = x_ref[...].astype(F32)
    r = lax.rsqrt(jnp.mean(x * x, axis=-1, keepdims=True) + EPSILON)
    normed = (x * r * gains_ref[:1, :]).astype(BF16)
    normed_ref[...] = normed
    w = w_ref[...].reshape(x_ref.shape[-1], w_ref.shape[-1])
    y = dot(normed, w)
    q = y[:, :width]
    both = y[:, width:]
    lane = lax.broadcasted_iota(jnp.int32, both.shape, 1)
    other = pltpu.roll(both, HEAD_WIDTH, 1)
    k = jnp.where(lane < HEAD_WIDTH, both, other)
    v = jnp.where(lane < HEAD_WIDTH, other, both)
    turn = lambda a: a * widen(cos_ref[...], a.shape[-1]) + half_swap(a) * widen(sin_ref[...], a.shape[-1])
    q_ref[...] = turn(q).astype(BF16)
    k = widen(turn(k), width)
    v = widen(v, width)
    k_ref[...] = k.astype(BF16)
    v_ref[...] = v.astype(BF16)
    kt_ref[...] = k.T.astype(BF16)
    vt_ref[...] = v.T.astype(BF16)


def project(places, x, dealt, cos, sin):
    rows, width = x.shape
    columns = dealt.shape[2]
    out = columns - 128
    block = 256
    row = lambda n: pl.BlockSpec((block, n), lambda i: (i, 0))
    across = pl.BlockSpec((out, block), lambda i: (0, i))
    shape = jax.ShapeDtypeStruct
    whole = (2, places, 2, 2, (dealt.shape[1] - 16) // 4, columns)
    return pl.pallas_call(
        project_kernel,
        grid=(rows // block,),
        in_specs=[row(width), pl.BlockSpec(dealt.shape, lambda i: (0, 0, 0)), row(128), row(128)],
        out_specs=[row(width), row(out), row(out), row(out), across, across]
        + [pl.BlockSpec((8, width), lambda i: (0, 0))]
        + [pl.BlockSpec(whole, lambda i: (0, 0, 0, 0, 0, 0))],
        out_shape=[shape((rows, n), BF16) for n in (width, out, out, out)]
        + [shape((out, rows), BF16)] * 2
        + [shape((8, width), F32), shape(whole, BF16)],
        compiler_params=pltpu.CompilerParams(vmem_limit_bytes=VMEM),
        cost_estimate=COST,
        name="project",
    )(x, dealt, cos, sin)


def forward_kernel(heads, q_ref, k_ref, vt_ref, pq_ref, dq_ref, pk_ref, dk_ref, out_ref, lse_ref):
    q = q_ref[...]
    visible = (pk_ref[...] <= pq_ref[...]) & (dk_ref[...] == dq_ref[...])
    lane = lax.broadcasted_iota(jnp.int32, q.shape, 1) // HEAD_WIDTH
    wide = (q.shape[1], q.shape[0])
    row = lax.broadcasted_iota(jnp.int32, wide, 0) // HEAD_WIDTH
    total = jnp.zeros(wide, F32)
    lse_ref[...] = jnp.zeros_like(lse_ref)
    for head in range(heads):
        own = jnp.where(lane == head, q, jnp.zeros_like(q))
        scores = jnp.where(visible, dot(k_ref[...], own, NT) * SCALE, -1e30)
        top = jnp.max(scores, axis=0, keepdims=True)
        powers = jnp.exp(scores - top)
        mass = jnp.sum(powers, axis=0, keepdims=True)
        lse_ref[head : head + 1, :] = top + jnp.log(mass)
        chances = (powers * (1.0 / mass)).astype(BF16)
        total = jnp.where(row == head, dot(vt_ref[...], chances), total)
    out_ref[...] = total.T.astype(BF16)


def query_block(rows):
    return 256 if rows <= 1024 else 128


def attend_forward(heads, q, k, vt, positions, docs):
    rows, width = q.shape
    block = query_block(rows)
    row = pl.BlockSpec((block, width), lambda i: (i, 0))
    across = pl.BlockSpec((1, block), lambda i: (0, i))
    whole = lambda a: pl.BlockSpec(a.shape, lambda i: (0, 0))
    down = (positions[:, None], docs[:, None])
    flat = (positions[None], docs[None])
    return pl.pallas_call(
        functools.partial(forward_kernel, heads),
        grid=(rows // block,),
        in_specs=[row, whole(k), whole(vt), across, across, whole(down[0]), whole(down[1])],
        out_specs=[row, pl.BlockSpec((8, block), lambda i: (0, i))],
        out_shape=[
            jax.ShapeDtypeStruct((rows, width), BF16),
            jax.ShapeDtypeStruct((8, rows), F32),
        ],
        compiler_params=pltpu.CompilerParams(vmem_limit_bytes=VMEM),
        cost_estimate=COST,
        name="attend_forward",
    )(q, k, vt, *flat, *down)


def backward_kernel(
    heads, q_ref, g_ref, k_ref, v_ref, kt_ref, pq_ref, dq_ref, pk_ref, dk_ref, lse_ref,
    cos_ref, sin_ref, cos_all_ref, sin_all_ref, gq_ref, gkv_ref, gk_sum, gv_sum,
):
    step = pl.program_id(0)

    @pl.when(step == 0)
    def _():
        gk_sum[...] = jnp.zeros_like(gk_sum)
        gv_sum[...] = jnp.zeros_like(gv_sum)

    q = q_ref[...]
    g = g_ref[...]
    visible = (pk_ref[...] <= pq_ref[...]) & (dk_ref[...] == dq_ref[...])
    lane = lax.broadcasted_iota(jnp.int32, q.shape, 1) // HEAD_WIDTH
    wide = (q.shape[1], q.shape[0])
    row = lax.broadcasted_iota(jnp.int32, wide, 0) // HEAD_WIDTH
    total = jnp.zeros(wide, F32)
    for head in range(heads):
        own = jnp.where(lane == head, q, jnp.zeros_like(q))
        own_g = jnp.where(lane == head, g, jnp.zeros_like(g))
        scores = dot(k_ref[...], own, NT) * SCALE
        chances = jnp.where(visible, jnp.exp(scores - lse_ref[head : head + 1, :]), 0.0)
        grads = dot(v_ref[...], own_g, NT)
        inner = jnp.sum(chances * grads, axis=0, keepdims=True)
        grad_scores = (chances * (grads - inner)).astype(BF16)
        gv_sum[...] += dot(chances.astype(BF16), own_g)
        gk_sum[...] += dot(grad_scores, own)
        total = jnp.where(row == head, dot(kt_ref[...], grad_scores), total)
    gq = total.T * SCALE
    width = gq.shape[-1]
    gq = gq * widen(cos_ref[...], width) - half_swap(gq) * widen(sin_ref[...], width)
    gq_ref[...] = gq.astype(BF16)

    @pl.when(step == pl.num_programs(0) - 1)
    def _():
        def fold(array):
            parts = [array[:, at : at + 128] for at in range(0, array.shape[-1], 128)]
            both = functools.reduce(lambda a, b: a + b, parts)
            return both + pltpu.roll(both, HEAD_WIDTH, 1)

        gk = fold(gk_sum[...]) * SCALE
        gk = gk * cos_all_ref[...] - half_swap(gk) * sin_all_ref[...]
        gv = fold(gv_sum[...])
        lane = lax.broadcasted_iota(jnp.int32, gk.shape, 1)
        gkv_ref[...] = jnp.where(lane < HEAD_WIDTH, gk, gv).astype(BF16)


def attend_backward(heads, q, g, k, v, kt, positions, docs, lse, cos, sin):
    rows, width = q.shape
    block = query_block(rows)
    row = lambda n: pl.BlockSpec((block, n), lambda i: (i, 0))
    across = lambda n: pl.BlockSpec((n, block), lambda i: (0, i))
    whole = lambda a: pl.BlockSpec(a.shape, lambda i: (0, 0))
    down = (positions[:, None], docs[:, None])
    flat = (positions[None], docs[None])
    return pl.pallas_call(
        functools.partial(backward_kernel, heads),
        grid=(rows // block,),
        in_specs=[
            row(width), row(width), whole(k), whole(v), whole(kt), across(1), across(1),
            whole(down[0]), whole(down[1]), across(8), row(128), row(128), whole(cos), whole(sin),
        ],
        out_specs=[row(width), pl.BlockSpec((rows, 128), lambda i: (0, 0))],
        out_shape=[
            jax.ShapeDtypeStruct((rows, width), BF16),
            jax.ShapeDtypeStruct((rows, 128), BF16),
        ],
        scratch_shapes=[pltpu.VMEM((rows, width), F32), pltpu.VMEM((rows, width), F32)],
        compiler_params=pltpu.CompilerParams(vmem_limit_bytes=VMEM),
        cost_estimate=COST,
        name="attend_backward",
    )(q, g, k, v, kt, *flat, *down, lse, cos, sin, cos, sin)


def feed_kernel(bits_ref, n_ref, g_ref, down_ref, *refs):
    parts = refs[:8]
    act_ref, back_ref, w_ref, sem = refs[8:]

    @pl.when(pl.program_id(0) == 0)
    def _():
        copies = []
        for at, part in enumerate(parts):
            which, chunk = at % 4, at // 4
            high, low = place_of(bits_ref, which)
            size = part.shape[0]
            places = pl.ds(chunk * size, size)
            copies.append(
                pltpu.make_async_copy(part, w_ref.at[high, places, low], sem.at[at])
            )
        for copy in copies:
            copy.start()
        for copy in copies:
            copy.wait()

    units = act_ref.shape[-1]
    both = dot(n_ref[...], w_ref[...].reshape(n_ref.shape[-1], 2 * units))
    gate, up = both[:, :units], both[:, units:]
    grad = dot(g_ref[...], down_ref[...], NT)
    s = jax.nn.sigmoid(gate)
    silu = gate * s
    act_ref[...] = (silu * up).astype(BF16)
    back = jnp.concatenate([grad * up * s * (1.0 + gate * (1.0 - s)), grad * silu], axis=1)
    back_ref[...] = back.astype(BF16)


def feed_forward(bits, n, g, down, parts):
    rows, width = n.shape
    places, piece, columns = parts[0].shape
    units = columns // 2
    block = 256
    row = lambda w: pl.BlockSpec((block, w), lambda i: (i, 0))
    whole = (2, 2 * places, 2, piece, columns)
    return pl.pallas_call(
        feed_kernel,
        grid=(rows // block,),
        in_specs=[
            pl.BlockSpec(memory_space=pltpu.SMEM),
            row(width),
            row(width),
            pl.BlockSpec(down.shape, lambda i: (0, 0)),
        ]
        + [pl.BlockSpec(memory_space=pl.ANY)] * 8,
        out_specs=[row(units), row(columns), pl.BlockSpec(whole, lambda i: (0, 0, 0, 0, 0))],
        out_shape=[
            jax.ShapeDtypeStruct((rows, units), BF16),
            jax.ShapeDtypeStruct((rows, columns), BF16),
            jax.ShapeDtypeStruct(whole, BF16),
        ],
        scratch_shapes=[pltpu.SemaphoreType.DMA((8,))],
        compiler_params=pltpu.CompilerParams(vmem_limit_bytes=VMEM),
        cost_estimate=COST,
        name="feed_forward",
    )(bits, n, g, down, *parts)


def rows_kernel(sides, chunks, bits_ref, left_ref, right_ref, *refs):
    outs, scratch = refs[:-1], refs[-1]
    step, chunk = pl.program_id(0), pl.program_id(1)
    low = bits_ref[1]
    scratch[...] = dot(left_ref[...], right_ref[...], TN).astype(BF16)
    for side in range(len(sides)):
        for part in range(chunks):

            @pl.when((step == side) & (chunk == part))
            def _():
                for beside in (0, 1):
                    out = outs[(side * 2 + beside) * chunks + part]
                    rows = out.shape[1]
                    column = 1 - low if beside else low
                    for place in range(out.shape[0]):
                        start = pl.multiple_of((2 * place + column) * rows, rows)
                        out[place] = scratch[pl.ds(start, rows), :]


def outer_rows(sides, chunks, places, bits, left, right):
    rows, width = left.shape
    columns = right.shape[1]
    piece = width // (4 * places)
    block = width // (2 * chunks)
    shape = (places // chunks, piece, columns)
    count = len(sides) * 2 * chunks
    first = sides[0]
    outs = pl.pallas_call(
        functools.partial(rows_kernel, sides, chunks),
        grid_spec=pltpu.PrefetchScalarGridSpec(
            num_scalar_prefetch=1,
            grid=(len(sides), chunks),
            in_specs=[
                pl.BlockSpec(
                    (rows, block),
                    lambda i, j, bits: (0, jnp.bitwise_xor(bits[0], jnp.bitwise_xor(i, first)) * chunks + j),
                ),
                pl.BlockSpec(right.shape, lambda i, j, bits: (0, 0)),
            ],
            out_specs=[pl.BlockSpec(shape, lambda i, j, bits: (0, 0, 0))] * count,
            scratch_shapes=[pltpu.VMEM((block, columns), BF16)],
        ),
        out_shape=[jax.ShapeDtypeStruct(shape, BF16)] * count,
        compiler_params=pltpu.CompilerParams(vmem_limit_bytes=VMEM),
        cost_estimate=COST,
        name="outer_rows",
    )(bits, left, right)
    return [list(outs[at : at + chunks]) for at in range(0, count, chunks)]


def quarters_kernel(flip, bits_ref, left_ref, right_ref, own, near, theirs, far, scratch):
    scratch[...] = dot(left_ref[...], right_ref[...], TN).astype(BF16)
    rows = own.shape[0]
    for ref, there, beside in ((own, 0, 0), (near, 0, 1), (theirs, 1, 0), (far, 1, 1)):
        high = 1 - bits_ref[0] if there else bits_ref[0]
        low = 1 - bits_ref[1] if beside else bits_ref[1]
        at = 2 * low + high if flip else 2 * high + low
        ref[...] = scratch[pl.ds(pl.multiple_of(at * rows, rows), rows), :]


def outer_quarters(flip, bits, left, right):
    rows, width = left.shape
    columns = right.shape[1]
    block = min(columns, 512)
    piece = width // 4
    if piece % 16:
        product = dot(left, right, TN).astype(BF16).reshape(2, 2, piece, columns)
        high, low = (bits[1], bits[0]) if flip else (bits[0], bits[1])
        sides = ((0, 0), (1, 0), (0, 1), (1, 1)) if flip else ((0, 0), (0, 1), (1, 0), (1, 1))
        return [pick(pick(product, high ^ a), low ^ b) for a, b in sides]
    return pl.pallas_call(
        functools.partial(quarters_kernel, flip),
        grid_spec=pltpu.PrefetchScalarGridSpec(
            num_scalar_prefetch=1,
            grid=(columns // block,),
            in_specs=[
                pl.BlockSpec(left.shape, lambda i, bits: (0, 0)),
                pl.BlockSpec((rows, block), lambda i, bits: (0, i)),
            ],
            out_specs=[pl.BlockSpec((piece, block), lambda i, bits: (0, i))] * 4,
            scratch_shapes=[pltpu.VMEM((width, block), BF16)],
        ),
        out_shape=[jax.ShapeDtypeStruct((piece, columns), BF16)] * 4,
        compiler_params=pltpu.CompilerParams(vmem_limit_bytes=VMEM),
        cost_estimate=COST,
        name="outer_quarters",
    )(bits, left, right)


def deal_kernel(places, gate_ref, up_ref, out_ref):
    rows, columns = gate_ref.shape
    piece = columns // (8 * places)
    for place in range(places):
        for core in (0, 1):
            starts = [
                (((high * places + place) * 2 + low) * 2 + core) * piece
                for high in (0, 1)
                for low in (0, 1)
            ]
            out_ref[2 * place + core] = jnp.concatenate(
                [ref[:, start : start + piece] for ref in (gate_ref, up_ref) for start in starts],
                axis=1,
            )


def deal(places, gate, up):
    rows, columns = gate.shape
    return pl.pallas_call(
        functools.partial(deal_kernel, places),
        out_shape=jax.ShapeDtypeStruct((2 * places, rows, columns // places), BF16),
        compiler_params=pltpu.CompilerParams(vmem_limit_bytes=VMEM),
        cost_estimate=COST,
        name="deal",
    )(gate, up)


def collect_kernel(places, in_ref, gate_ref, up_ref):
    rows, columns = gate_ref.shape
    piece = columns // (8 * places)
    for which, ref in enumerate((gate_ref, up_ref)):
        pieces = []
        for high in (0, 1):
            for place in range(places):
                for low in (0, 1):
                    for core in (0, 1):
                        start = (4 * which + 2 * high + low) * piece
                        got = in_ref[2 * place + core][:, start : start + piece]
                        pieces.append(got.astype(F32))
        ref[...] = jnp.concatenate(pieces, axis=1)


def collect(places, array):
    _, rows, columns = array.shape
    shape = jax.ShapeDtypeStruct((rows, places * columns), F32)
    return pl.pallas_call(
        functools.partial(collect_kernel, places),
        out_shape=[shape, shape],
        compiler_params=pltpu.CompilerParams(vmem_limit_bytes=VMEM),
        cost_estimate=COST,
        name="collect",
    )(array)


def sum_kernel(count, *refs):
    outs = refs[3 * count + 1 :]
    for at in range(count):
        own, near, relayed = refs[3 * at : 3 * at + 3]
        total = own[...].astype(F32) + near[...].astype(F32) + relayed[...].astype(F32)
        outs[at][...] = total.astype(outs[at].dtype)


def sum_parts(dtype, after, *groups):
    vmem = pl.BlockSpec(memory_space=pltpu.VMEM)
    return pl.pallas_call(
        functools.partial(sum_kernel, len(groups)),
        in_specs=[vmem] * (3 * len(groups)) + [pl.BlockSpec(memory_space=pl.ANY)],
        out_shape=[jax.ShapeDtypeStruct(group[0].shape, dtype) for group in groups],
        compiler_params=pltpu.CompilerParams(vmem_limit_bytes=VMEM),
        cost_estimate=COST,
        name="sum_parts",
    )(*[part for group in groups for part in group], after)


def rope_tables(positions):
    inverse = 10000.0 ** (-jnp.arange(0, HEAD_WIDTH, 2).astype(F32) / HEAD_WIDTH)
    angles = positions.astype(F32)[:, None] * inverse[None, :]
    cos, sin = jnp.cos(angles), jnp.sin(angles)
    return jnp.concatenate([cos] * 4, 1), jnp.concatenate([-sin, sin] * 2, 1)


def norm_back(upstream, values, gain):
    scaling = lax.rsqrt(jnp.mean(values * values, axis=-1, keepdims=True) + EPSILON)
    scaled_grad = upstream * gain
    return scaling * scaled_grad - values * (scaling * scaling * scaling) * jnp.mean(
        scaled_grad * values, axis=-1, keepdims=True
    )


class Layout:
    def __init__(self, mesh):
        bits = mesh.shape["ctx"].bit_length() - 1
        self.ctx = tuple(f"p{i}" for i in range(bits))
        self.mesh = Mesh(
            mesh.devices.reshape((2,) * bits + (mesh.shape["fsdp"],)), self.ctx + ("core",)
        )
        self.high, self.low = self.ctx[0], self.ctx[-1]
        self.mid = self.ctx[1:-1]
        self.places = 2 ** len(self.mid)
        self.members = 2 * self.places
        self.all = self.ctx + ("core",)
        self.turn = [
            [(4 * h + 2 * l + c, 4 * c + 2 * (l ^ other) + h) for h in (0, 1) for l in (0, 1) for c in (0, 1)]
            for other in (0, 1)
        ]

    def cross(self, array):
        got = lax.ppermute(array, (self.high, "core"), CROSS)
        return jnp.where(bit(self.high) == bit("core"), array, got)

    def turned(self, array, other, name):
        with jax.named_scope(name):
            return lax.ppermute(array, (self.high, self.low, "core"), self.turn[other])

    def to_team(self, array, name):
        low = bit(self.low)
        return self.turned(pick(array, low), 0, name), self.turned(pick(array, 1 - low), 1, name)

    def in_order(self, blocks):
        both = pair(self.low, *blocks)
        return both.reshape(-1, both.shape[-1])

    def from_team(self, array, name):
        low = bit(self.low)
        both = array.reshape(2, -1, array.shape[-1])
        return pair(
            self.low,
            self.turned(pick(both, low), 0, name),
            self.turned(pick(both, 1 - low), 1, name),
        )

    def team_gather(self, array):
        return lax.all_gather(array, ("core",) + self.mid, axis=0, tiled=True)


    def scatter_cores(self, rows_of, then=None):
        core = bit("core")
        sent = rows_of(1 - core).astype(BF16)
        got = swap(sent, "core", "sum_cores")
        if then is not None:
            then(sent)
        mine = rows_of(core) + got.astype(F32)
        width = mine.shape[1]
        mine = mine.astype(BF16).reshape((2,) * len(self.mid) + (-1, width))
        return [mine[..., : width // 2], mine[..., width // 2 :]]

    def scatter_send(self, parts, count):
        pending = []
        for part, order in zip(parts, (list(self.mid), list(self.mid[::-1]))):
            left = [axis for axis in self.mid if axis not in order[:count]]
            at = left.index(order[count])
            there = bit(order[count])
            pending.append((pick(part, there, at), swap(pick(part, 1 - there, at), order[count], f"sum_places_{count}")))
        return pending

    def scatter_add(self, pending):
        last = pending[0][0].ndim == 2
        parts = [own.astype(F32) + got.astype(F32) for own, got in pending]
        return jnp.concatenate(parts, 1) if last else [part.astype(BF16) for part in parts]

    def scatter_rows(self, rows_of, then=()):
        then = list(then) + [lambda parts: parts] * (1 + len(self.mid) - len(then))
        parts = self.scatter_cores(rows_of, then[0])
        for count in range(len(self.mid)):
            parts = self.scatter_add(self.scatter_send(then[1 + count](parts), count))
        return parts

    def exchange(self, array):
        return lax.all_to_all(array, self.mid + ("core",), 0, 0, tiled=True)

    def rows_out(self, array):
        shape = array.shape
        return jnp.swapaxes(array.reshape((2, self.places) + shape[1:]), 0, 1).reshape(shape)

    def rows_in(self, array):
        shape = array.shape
        return jnp.swapaxes(array.reshape((self.places, 2) + shape[1:]), 0, 1).reshape(shape)


    def start_four(self, array, name):
        return swap(array, self.high, name + "_far"), swap(array, self.low, name + "_near")

    def corner_four(self, far, name):
        return swap(far, self.low, name + "_corner")

    def join_four(self, first, second, own, far, near, corner):
        return pair(first, pair(second, own, near), pair(second, far, corner))

    def relay_sum(self, theirs, got_far, name):
        relay = theirs.astype(F32) + got_far.astype(F32)
        return swap(relay.astype(BF16), self.high, name + "_relay")


def shards(
    layout,
    hidden_in,
    positions,
    doc_ids,
    norm_attn,
    w_query,
    key_weight,
    value_weight,
    w_out,
    norm_mlp,
    w_gate,
    w_up,
    w_down,
    cotangent,
):
    members, places = layout.members, layout.places
    width = hidden_in.shape[-1]
    weight_rows = w_query.shape[0]
    heads = QUERY_HEADS // members
    padded = max(heads, 2)
    query_width = heads * HEAD_WIDTH
    padding = (padded - heads) * HEAD_WIDTH
    tie = lax.optimization_barrier
    place = sum(bit(axis) * 2**at for at, axis in enumerate(layout.mid[::-1]))
    bits = jnp.stack([bit(layout.high), bit(layout.low), 2 * place + bit("core")])
    bits = bits.astype(jnp.int32)
    order = [core * places + place for place in range(places) for core in (0, 1)]
    kv_of = [member * heads // GROUP for member in order]


    blocks = layout.to_team(hidden_in, "hidden")
    docs = layout.cross(pick(doc_ids, bit(layout.low)))
    gains = jnp.stack([norm_attn, norm_mlp], axis=1)
    gains = jnp.pad(gains, ((0, 0), (0, 126)))
    raw = jnp.concatenate([w_query, key_weight, value_weight, gains], axis=1)
    raw_far, raw_near = layout.start_four(raw, "raw")
    x = layout.in_order(blocks)
    x_team = layout.team_gather(x)
    cos, sin = rope_tables(positions)
    dealt = deal(places, w_gate, w_up)
    raw_far, raw_near, w_out, down_sent, cotangent, cos, sin, positions, docs, dealt = tie(
        (raw_far, raw_near, w_out, w_down, cotangent, cos, sin, positions, docs, dealt)
    )
    raw_corner = layout.corner_four(raw_far, "raw")
    out_part = layout.cross(w_out)
    g_blocks = layout.to_team(cotangent, "cotangent")
    dealt_attn = deal_attn(
        bits, order, kv_of, query_width, query_width + padding, (raw, raw_far, raw_near, raw_corner)
    )
    dealt_attn, out_part, down_sent, *g_blocks = tie((dealt_attn, out_part, down_sent, *g_blocks))
    dealt_attn = layout.exchange(dealt_attn)
    out_far, out_near = layout.start_four(out_part, "out")
    down_far, down_near = layout.start_four(down_sent, "down")
    g_rows = layout.in_order(g_blocks)
    g = layout.team_gather(g_rows)
    dealt_attn, out_far, out_near, dealt = tie((dealt_attn, out_far, out_near, dealt))
    dealt = layout.exchange(dealt)
    out_corner = layout.corner_four(out_far, "out")

    normed_attn, q, k, v, kt, vt, gains, w_attn = project(places, x_team, dealt_attn, cos, sin)
    gain_attn, gain_mlp = gains[:1], gains[1:2]
    q, out_corner, down_far, down_near = tie((q, out_corner, down_far, down_near))
    down_corner = layout.corner_four(down_far, "down")
    attended, lse = attend_forward(heads, q, k, vt, positions, docs)
    attended, dealt, down_corner = tie((attended, dealt, down_corner))
    dealt = dealt.reshape(places, 2 * weight_rows, -1)
    chunk = lambda a, at: a[at * places // 2 : (at + 1) * places // 2]
    gu_parts = [chunk(dealt, 0), chunk(dealt, 1)]
    gu_far, gu_near, gu_corner = [None] * 2, [None] * 2, [None] * 2
    gu_far[0], gu_near[0] = layout.start_four(gu_parts[0], "gate_up_0")
    out_own = layout.join_four(layout.low, layout.high, out_part, out_near, out_far, out_corner)
    out_own = out_own.reshape(query_width, width)
    down_own = layout.join_four(
        layout.high, layout.low, w_down, down_far, down_near, down_corner
    ).reshape(-1, width)
    attended = attended[:, :query_width]

    half = x_team.shape[0] // 2
    part = lambda a, core: lax.dynamic_slice_in_dim(a, core * half, half, 0)
    same = lambda parts: parts
    late = {}

    def weights_on(parts):
        *parts, gu_far[0], gu_near[0], gu_parts[1] = tie(
            (*parts, gu_far[0], gu_near[0], gu_parts[1])
        )
        gu_corner[0] = layout.corner_four(gu_far[0], "gate_up_0")
        gu_far[1], gu_near[1] = layout.start_four(gu_parts[1], "gate_up_1")
        return parts

    branch = layout.scatter_rows(
        lambda core: dot(part(attended, core), out_own), (None, same, weights_on)
    )
    x_wide = x.astype(F32)
    middle = x_wide + branch
    scale_mlp = lax.rsqrt(jnp.mean(middle * middle, axis=-1, keepdims=True) + EPSILON)
    normed_mlp = layout.team_gather((middle * scale_mlp * gain_mlp).astype(BF16))
    gu_corner[1] = layout.corner_four(gu_far[1], "gate_up_1")

    activated, grad_gu, w_gu = feed_forward(
        bits,
        normed_mlp,
        g,
        down_own,
        [
            parts[at]
            for at in range(2)
            for parts in (gu_parts, gu_far, gu_near, gu_corner)
        ],
    )
    w_gu = w_gu.reshape(width, -1)

    down_parts = outer_quarters(False, bits, activated, g)
    grad_gu, activated, down_parts = tie((grad_gu, activated, down_parts))
    down_far = swap(down_parts[3], layout.low, "grad_down_far")

    def gu_terms(parts):
        *parts, right = tie((*parts, grad_gu))
        late["theirs"], late["far"] = outer_rows((1,), 2, places, bits, normed_mlp, right)
        return parts

    def gu_others(parts):
        *parts, late["far"], late["theirs"], right, late["down_far"] = tie(
            (*parts, late["far"], late["theirs"], grad_gu, down_far)
        )
        late["far"][0] = swap(late["far"][0], layout.low, "grad_gate_up_far_0")
        late["down_relay"] = layout.relay_sum(down_parts[2], late["down_far"], "grad_down")
        late["own"], late["near"] = outer_rows((0,), 2, places, bits, normed_mlp, right)
        return parts

    grad_normed_mlp = layout.scatter_rows(
        lambda core: dot(part(grad_gu, core), w_gu, NT), (None, gu_terms, gu_others)
    )
    gu_theirs, gu_far, gu_own, gu_near = (late[key] for key in ("theirs", "far", "own", "near"))
    down_relay = late["down_relay"]
    grad_normed_mlp, gu_own, gu_near = tie((grad_normed_mlp, gu_own, gu_near))
    grad_middle = g_rows.astype(F32) + norm_back(grad_normed_mlp, middle, gain_mlp)
    grad_branch = grad_middle.astype(BF16)
    branch_team = layout.team_gather(grad_branch)
    gu_far[0], act, grad_branch, sent = tie((gu_far[0], activated, grad_branch, gu_far[1]))
    gu_far[1] = swap(sent, layout.low, "grad_gate_up_far_1")
    gu_relay = [layout.relay_sum(gu_theirs[0], gu_far[0], "grad_gate_up_0")]
    final = layout.scatter_cores(lambda core: dot(part(act, core), down_own))
    branch_team, gu_far[1], down_sent, near_sent, *final = tie(
        (branch_team, gu_far[1], down_parts[1], gu_near[0], *final)
    )
    gu_relay.append(layout.relay_sum(gu_theirs[1], gu_far[1], "grad_gate_up_1"))
    down_near = swap(down_sent, layout.low, "grad_down_near")
    final = layout.scatter_send(final, 0)
    grad_attended = dot(branch_team, out_own, NT).astype(BF16)
    if padding:
        grad_attended = jnp.pad(grad_attended, ((0, 0), (0, padding)))

    gq, gkv = attend_backward(heads, q, grad_attended, k, v, kt, positions, docs, lse, cos, sin)
    grad_qkv = jnp.concatenate([gq, gkv], axis=1)
    grad_qkv, final, down_near, near_sent = tie((grad_qkv, final, down_near, near_sent))
    gu_near[0] = swap(near_sent, layout.low, "grad_gate_up_near_0")
    for count in range(1, len(layout.mid)):
        final = layout.scatter_send(layout.scatter_add(final), count)

    w_attn_own = w_attn.reshape(width, -1)[:, : grad_qkv.shape[1]]

    def attn_terms(sent):
        _, right = tie((sent, grad_qkv))
        late["attn"] = [part for (part,) in outer_rows((1, 0), 1, places, bits, normed_attn, right)]
        late["attn_far"] = swap(late["attn"][1], layout.low, "grad_attn_far")

    def out_terms(parts):
        *parts, late["attn"], right, late["final"] = tie(
            (*parts, late["attn"], branch_team, final)
        )
        late["out"] = outer_quarters(True, bits, attended, right)
        return parts

    def relays_on(parts):
        *parts, late["attn_far"], late["out"], gu_near[0], sent, gu_relay[0] = tie(
            (*parts, late["attn_far"], late["out"], gu_near[0], gu_near[1], gu_relay[0])
        )
        gu_near[1] = swap(sent, layout.low, "grad_gate_up_near_1")
        late["out_far"] = swap(late["out"][3], layout.low, "grad_out_far")
        return parts

    grad_normed_attn = layout.scatter_rows(
        lambda core: dot(part(grad_qkv, core), w_attn_own, NT), (attn_terms, out_terms, relays_on)
    )
    attn_parts, out_parts = late["attn"], late["out"]
    grad_normed_attn, final, out_far, attn_far, attn_sent = tie(
        (grad_normed_attn, late["final"], late["out_far"], late["attn_far"], attn_parts[3])
    )
    attn_relay = layout.relay_sum(attn_parts[0], attn_far, "grad_attn")
    attn_near = swap(attn_sent, layout.low, "grad_attn_near")
    final = layout.scatter_add(final)
    block_out = layout.from_team((middle + final).astype(BF16), "block_out")
    out_relay = layout.relay_sum(out_parts[2], out_far, "grad_out")
    out_near = swap(out_parts[1], layout.low, "grad_out_near")
    grad_input = grad_middle + norm_back(grad_normed_attn, x_wide, gain_attn)
    grad_rows = grad_input.astype(BF16)
    grad_input = layout.from_team(grad_rows, "grad_input").astype(F32)

    by_member = lambda a: a.reshape(members, weight_rows, -1)
    dealt = sum_parts(BF16, grad_rows, *zip(gu_own, gu_near, gu_relay))
    dealt = layout.exchange(by_member(jnp.concatenate(dealt)))
    (grad_attn,) = sum_parts(BF16, grad_rows, (attn_parts[2], attn_near, attn_relay))
    grad_attn = layout.rows_in(layout.exchange(by_member(grad_attn))).astype(F32)
    (grad_out,) = sum_parts(BF16, grad_rows, (out_parts[0], out_near, out_relay))
    grad_out = layout.cross(grad_out).astype(F32)
    (grad_down,) = sum_parts(F32, grad_rows, (down_parts[0], down_near, down_relay))
    grad_gate, grad_up = collect(places, dealt)

    def sum_kv(array):
        return array.reshape((KEY_VALUE_HEADS, -1) + array.shape[1:]).sum(1)

    def lay(array):
        return jnp.swapaxes(array, 0, 1).reshape(array.shape[1], -1)

    grad_query = lay(grad_attn[:, :, :query_width])
    grad_kv = sum_kv(grad_attn[:, :, query_width + padding :])
    grad_key = lay(grad_kv[:, :, :HEAD_WIDTH])
    grad_value = lay(grad_kv[:, :, HEAD_WIDTH:])

    def gain_gradient(gain, *terms):
        total = sum(jnp.sum(w.astype(F32) * grad, axis=1) for w, grad in terms)
        return total / gain.astype(F32)

    grad_norm_attn = gain_gradient(
        norm_attn, (w_query, grad_query), (key_weight, grad_key), (value_weight, grad_value)
    )
    grad_norm_mlp = gain_gradient(norm_mlp, (w_gate, grad_gate), (w_up, grad_up))

    return (
        block_out,
        grad_input,
        grad_norm_attn,
        grad_query,
        grad_key,
        grad_value,
        grad_out,
        grad_norm_mlp,
        grad_gate,
        grad_up,
        grad_down,
    )


def solution(mesh):
    layout = Layout(mesh)
    tokens = P("core", layout.ctx, None)
    rows = P(layout.all, None)
    line = P(layout.all)
    in_specs = (
        tokens, P(), P("core", None), line, rows, rows, rows, rows, line, rows, rows, rows, tokens,
    )
    out_specs = (tokens, tokens, line, rows, rows, rows, rows, line, rows, rows, rows)
    return jax.shard_map(
        functools.partial(shards, layout),
        mesh=layout.mesh,
        in_specs=in_specs,
        out_specs=out_specs,
        check_vma=False,
    )
```

time: 3340 us -> 634 us (0.19)
  waiting for transfers between devices: 2880 us -> 286 us
  matrix products: 214 us -> 28.1 us
  Pallas kernels: 0 us -> 122 us
  starting transfers between devices: 1.39 us -> 107 us
  local copies, waits for them, and re-layouts: 123 us -> 27.4 us
  blocking collectives: 79.2 us -> 0 us
    reduce_scatter x8 -> x0, waiting for transfers between devices: 2060 us -> none  [the longest x1 496 us: shards(): lax.psum_scatter(contract_rows(activated, upstream), ('ctx', 'fsdp'), sca...]
    all_gather x9 -> x4, waiting for transfers between devices: 689 us -> 0.03 us  [team_gather(): return lax.all_gather(array, ('core',) + self.mid, axis=0, tiled=True)]
    ppermute x0 -> x61, waiting for transfers between devices: none -> 272 us  [the longest x50 266 us: swap(): return lax.ppermute(array, axis, SWAP)]
    dot_general x77 -> x9, matrix products: 214 us -> 28.1 us  [dot(): return lax.dot_general(left, right, dims, preferred_element_type=F32)]
    unnamed x19 -> x4, waiting for transfers between devices: 128 us -> 0.07 us
    pallas_call x0 -> x16, Pallas kernels: none -> 122 us  [the longest x3 23.7 us: outer_rows(): pl.pallas_call(functools.partial(rows_kernel, sides, chunks), grid_spec=p...]
    unnamed x2 -> x0, blocking collectives: 79.2 us -> none
    ppermute x0 -> x61, starting transfers between devices: none -> 77.1 us  [the longest x50 60.3 us: swap(): return lax.ppermute(array, axis, SWAP)]
  transfers between devices with their start and end apart: 18 -> 69, of which waited for: 17 -> 35; matrix products, arithmetic and copies ran while one was open for 6% -> 12% of each run, Pallas kernels for 0% -> 15%
where the time goes in v1:
time: 634 us; the launch traced here: 627 us
  waiting for transfers between devices  286 us (45%)
  Pallas kernels  122 us (19%)
  starting transfers between devices  107 us (17%)
  other arithmetic  41.9 us (7%)
  matrix products  28.1 us (4%)
  local copies, waits for them, and re-layouts  27.4 us (4%)
  between operations  15.6 us (2%)
    ppermute x50, waiting for transfers between devices, swap(): return lax.ppermute(array, axis, SWAP)  266 us
    ppermute x50, starting transfers between devices, swap(): return lax.ppermute(array, axis, SWAP)  60.3 us
    all_to_all x4, starting transfers between devices, exchange(): return lax.all_to_all(array, self.mid + ('core',), 0, 0, tiled=True)  29 us
    dot_general x9, matrix products, dot(): return lax.dot_general(left, right, dims, preferred_element_type=F32)  28.1 us
    pallas_call x3, Pallas kernels, outer_rows(): pl.pallas_call(functools.partial(rows_kernel, sides, chunks), grid_spec=p...  23.7 us
    pallas_call x1, Pallas kernels, attend_backward(): pl.pallas_call(functools.partial(backward_kernel, heads), grid=(rows // b...  22.5 us
    pallas_call x1, Pallas kernels, feed_forward(): pl.pallas_call(feed_kernel, grid=(rows // block,), in_specs=[pl.BlockSpec...  17.6 us
    pallas_call x1, Pallas kernels, attend_forward(): pl.pallas_call(functools.partial(forward_kernel, heads), grid=(rows // bl...  14.5 us
  transfers between devices with their start and end apart: 69, of which 35 were waited for; matrix products, arithmetic and copies ran while one was open for 12% of the time, Pallas kernels for 15%

profile of v1, /device:TPU:0, one launch (start us, length us, event | category | flops | bytes accessed | tf_op | source)
XLA Modules:
  0.0 627.5 jit_solution(16056847719072599031)
XLA Ops:
  12.1 4.3 collective-permute-done.1
  17.6 10.3 %collective-permute-start.2 = (bf16[64,2688]{1,0:T(8,128)(2,1)S(1)}, bf16[64,2688]{1,0:T(8,128)(2,1)S(1)}, u32[]{:S(2)}, u32[]{:S(2)}) collective-permute-start(bf16[64,2688]{1,0:T(8,128)(2,1)S(1)} %fusion.20.own), channel_id=1, source_target_pairs={{0,16},{16,0},{1,17},{17,1},{2,18},{18,2},{3,19},{19,3},{4,20},{20... | collective-permute-start | bytes 1032200 | tf_op jit(solution)/shard_map/raw_far/ppermute | solution.py:43
  37.0 4.8 collective-permute-done.2.far
  45.9 5.3 collective-permute-done.5.corner
  56.9 15.7 %all-to-all-start = ((bf16[8,272,384]{2,1,0:T(8,128)(2,1)}), bf16[8,272,384]{2,1,0:T(8,128)(2,1)S(1)}, u32[]{:S(2)}, u32[]{:S(2)}) async-start(bf16[8,272,384]{2,1,0:T(8,128)(2,1)} %deal_attn.1), calls=%async_computation | async-start | bytes 3342336 | tf_op jit(solution)/shard_map/all_to_all | solution.py:617
  74.8 6.5 %collective-permute-done.10 = bf16[64,2048]{1,0:T(8,128)(2,1)S(1)} collective-permute-done((bf16[64,2048]{1,0:T(8,128)(2,1)S(1)}, bf16[64,2048]{1,0:T(8,128)(2,1)S(1)}, u32[]{:S(2)}, u32[]{:S(2)}) %collective-permute-start.10) | collective-permute-done | bytes 262176 | tf_op jit(solution)/shard_map/out_near/ppermute | solution.py:43
  81.3 16.0 %collective-permute-done.9 = bf16[64,2048]{1,0:T(8,128)(2,1)S(1)} collective-permute-done((bf16[64,2048]{1,0:T(8,128)(2,1)S(1)}, bf16[64,2048]{1,0:T(8,128)(2,1)S(1)}, u32[]{:S(2)}, u32[]{:S(2)}) %collective-permute-start.9) | collective-permute-done | bytes 262176 | tf_op jit(solution)/shard_map/out_far/ppermute | solution.py:43
  99.3 4.3 all-to-all-start.1
  111.7 9.6 %project.1 = (bf16[1024,2048]{1,0:T(8,128)(2,1)}, bf16[1024,256]{1,0:T(8,128)(2,1)}, bf16[1024,256]{1,0:T(8,128)(2,1)}, bf16[1024,256]{1,0:T(8,128)(2,1)}, bf16[...) custom-call(bf16[1024,2048]{1,0:T(8,128)(2,1)} %all-gather.5.cloned., ...), custom_call_target="tpu_custom_call" | custom-call | flops 1 | bytes 1 | tf_op jit(solution)/shard_map/project/pallas_call | solution.py:161
  121.3 31.1 %collective-permute-done.12 = bf16[176,2048]{1,0:T(8,128)(2,1)} collective-permute-done((bf16[176,2048]{1,0:T(8,128)(2,1)}, bf16[176,2048]{1,0:T(8,128)(2,1)}, u32[]{:S(2)}, u32[]{:S(2)}) %collective-permute-start.12) | collective-permute-done | bytes 720928 | tf_op jit(solution)/shard_map/down_far/ppermute | solution.py:43
  152.5 14.5 %attend_forward.1 = (bf16[1024,256]{1,0:T(8,128)(2,1)}, f32[8,1024]{1,0:T(8,128)}) custom-call(bf16[1024,256]{1,0:T(8,128)(2,1)} %get-tuple-element.162.q_ref, bf16[1024,256]{1,0:T(8,128)(2,1)} %get-tuple-element.163.k_ref, bf16[256,1024]{1,0:T(8,128)(2,1)} %get-tuple-element.164.vt_ref, s32[1,1024]{1,0:T(1,128)} %bitcast.226, s32[1,1024]{1,0:T(1,128)} %bitcast.224, ...), custom_call_target="tpu_custom_call" | custom-call | flops 1 | bytes 1 | tf_op jit(solution)/shard_map/attend_forward/pallas_call | solution.py:209
  172.3 4.5 collective-permute-done.15
  188.7 5.9 collective-permute-done.17
  196.0 9.6 %collective-permute-done.16 = bf16[2,128,1024]{2,1,0:T(8,128)(2,1)S(1)} collective-permute-done((bf16[2,128,1024]{2,1,0:T(8,128)(2,1)}, bf16[2,128,1024]{2,1,0:T(8,128)(2,1)S(1)}, u32[]{:S(2)}, u32[]{:S(2)}) %collective-permute-start.16) | collective-permute-done | bytes 524320 | tf_op jit(solution)/shard_map/sum_places_0/ppermute | solution.py:43
  205.8 15.4 %collective-permute-done.18.refs_1_ = bf16[2,128,1408]{2,1,0:T(8,128)(2,1)} collective-permute-done((bf16[2,128,1408]{2,1,0:T(8,128)(2,1)}, bf16[2,128,1408]{2,1,0:T(8,128)(2,1)}, u32[]{:S(2)}, u32[]{:S(2)}) %collective-permute-start.18) | collective-permute-done | bytes 720928 | tf_op jit(solution)/shard_map/gate_up_0_far/ppermute | solution.py:43
  223.2 5.0 collective-permute-done.20
  235.9 27.1 %collective-permute-done.23.refs_5_ = bf16[2,128,1408]{2,1,0:T(8,128)(2,1)} collective-permute-done((bf16[2,128,1408]{2,1,0:T(8,128)(2,1)}, bf16[2,128,1408]{2,1,0:T(8,128)(2,1)}, u32[]{:S(2)}, u32[]{:S(2)}) %collective-permute-start.23) | collective-permute-done | bytes 720928 | tf_op jit(solution)/shard_map/gate_up_1_far/ppermute | solution.py:43
  267.1 14.0 %collective-permute-done.25.refs_7_ = bf16[2,128,1408]{2,1,0:T(8,128)(2,1)} collective-permute-done((bf16[2,128,1408]{2,1,0:T(8,128)(2,1)}, bf16[2,128,1408]{2,1,0:T(8,128)(2,1)}, u32[]{:S(2)}, u32[]{:S(2)}) %collective-permute-start.25) | collective-permute-done | bytes 720928 | tf_op jit(solution)/shard_map/gate_up_1_corner/ppermute | solution.py:43
  281.2 17.6 %feed_forward.1 = (bf16[1024,704]{1,0:T(8,128)(2,1)}, bf16[1024,1408]{1,0:T(8,128)(2,1)}, bf16[2,4,2,128,1408]{4,3,2,1,0:T(8,128)(2,1)}) custom-call(s32[3]{0:T(128)} %pad_add_fusion.bits_ref, bf16[1024,2048]{1,0:T(8,128)(2,1)} %all-gather.7.cloned.1.call-done.n_ref.left_ref, bf16[1024,2048]{1,0:T(8,128)(2,1)} %all-gather.9.cloned.1.call-done.g_ref.right_ref, ...), custom_call_target="tpu_custom_call" | custom-call | flops 1 | bytes 1 | tf_op jit(solution)/shard_map/feed_forward/pallas_call | solution.py:337
  298.7 7.9 %outer_quarters.2 = (bf16[176,2048]{1,0:T(8,128)(2,1)}, bf16[176,2048]{1,0:T(8,128)(2,1)}, bf16[176,2048]{1,0:T(8,128)(2,1)}, bf16[176,2048]{1,0:T(8,128)(2,1)}) custom-call(s32[3]{0:T(128)} %pad_add_fusion.bits_ref, bf16[1024,704]{1,0:T(8,128)(2,1)} %get-tuple-element.214.left_ref, bf16[1024,2048]{1,0:T(8,128)(2,1)} %all-gather.9.cloned.1.call-done.g_ref.right_ref), custom_call_target="tpu_custom_call" | custom-call | flops 1 | bytes 1 | tf_op jit(solution)/shard_map/outer_quarters/pallas_call | solution.py:430
  306.7 6.5 %convolution_convert_fusion.3 = bf16[512,2048]{1,0:T(8,128)(2,1)S(1)} fusion(bf16[2048,1408]{1,0:T(8,128)(2,1)} %bitcast.233, bf16[1024,1408]{1,0:T(8,128)(2,1)S(1)} %copy-done.5, s32[]{:T(128)S(6)} %select_n.232), kind=kOutput, calls=%fused_computation.7 | convolution fusion | flops 2953838592 | bytes 9306116 | tf_op jit(solution)/shard_map/dot_general | solution.py:30
  313.3 4.1 collective-permute-done.26
  317.4 3.7 add_convert_fusion.2
  324.9 8.3 %outer_rows.3 = (bf16[2,128,1408]{2,1,0:T(8,128)(2,1)}, bf16[2,128,1408]{2,1,0:T(8,128)(2,1)}, bf16[2,128,1408]{2,1,0:T(8,128)(2,1)}, bf16[2,128,1408]{2,1,0:T(8,128)(2,1)}) custom-call(s32[3]{0:T(128)} %pad_add_fusion.bits_ref, bf16[1024,2048]{1,0:T(8,128)(2,1)} %all-gather.7.cloned.1.call-done.n_ref.left_ref, bf16[1024,1408]{1,0:T(8,128)(2,1)} %get-tuple-element.202.right_ref), custom_call_target="tpu_custom_call" | custom-call | flops 1 | bytes 1 | tf_op jit(solution)/shard_map/outer_rows/pallas_call | solution.py:387
  337.4 5.1 collective-permute-done.29
  344.4 8.5 %outer_rows.4 = (bf16[2,128,1408]{2,1,0:T(8,128)(2,1)}, bf16[2,128,1408]{2,1,0:T(8,128)(2,1)}, bf16[2,128,1408]{2,1,0:T(8,128)(2,1)}, bf16[2,128,1408]{2,1,0:T(8,128)(2,1)}) custom-call(s32[3]{0:T(128)} %pad_add_fusion.bits_ref, bf16[1024,2048]{1,0:T(8,128)(2,1)} %all-gather.7.cloned.1.call-done.n_ref.left_ref, bf16[1024,1408]{1,0:T(8,128)(2,1)} %get-tuple-element.202.right_ref), custom_call_target="tpu_custom_call" | custom-call | flops 1 | bytes 1 | tf_op jit(solution)/shard_map/outer_rows/pallas_call | solution.py:387
  356.6 15.6 %collective-permute-done.32 = bf16[2,128,1408]{2,1,0:T(8,128)(2,1)S(1)} collective-permute-done((bf16[2,128,1408]{2,1,0:T(8,128)(2,1)}, bf16[2,128,1408]{2,1,0:T(8,128)(2,1)S(1)}, u32[]{:S(2)}, u32[]{:S(2)}) %collective-permute-start.32) | collective-permute-done | bytes 720928 | tf_op jit(solution)/shard_map/grad_gate_up_far_0/ppermute | solution.py:43
  372.2 4.2 convolution_convert_fusion.2
  377.3 3.3 collective-permute-done.34
  384.0 11.2 %collective-permute-done.33 = bf16[2,128,1408]{2,1,0:T(8,128)(2,1)} collective-permute-done((bf16[2,128,1408]{2,1,0:T(8,128)(2,1)S(1)}, bf16[2,128,1408]{2,1,0:T(8,128)(2,1)}, u32[]{:S(2)}, u32[]{:S(2)}) %collective-permute-start.33) | collective-permute-done | bytes 720928 | tf_op jit(solution)/shard_map/grad_gate_up_far_1/ppermute | solution.py:43
  404.1 22.5 %attend_backward.1 = (bf16[1024,256]{1,0:T(8,128)(2,1)}, bf16[1024,128]{1,0:T(8,128)(2,1)}) custom-call(bf16[1024,256]{1,0:T(8,128)(2,1)} %get-tuple-element.162.q_ref, bf16[1024,256]{1,0:T(8,128)(2,1)} %convolution_convert_fusion.4.g_ref, bf16[1024,256]{1,0:T(8,128)(2,1)} %get-tuple-element.163.k_ref, bf16[1024,256]{1,0:T(8,128)(2,1)} %get-tuple-element.216.v_ref, ...), custom_call_target="tpu_custom_call" | custom-call | flops 1 | bytes 1 | tf_op jit(solution)/shard_map/attend_backward/pallas_call | solution.py:280
  440.6 6.9 %outer_rows.5 = (bf16[4,128,384]{2,1,0:T(8,128)(2,1)}, bf16[4,128,384]{2,1,0:T(8,128)(2,1)}, bf16[4,128,384]{2,1,0:T(8,128)(2,1)}, bf16[4,128,384]{2,1,0:T(8,128)(2,1)}) custom-call(s32[3]{0:T(128)} %pad_add_fusion.bits_ref, bf16[1024,2048]{1,0:T(8,128)(2,1)} %get-tuple-element.227.left_ref, bf16[1024,384]{1,0:T(8,128)(2,1)} %copy-done.6), custom_call_target="tpu_custom_call" | custom-call | flops 1 | bytes 1 | tf_op jit(solution)/shard_map/outer_rows/pallas_call | solution.py:387
  450.8 7.2 %collective-permute-done.40 = bf16[128,1024]{1,0:T(8,128)(2,1)} collective-permute-done((bf16[128,1024]{1,0:T(8,128)(2,1)}, bf16[128,1024]{1,0:T(8,128)(2,1)}, u32[]{:S(2)}, u32[]{:S(2)}) %collective-permute-start.40) | collective-permute-done | bytes 262176 | tf_op jit(solution)/shard_map/sum_places_1/ppermute | solution.py:43
  463.1 5.8 outer_quarters.3
  468.9 3.7 collective-permute-done.42
  475.4 11.6 %collective-permute-done.41 = bf16[2,128,1024]{2,1,0:T(8,128)(2,1)S(1)} collective-permute-done((bf16[2,128,1024]{2,1,0:T(8,128)(2,1)}, bf16[2,128,1024]{2,1,0:T(8,128)(2,1)S(1)}, u32[]{:S(2)}, u32[]{:S(2)}) %collective-permute-start.41) | collective-permute-done | bytes 524320 | tf_op jit(solution)/shard_map/sum_places_0/ppermute | solution.py:43
  490.6 3.2 collective-permute-start.59
  496.6 6.1 collective-permute-done.47
  510.5 18.8 %collective-permute-done.60.refs_2_ = bf16[176,2048]{1,0:T(8,128)(2,1)} collective-permute-done((bf16[176,2048]{1,0:T(8,128)(2,1)S(1)}, bf16[176,2048]{1,0:T(8,128)(2,1)}, u32[]{:S(2)}, u32[]{:S(2)}) %collective-permute-start.60) | collective-permute-done | bytes 720928 | tf_op jit(solution)/shard_map/grad_down_relay/ppermute | solution.py:43
  531.4 18.9 %collective-permute-done.56.refs_2_ = bf16[64,2048]{1,0:T(8,128)(2,1)S(1)} collective-permute-done((bf16[64,2048]{1,0:T(8,128)(2,1)S(1)}, bf16[64,2048]{1,0:T(8,128)(2,1)S(1)}, u32[]{:S(2)}, u32[]{:S(2)}) %collective-permute-start.56) | collective-permute-done | bytes 262176 | tf_op jit(solution)/shard_map/grad_out_relay/ppermute | solution.py:43
  550.3 3.6 collective-permute-start.51
  553.8 7.3 %collective-permute-done.54.refs_2_ = bf16[4,128,384]{2,1,0:T(8,128)(2,1)S(1)} collective-permute-done((bf16[4,128,384]{2,1,0:T(8,128)(2,1)S(1)}, bf16[4,128,384]{2,1,0:T(8,128)(2,1)S(1)}, u32[]{:S(2)}, u32[]{:S(2)}) %collective-permute-start.54) | collective-permute-done | bytes 393248 | tf_op jit(solution)/shard_map/grad_attn_relay/ppermute | solution.py:43
  568.5 3.7 collective-permute-start.49
  574.4 3.5 all-to-all-start.2
  581.7 3.6 sum_parts.6
  589.0 5.6 all-to-all-start.3
  602.3 10.9 %all-to-all-done.3.in_ref = bf16[8,64,1408]{2,1,0:T(8,128)(2,1)S(1)} async-done(((bf16[8,64,1408]{2,1,0:T(8,128)(2,1)}), bf16[8,64,1408]{2,1,0:T(8,128)(2,1)S(1)}, u32[]{:S(2)}, u32[]{:S(2)}) %all-to-all-start.3) | async-done | bytes 1441824 | tf_op jit(solution)/shard_map/all_to_all | solution.py:617
  614.3 3.5 collect.1
  (366 shorter events, 165.7 us)
Async XLA Ops:
  7.3 104.5 %all-gather.5.cloned.1.call-start = ((), (), s32[]{:S(2)}) async-start(), calls=%async_computation.4 | async-start | bytes 4718592 | tf_op jit(solution)/shard_map/all_gather | solution.py:581
  17.6 24.2 %collective-permute-start.2 = (bf16[64,2688]{1,0:T(8,128)(2,1)S(1)}, bf16[64,2688]{1,0:T(8,128)(2,1)S(1)}, u32[]{:S(2)}, u32[]{:S(2)}) collective-permute-start(bf16[64,2688]{1,0:T(8,128)(2,1)S(1)} %fusion.20.own), channel_id=1, source_target_pairs={{0,16},{16,0},{1,17},{17,1},{2,18},{18,2},{3,19},{19,3},{4,20},{20... | collective-permute-start | bytes 1032200 | tf_op jit(solution)/shard_map/raw_far/ppermute | solution.py:43
  56.9 42.4 %all-to-all-start = ((bf16[8,272,384]{2,1,0:T(8,128)(2,1)}), bf16[8,272,384]{2,1,0:T(8,128)(2,1)S(1)}, u32[]{:S(2)}, u32[]{:S(2)}) async-start(bf16[8,272,384]{2,1,0:T(8,128)(2,1)} %deal_attn.1), calls=%async_computation | async-start | bytes 3342336 | tf_op jit(solution)/shard_map/all_to_all | solution.py:617
  73.1 24.1 %collective-permute-start.9 = (bf16[64,2048]{1,0:T(8,128)(2,1)S(1)}, bf16[64,2048]{1,0:T(8,128)(2,1)S(1)}, u32[]{:S(2)}, u32[]{:S(2)}) collective-permute-start(bf16[64,2048]{1,0:T(8,128)(2,1)S(1)} %broadcast_select_fusion.4), channel_id=1, source_target_pairs={{0,16},{16,0},{1,17},{17,1},{2,18},{18,2},{3,19},{19,3},{4,20},{20... | collective-permute-start | bytes 786440 | tf_op jit(solution)/shard_map/out_far/ppermute | solution.py:43
  99.3 68.0 %all-to-all-start.1 = ((bf16[8,64,1408]{2,1,0:T(8,128)(2,1)}), bf16[8,64,1408]{2,1,0:T(8,128)(2,1)}, u32[]{:S(2)}, u32[]{:S(2)}) async-start(bf16[8,64,1408]{2,1,0:T(8,128)(2,1)} %deal.1), calls=%async_computation.1 | async-start | bytes 2883584 | tf_op jit(solution)/shard_map/all_to_all | solution.py:617
  103.6 163.5 %all-gather.9.cloned.1.call-start = ((), (), s32[]{:S(2)}) async-start(), calls=%async_computation.6 | async-start | bytes 4718592 | tf_op jit(solution)/shard_map/all_gather | solution.py:581
  105.7 46.8 %collective-permute-start.12 = (bf16[176,2048]{1,0:T(8,128)(2,1)}, bf16[176,2048]{1,0:T(8,128)(2,1)}, u32[]{:S(2)}, u32[]{:S(2)}) collective-permute-start(bf16[176,2048]{1,0:T(8,128)(2,1)} %param.24), channel_id=1, source_target_pairs={{0,16},{16,0},{1,17},{17,1},{2,18},{18,2},{3,19},{19,3},{4,20},{20... | collective-permute-start | bytes 2162696 | tf_op jit(solution)/shard_map/down_far/ppermute | solution.py:43
  107.0 45.5 %collective-permute-start.13 = (bf16[176,2048]{1,0:T(8,128)(2,1)}, bf16[176,2048]{1,0:T(8,128)(2,1)}, u32[]{:S(2)}, u32[]{:S(2)}) collective-permute-start(bf16[176,2048]{1,0:T(8,128)(2,1)} %param.24), channel_id=1, source_target_pairs={{0,2},{2,0},{1,3},{3,1},{4,6},{6,4},{5,7},{7,5},{8,10},{10,8},{9,1... | collective-permute-start | bytes 2162696 | tf_op jit(solution)/shard_map/down_near/ppermute | solution.py:43
  109.5 171.6 %all-gather.7.cloned.1.call-start = ((), (), s32[]{:S(2)}) async-start(), calls=%async_computation.5 | async-start | bytes 4718592 | tf_op jit(solution)/shard_map/all_gather | solution.py:581
  110.1 42.4 %collective-permute-start.11 = (bf16[64,2048]{1,0:T(8,128)(2,1)S(1)}, bf16[64,2048]{1,0:T(8,128)(2,1)S(1)}, u32[]{:S(2)}, u32[]{:S(2)}) collective-permute-start(bf16[64,2048]{1,0:T(8,128)(2,1)S(1)} %collective-permute-done.9), channel_id=1, source_target_pairs={{0,2},{2,0},{1,3},{3,1},{4,6},{6,4},{5,7},{7,5},{8,10},{10,8},{9,1... | collective-permute-start | bytes 786440 | tf_op jit(solution)/shard_map/out_corner/ppermute | solution.py:43
  152.5 17.8 %collective-permute-start.14 = (bf16[176,2048]{1,0:T(8,128)(2,1)}, bf16[176,2048]{1,0:T(8,128)(2,1)}, u32[]{:S(2)}, u32[]{:S(2)}) collective-permute-start(bf16[176,2048]{1,0:T(8,128)(2,1)} %collective-permute-done.12), channel_id=1, source_target_pairs={{0,2},{2,0},{1,3},{3,1},{4,6},{6,4},{5,7},{7,5},{8,10},{10,8},{9,1... | collective-permute-start | bytes 2162696 | tf_op jit(solution)/shard_map/down_corner/ppermute | solution.py:43
  180.3 14.3 %collective-permute-start.17 = (bf16[2,128,1024]{2,1,0:T(8,128)(2,1)}, bf16[2,128,1024]{2,1,0:T(8,128)(2,1)}, u32[]{:S(2)}, u32[]{:S(2)}) collective-permute-start(bf16[2,128,1024]{2,1,0:T(8,128)(2,1)} %dynamic-slice_bitcast_fusion.8), channel_id=1, source_target_pairs={{0,4},{4,0},{1,5},{5,1},{2,6},{6,2},{3,7},{7,3},{8,12},{12,8},{9,1... | collective-permute-start | bytes 1572872 | tf_op jit(solution)/shard_map/sum_places_0/ppermute | solution.py:43
  182.5 23.1 %collective-permute-start.16 = (bf16[2,128,1024]{2,1,0:T(8,128)(2,1)}, bf16[2,128,1024]{2,1,0:T(8,128)(2,1)S(1)}, u32[]{:S(2)}, u32[]{:S(2)}) collective-permute-start(bf16[2,128,1024]{2,1,0:T(8,128)(2,1)} %dynamic-slice_bitcast_fusion.9), channel_id=1, source_target_pairs={{0,8},{8,0},{1,9},{9,1},{2,10},{10,2},{3,11},{11,3},{4,12},{12,4},... | collective-permute-start | bytes 1572872 | tf_op jit(solution)/shard_map/sum_places_0/ppermute | solution.py:43
  186.9 34.3 %collective-permute-start.18 = (bf16[2,128,1408]{2,1,0:T(8,128)(2,1)}, bf16[2,128,1408]{2,1,0:T(8,128)(2,1)}, u32[]{:S(2)}, u32[]{:S(2)}) collective-permute-start(bf16[2,128,1408]{2,1,0:T(8,128)(2,1)} %bitcast.27.refs_0_), channel_id=1, source_target_pairs={{0,16},{16,0},{1,17},{17,1},{2,18},{18,2},{3,19},{19,3},{4,20},{20... | collective-permute-start | bytes 2162696 | tf_op jit(solution)/shard_map/gate_up_0_far/ppermute | solution.py:43
  188.4 32.8 %collective-permute-start.19 = (bf16[2,128,1408]{2,1,0:T(8,128)(2,1)}, bf16[2,128,1408]{2,1,0:T(8,128)(2,1)}, u32[]{:S(2)}, u32[]{:S(2)}) collective-permute-start(bf16[2,128,1408]{2,1,0:T(8,128)(2,1)} %bitcast.27.refs_0_), channel_id=1, source_target_pairs={{0,2},{2,0},{1,3},{3,1},{4,6},{6,4},{5,7},{7,5},{8,10},{10,8},{9,1... | collective-permute-start | bytes 2162696 | tf_op jit(solution)/shard_map/gate_up_0_near/ppermute | solution.py:43
  230.4 164.7 %all-gather.11.cloned.1.call-start = ((), (), s32[]{:S(2)}) async-start(), calls=%async_computation.7 | async-start | bytes 4718592 | tf_op jit(solution)/shard_map/all_gather | solution.py:581
  230.7 32.3 %collective-permute-start.23 = (bf16[2,128,1408]{2,1,0:T(8,128)(2,1)}, bf16[2,128,1408]{2,1,0:T(8,128)(2,1)}, u32[]{:S(2)}, u32[]{:S(2)}) collective-permute-start(bf16[2,128,1408]{2,1,0:T(8,128)(2,1)} %bitcast.28.refs_4_), channel_id=1, source_target_pairs={{0,16},{16,0},{1,17},{17,1},{2,18},{18,2},{3,19},{19,3},{4,20},{20... | collective-permute-start | bytes 2162696 | tf_op jit(solution)/shard_map/gate_up_1_far/ppermute | solution.py:43
  233.8 33.4 %collective-permute-start.24 = (bf16[2,128,1408]{2,1,0:T(8,128)(2,1)}, bf16[2,128,1408]{2,1,0:T(8,128)(2,1)}, u32[]{:S(2)}, u32[]{:S(2)}) collective-permute-start(bf16[2,128,1408]{2,1,0:T(8,128)(2,1)} %bitcast.28.refs_4_), channel_id=1, source_target_pairs={{0,2},{2,0},{1,3},{3,1},{4,6},{6,4},{5,7},{7,5},{8,10},{10,8},{9,1... | collective-permute-start | bytes 2162696 | tf_op jit(solution)/shard_map/gate_up_1_near/ppermute | solution.py:43
  234.1 33.0 %collective-permute-start.22 = (bf16[2,128,1408]{2,1,0:T(8,128)(2,1)}, bf16[2,128,1408]{2,1,0:T(8,128)(2,1)}, u32[]{:S(2)}, u32[]{:S(2)}) collective-permute-start(bf16[2,128,1408]{2,1,0:T(8,128)(2,1)} %collective-permute-done.18.refs_1_), channel_id=1, source_target_pairs={{0,2},{2,0},{1,3},{3,1},{4,6},{6,4},{5,7},{7,5},{8,10},{10,8},{9,1... | collective-permute-start | bytes 2162696 | tf_op jit(solution)/shard_map/gate_up_0_corner/ppermute | solution.py:43
  263.0 18.2 %collective-permute-start.25 = (bf16[2,128,1408]{2,1,0:T(8,128)(2,1)}, bf16[2,128,1408]{2,1,0:T(8,128)(2,1)}, u32[]{:S(2)}, u32[]{:S(2)}) collective-permute-start(bf16[2,128,1408]{2,1,0:T(8,128)(2,1)} %collective-permute-done.23.refs_5_), channel_id=1, source_target_pairs={{0,2},{2,0},{1,3},{3,1},{4,6},{6,4},{5,7},{7,5},{8,10},{10,8},{9,1... | collective-permute-start | bytes 2162696 | tf_op jit(solution)/shard_map/gate_up_1_corner/ppermute | solution.py:43
  324.6 17.8 %collective-permute-start.29 = (bf16[176,2048]{1,0:T(8,128)(2,1)}, bf16[176,2048]{1,0:T(8,128)(2,1)S(1)}, u32[]{:S(2)}, u32[]{:S(2)}) collective-permute-start(bf16[176,2048]{1,0:T(8,128)(2,1)} %get-tuple-element.199), channel_id=1, source_target_pairs={{0,2},{2,0},{1,3},{3,1},{4,6},{6,4},{5,7},{7,5},{8,10},{10,8},{9,1... | collective-permute-start | bytes 2162696 | tf_op jit(solution)/shard_map/grad_down_far/ppermute | solution.py:43
  355.8 16.4 %collective-permute-start.32 = (bf16[2,128,1408]{2,1,0:T(8,128)(2,1)}, bf16[2,128,1408]{2,1,0:T(8,128)(2,1)S(1)}, u32[]{:S(2)}, u32[]{:S(2)}) collective-permute-start(bf16[2,128,1408]{2,1,0:T(8,128)(2,1)} %get-tuple-element.208), channel_id=1, source_target_pairs={{0,2},{2,0},{1,3},{3,1},{4,6},{6,4},{5,7},{7,5},{8,10},{10,8},{9,1... | collective-permute-start | bytes 2162696 | tf_op jit(solution)/shard_map/grad_gate_up_far_0/ppermute | solution.py:43
  376.5 18.7 %collective-permute-start.33 = (bf16[2,128,1408]{2,1,0:T(8,128)(2,1)S(1)}, bf16[2,128,1408]{2,1,0:T(8,128)(2,1)}, u32[]{:S(2)}, u32[]{:S(2)}) collective-permute-start(bf16[2,128,1408]{2,1,0:T(8,128)(2,1)S(1)} %copy-done.62), channel_id=1, source_target_pairs={{0,2},{2,0},{1,3},{3,1},{4,6},{6,4},{5,7},{7,5},{8,10},{10,8},{9,1... | collective-permute-start | bytes 2162696 | tf_op jit(solution)/shard_map/grad_gate_up_far_1/ppermute | solution.py:43
  395.2 32.8 %collective-permute-start.37 = (bf16[176,2048]{1,0:T(8,128)(2,1)}, bf16[176,2048]{1,0:T(8,128)(2,1)S(1)}, u32[]{:S(2)}, u32[]{:S(2)}) collective-permute-start(bf16[176,2048]{1,0:T(8,128)(2,1)} %get-tuple-element.223), channel_id=1, source_target_pairs={{0,2},{2,0},{1,3},{3,1},{4,6},{6,4},{5,7},{7,5},{8,10},{10,8},{9,1... | collective-permute-start | bytes 2162696 | tf_op jit(solution)/shard_map/grad_down_near/ppermute | solution.py:43
  398.4 29.5 %collective-permute-start.35 = (bf16[2,128,1024]{2,1,0:T(8,128)(2,1)S(1)}, bf16[2,128,1024]{2,1,0:T(8,128)(2,1)S(1)}, u32[]{:S(2)}, u32[]{:S(2)}) collective-permute-start(bf16[2,128,1024]{2,1,0:T(8,128)(2,1)S(1)} %get-tuple-element.307), channel_id=1, source_target_pairs={{0,8},{8,0},{1,9},{9,1},{2,10},{10,2},{3,11},{11,3},{4,12},{12,4},... | collective-permute-start | bytes 1572872 | tf_op jit(solution)/shard_map/sum_places_0/ppermute | solution.py:43
  400.7 27.3 %collective-permute-start.36 = (bf16[2,128,1024]{2,1,0:T(8,128)(2,1)S(1)}, bf16[2,128,1024]{2,1,0:T(8,128)(2,1)S(1)}, u32[]{:S(2)}, u32[]{:S(2)}) collective-permute-start(bf16[2,128,1024]{2,1,0:T(8,128)(2,1)S(1)} %get-tuple-element.305), channel_id=1, source_target_pairs={{0,4},{4,0},{1,5},{5,1},{2,6},{6,2},{3,7},{7,3},{8,12},{12,8},{9,1... | collective-permute-start | bytes 1572872 | tf_op jit(solution)/shard_map/sum_places_0/ppermute | solution.py:43
  430.6 16.9 %collective-permute-start.38 = (bf16[512,2048]{1,0:T(8,128)(2,1)}, bf16[512,2048]{1,0:T(8,128)(2,1)}, u32[]{:S(2)}, u32[]{:S(2)}) collective-permute-start(bf16[512,2048]{1,0:T(8,128)(2,1)} %convolution_convert_fusion.1), channel_id=1, source_target_pairs={{0,1},{1,0},{2,3},{3,2},{4,5},{5,4},{6,7},{7,6},{8,9},{9,8},{10,11... | collective-permute-start | bytes 6291464 | tf_op jit(solution)/shard_map/sum_cores/ppermute | solution.py:43
  433.2 54.0 %collective-permute-start.45 = (bf16[2,128,1408]{2,1,0:T(8,128)(2,1)}, bf16[2,128,1408]{2,1,0:T(8,128)(2,1)}, u32[]{:S(2)}, u32[]{:S(2)}) collective-permute-start(bf16[2,128,1408]{2,1,0:T(8,128)(2,1)} %add_convert_fusion.6), channel_id=1, source_target_pairs={{0,16},{16,0},{1,17},{17,1},{2,18},{18,2},{3,19},{19,3},{4,20},{20... | collective-permute-start | bytes 2162696 | tf_op jit(solution)/shard_map/grad_gate_up_0_relay/ppermute | solution.py:43
  436.8 21.1 %collective-permute-start.40 = (bf16[128,1024]{1,0:T(8,128)(2,1)}, bf16[128,1024]{1,0:T(8,128)(2,1)}, u32[]{:S(2)}, u32[]{:S(2)}) collective-permute-start(bf16[128,1024]{1,0:T(8,128)(2,1)} %get-tuple-element.319), channel_id=1, source_target_pairs={{0,8},{8,0},{1,9},{9,1},{2,10},{10,2},{3,11},{11,3},{4,12},{12,4},... | collective-permute-start | bytes 786440 | tf_op jit(solution)/shard_map/sum_places_1/ppermute | solution.py:43
  438.4 19.5 %collective-permute-start.39 = (bf16[128,1024]{1,0:T(8,128)(2,1)}, bf16[128,1024]{1,0:T(8,128)(2,1)}, u32[]{:S(2)}, u32[]{:S(2)}) collective-permute-start(bf16[128,1024]{1,0:T(8,128)(2,1)} %get-tuple-element.321), channel_id=1, source_target_pairs={{0,4},{4,0},{1,5},{5,1},{2,6},{6,2},{3,7},{7,3},{8,12},{12,8},{9,1... | collective-permute-start | bytes 786440 | tf_op jit(solution)/shard_map/sum_places_1/ppermute | solution.py:43
  439.0 48.2 %collective-permute-start.44 = (bf16[2,128,1408]{2,1,0:T(8,128)(2,1)}, bf16[2,128,1408]{2,1,0:T(8,128)(2,1)S(1)}, u32[]{:S(2)}, u32[]{:S(2)}) collective-permute-start(bf16[2,128,1408]{2,1,0:T(8,128)(2,1)} %get-tuple-element.244), channel_id=1, source_target_pairs={{0,2},{2,0},{1,3},{3,1},{4,6},{6,4},{5,7},{7,5},{8,10},{10,8},{9,1... | collective-permute-start | bytes 2162696 | tf_op jit(solution)/shard_map/grad_gate_up_near_0/ppermute | solution.py:43
  460.1 26.8 %collective-permute-start.41 = (bf16[2,128,1024]{2,1,0:T(8,128)(2,1)}, bf16[2,128,1024]{2,1,0:T(8,128)(2,1)S(1)}, u32[]{:S(2)}, u32[]{:S(2)}) collective-permute-start(bf16[2,128,1024]{2,1,0:T(8,128)(2,1)} %dynamic-slice_bitcast_fusion.1), channel_id=1, source_target_pairs={{0,8},{8,0},{1,9},{9,1},{2,10},{10,2},{3,11},{11,3},{4,12},{12,4},... | collective-permute-start | bytes 1572872 | tf_op jit(solution)/shard_map/sum_places_0/ppermute | solution.py:43
  462.9 66.4 %collective-permute-start.60 = (bf16[176,2048]{1,0:T(8,128)(2,1)S(1)}, bf16[176,2048]{1,0:T(8,128)(2,1)}, u32[]{:S(2)}, u32[]{:S(2)}) collective-permute-start(bf16[176,2048]{1,0:T(8,128)(2,1)S(1)} %add_convert_fusion.4), channel_id=1, source_target_pairs={{0,16},{16,0},{1,17},{17,1},{2,18},{18,2},{3,19},{19,3},{4,20},{20... | collective-permute-start | bytes 2162696 | tf_op jit(solution)/shard_map/grad_down_relay/ppermute | solution.py:43
  472.6 14.6 %collective-permute-start.43 = (bf16[4,128,384]{2,1,0:T(8,128)(2,1)}, bf16[4,128,384]{2,1,0:T(8,128)(2,1)S(1)}, u32[]{:S(2)}, u32[]{:S(2)}) collective-permute-start(bf16[4,128,384]{2,1,0:T(8,128)(2,1)} %get-tuple-element.230), channel_id=1, source_target_pairs={{0,2},{2,0},{1,3},{3,1},{4,6},{6,4},{5,7},{7,5},{8,10},{10,8},{9,1... | collective-permute-start | bytes 1179656 | tf_op jit(solution)/shard_map/grad_attn_far/ppermute | solution.py:43
  488.4 14.3 %collective-permute-start.47 = (bf16[128,1024]{1,0:T(8,128)(2,1)S(1)}, bf16[128,1024]{1,0:T(8,128)(2,1)S(1)}, u32[]{:S(2)}, u32[]{:S(2)}) collective-permute-start(bf16[128,1024]{1,0:T(8,128)(2,1)S(1)} %dynamic-slice_bitcast_fusion.14), channel_id=1, source_target_pairs={{0,8},{8,0},{1,9},{9,1},{2,10},{10,2},{3,11},{11,3},{4,12},{12,4},... | collective-permute-start | bytes 786440 | tf_op jit(solution)/shard_map/sum_places_1/ppermute | solution.py:43
  490.6 90.2 %collective-permute-start.59 = (bf16[2,128,1408]{2,1,0:T(8,128)(2,1)}, bf16[2,128,1408]{2,1,0:T(8,128)(2,1)}, u32[]{:S(2)}, u32[]{:S(2)}) collective-permute-start(bf16[2,128,1408]{2,1,0:T(8,128)(2,1)} %add_convert_fusion.5), channel_id=1, source_target_pairs={{0,16},{16,0},{1,17},{17,1},{2,18},{18,2},{3,19},{19,3},{4,20},{20... | collective-permute-start | bytes 2162696 | tf_op jit(solution)/shard_map/grad_gate_up_1_relay/ppermute | solution.py:43
  495.7 35.1 %collective-permute-start.55 = (bf16[64,2048]{1,0:T(8,128)(2,1)S(1)}, bf16[64,2048]{1,0:T(8,128)(2,1)S(1)}, u32[]{:S(2)}, u32[]{:S(2)}) collective-permute-start(bf16[64,2048]{1,0:T(8,128)(2,1)S(1)} %copy-done.64), channel_id=1, source_target_pairs={{0,2},{2,0},{1,3},{3,1},{4,6},{6,4},{5,7},{7,5},{8,10},{10,8},{9,1... | collective-permute-start | bytes 786440 | tf_op jit(solution)/shard_map/grad_out_near/ppermute | solution.py:43
  503.8 46.4 %collective-permute-start.56 = (bf16[64,2048]{1,0:T(8,128)(2,1)S(1)}, bf16[64,2048]{1,0:T(8,128)(2,1)S(1)}, u32[]{:S(2)}, u32[]{:S(2)}) collective-permute-start(bf16[64,2048]{1,0:T(8,128)(2,1)S(1)} %add_convert_fusion.10), channel_id=1, source_target_pairs={{0,16},{16,0},{1,17},{17,1},{2,18},{18,2},{3,19},{19,3},{4,20},{20... | collective-permute-start | bytes 786440 | tf_op jit(solution)/shard_map/grad_out_relay/ppermute | solution.py:43
  504.0 57.1 %collective-permute-start.54 = (bf16[4,128,384]{2,1,0:T(8,128)(2,1)S(1)}, bf16[4,128,384]{2,1,0:T(8,128)(2,1)S(1)}, u32[]{:S(2)}, u32[]{:S(2)}) collective-permute-start(bf16[4,128,384]{2,1,0:T(8,128)(2,1)S(1)} %add_convert_fusion.9), channel_id=1, source_target_pairs={{0,16},{16,0},{1,17},{17,1},{2,18},{18,2},{3,19},{19,3},{4,20},{20... | collective-permute-start | bytes 1179656 | tf_op jit(solution)/shard_map/grad_attn_relay/ppermute | solution.py:43
  529.3 51.5 %collective-permute-start.58 = (bf16[2,128,1408]{2,1,0:T(8,128)(2,1)}, bf16[2,128,1408]{2,1,0:T(8,128)(2,1)S(1)}, u32[]{:S(2)}, u32[]{:S(2)}) collective-permute-start(bf16[2,128,1408]{2,1,0:T(8,128)(2,1)} %get-tuple-element.274), channel_id=1, source_target_pairs={{0,2},{2,0},{1,3},{3,1},{4,6},{6,4},{5,7},{7,5},{8,10},{10,8},{9,1... | collective-permute-start | bytes 2162696 | tf_op jit(solution)/shard_map/grad_gate_up_near_1/ppermute | solution.py:43
  530.7 37.7 %collective-permute-start.53 = (bf16[4,128,384]{2,1,0:T(8,128)(2,1)S(1)}, bf16[4,128,384]{2,1,0:T(8,128)(2,1)S(1)}, u32[]{:S(2)}, u32[]{:S(2)}) collective-permute-start(bf16[4,128,384]{2,1,0:T(8,128)(2,1)S(1)} %copy-done.63), channel_id=1, source_target_pairs={{0,2},{2,0},{1,3},{3,1},{4,6},{6,4},{5,7},{7,5},{8,10},{10,8},{9,1... | collective-permute-start | bytes 1179656 | tf_op jit(solution)/shard_map/grad_attn_near/ppermute | solution.py:43
  550.3 27.6 %collective-permute-start.51 = (bf16[64,2048]{1,0:T(8,128)(2,1)}, bf16[64,2048]{1,0:T(8,128)(2,1)}, u32[]{:S(2)}, u32[]{:S(2)}) collective-permute-start(bf16[64,2048]{1,0:T(8,128)(2,1)} %get-tuple-element.313), channel_id=1, source_target_pairs={{0,0},{1,16},{2,2},{3,18},{16,1},{17,17},{18,3},{19,19},{4,4},{5,2... | collective-permute-start | bytes 786440 | tf_op jit(solution)/shard_map/grad_input/ppermute | solution.py:561
  561.1 17.3 %collective-permute-start.52 = (bf16[64,2048]{1,0:T(8,128)(2,1)S(1)}, bf16[64,2048]{1,0:T(8,128)(2,1)}, u32[]{:S(2)}, u32[]{:S(2)}) collective-permute-start(bf16[64,2048]{1,0:T(8,128)(2,1)S(1)} %get-tuple-element.314), channel_id=1, source_target_pairs={{0,2},{1,18},{2,0},{3,16},{16,3},{17,19},{18,1},{19,17},{4,6},{5,2... | collective-permute-start | bytes 786440 | tf_op jit(solution)/shard_map/grad_input/ppermute | solution.py:561
  568.5 26.1 %collective-permute-start.49 = (bf16[64,2048]{1,0:T(8,128)(2,1)}, bf16[64,2048]{1,0:T(8,128)(2,1)}, u32[]{:S(2)}, u32[]{:S(2)}) collective-permute-start(bf16[64,2048]{1,0:T(8,128)(2,1)} %get-tuple-element.317), channel_id=1, source_target_pairs={{0,0},{1,16},{2,2},{3,18},{16,1},{17,17},{18,3},{19,19},{4,4},{5,2... | collective-permute-start | bytes 786440 | tf_op jit(solution)/shard_map/block_out/ppermute | solution.py:561
  574.4 14.6 %all-to-all-start.2 = ((bf16[8,64,384]{2,1,0:T(8,128)(2,1)}), bf16[8,64,384]{2,1,0:T(8,128)(2,1)S(1)}, u32[]{:S(2)}, u32[]{:S(2)}) async-start(bf16[8,64,384]{2,1,0:T(8,128)(2,1)} %bitcast.215), calls=%async_computation.2 | async-start | bytes 786432 | tf_op jit(solution)/shard_map/all_to_all | solution.py:617
  577.8 16.8 %collective-permute-start.50 = (bf16[64,2048]{1,0:T(8,128)(2,1)}, bf16[64,2048]{1,0:T(8,128)(2,1)}, u32[]{:S(2)}, u32[]{:S(2)}) collective-permute-start(bf16[64,2048]{1,0:T(8,128)(2,1)} %get-tuple-element.318), channel_id=1, source_target_pairs={{0,2},{1,18},{2,0},{3,16},{16,3},{17,19},{18,1},{19,17},{4,6},{5,2... | collective-permute-start | bytes 786440 | tf_op jit(solution)/shard_map/block_out/ppermute | solution.py:561
  578.4 19.2 %collective-permute-start.57 = (bf16[64,2048]{1,0:T(8,128)(2,1)S(1)}, bf16[64,2048]{1,0:T(8,128)(2,1)}, u32[]{:S(2)}, u32[]{:S(2)}) collective-permute-start(bf16[64,2048]{1,0:T(8,128)(2,1)S(1)} %copy-done.26), channel_id=1, source_target_pairs={{1,16},{16,1},{3,18},{18,3},{5,20},{20,5},{7,22},{22,7},{9,24},{24... | collective-permute-start | bytes 786440 | tf_op jit(solution)/shard_map/ppermute | solution.py:556
  589.0 24.2 %all-to-all-start.3 = ((bf16[8,64,1408]{2,1,0:T(8,128)(2,1)}), bf16[8,64,1408]{2,1,0:T(8,128)(2,1)S(1)}, u32[]{:S(2)}, u32[]{:S(2)}) async-start(bf16[8,64,1408]{2,1,0:T(8,128)(2,1)} %bitcast.92), calls=%async_computation.3 | async-start | bytes 2883584 | tf_op jit(solution)/shard_map/all_to_all | solution.py:617
  (87 other events, 962.0 us)
Sparse Core Ops, SparseCore 0:
  17.5 53.6 all-gather.4
  109.7 46.4 all-gather.8
  230.6 43.4 all-gather.6
  355.9 28.6 all-gather.10

commit v2 on v1

--- a/solution.py
+++ b/solution.py
@@ -18,7 +18,7 @@
 CROSS = ((1, 2), (2, 1))
 BF16 = jnp.bfloat16
 F32 = jnp.float32
-VMEM = 56 * 1024 * 1024
+VMEM = 32 * 1024 * 1024
 COST = pl.CostEstimate(flops=1, bytes_accessed=1, transcendentals=0)
 
 NT = (((1,), (1,)), ((), ()))
@@ -174,9 +174,14 @@
     )(x, dealt, cos, sin)
 
 
-def forward_kernel(heads, q_ref, k_ref, vt_ref, pq_ref, dq_ref, pk_ref, dk_ref, out_ref, lse_ref):
+def visible_to(marks_all, marks):
+    marks = marks.T
+    return (marks_all[:, :1] <= marks[:1, :]) & (marks_all[:, 1:2] == marks[1:2, :])
+
+
+def forward_kernel(heads, q_ref, k_ref, vt_ref, marks_ref, marks_all_ref, out_ref, lse_ref):
     q = q_ref[...]
-    visible = (pk_ref[...] <= pq_ref[...]) & (dk_ref[...] == dq_ref[...])
+    visible = visible_to(marks_all_ref[...], marks_ref[...])
     lane = lax.broadcasted_iota(jnp.int32, q.shape, 1) // HEAD_WIDTH
     wide = (q.shape[1], q.shape[0])
     row = lax.broadcasted_iota(jnp.int32, wide, 0) // HEAD_WIDTH
@@ -198,18 +203,16 @@
     return 256 if rows <= 1024 else 128
 
 
-def attend_forward(heads, q, k, vt, positions, docs):
+def attend_forward(heads, q, k, vt, marks):
     rows, width = q.shape
     block = query_block(rows)
     row = pl.BlockSpec((block, width), lambda i: (i, 0))
-    across = pl.BlockSpec((1, block), lambda i: (0, i))
+    mark = pl.BlockSpec((block, 128), lambda i: (i, 0))
     whole = lambda a: pl.BlockSpec(a.shape, lambda i: (0, 0))
-    down = (positions[:, None], docs[:, None])
-    flat = (positions[None], docs[None])
     return pl.pallas_call(
         functools.partial(forward_kernel, heads),
         grid=(rows // block,),
-        in_specs=[row, whole(k), whole(vt), across, across, whole(down[0]), whole(down[1])],
+        in_specs=[row, whole(k), whole(vt), mark, whole(marks)],
         out_specs=[row, pl.BlockSpec((8, block), lambda i: (0, i))],
         out_shape=[
             jax.ShapeDtypeStruct((rows, width), BF16),
@@ -218,11 +221,11 @@
         compiler_params=pltpu.CompilerParams(vmem_limit_bytes=VMEM),
         cost_estimate=COST,
         name="attend_forward",
-    )(q, k, vt, *flat, *down)
+    )(q, k, vt, marks, marks)
 
 
 def backward_kernel(
-    heads, q_ref, g_ref, k_ref, v_ref, kt_ref, pq_ref, dq_ref, pk_ref, dk_ref, lse_ref,
+    heads, q_ref, g_ref, k_ref, v_ref, kt_ref, marks_ref, marks_all_ref, lse_ref,
     cos_ref, sin_ref, cos_all_ref, sin_all_ref, gq_ref, gkv_ref, gk_sum, gv_sum,
 ):
     step = pl.program_id(0)
@@ -234,7 +237,7 @@
 
     q = q_ref[...]
     g = g_ref[...]
-    visible = (pk_ref[...] <= pq_ref[...]) & (dk_ref[...] == dq_ref[...])
+    visible = visible_to(marks_all_ref[...], marks_ref[...])
     lane = lax.broadcasted_iota(jnp.int32, q.shape, 1) // HEAD_WIDTH
     wide = (q.shape[1], q.shape[0])
     row = lax.broadcasted_iota(jnp.int32, wide, 0) // HEAD_WIDTH
@@ -269,20 +272,18 @@
         gkv_ref[...] = jnp.where(lane < HEAD_WIDTH, gk, gv).astype(BF16)
 
 
-def attend_backward(heads, q, g, k, v, kt, positions, docs, lse, cos, sin):
+def attend_backward(heads, q, g, k, v, kt, marks, lse, cos, sin):
     rows, width = q.shape
     block = query_block(rows)
     row = lambda n: pl.BlockSpec((block, n), lambda i: (i, 0))
     across = lambda n: pl.BlockSpec((n, block), lambda i: (0, i))
     whole = lambda a: pl.BlockSpec(a.shape, lambda i: (0, 0))
-    down = (positions[:, None], docs[:, None])
-    flat = (positions[None], docs[None])
     return pl.pallas_call(
         functools.partial(backward_kernel, heads),
         grid=(rows // block,),
         in_specs=[
-            row(width), row(width), whole(k), whole(v), whole(kt), across(1), across(1),
-            whole(down[0]), whole(down[1]), across(8), row(128), row(128), whole(cos), whole(sin),
+            row(width), row(width), whole(k), whole(v), whole(kt), row(128), whole(marks),
+            across(8), row(128), row(128), whole(cos), whole(sin),
         ],
         out_specs=[row(width), pl.BlockSpec((rows, 128), lambda i: (0, 0))],
         out_shape=[
@@ -293,7 +294,7 @@
         compiler_params=pltpu.CompilerParams(vmem_limit_bytes=VMEM),
         cost_estimate=COST,
         name="attend_backward",
-    )(q, g, k, v, kt, *flat, *down, lse, cos, sin, cos, sin)
+    )(q, g, k, v, kt, marks, marks, lse, cos, sin, cos, sin)
 
 
 def feed_kernel(bits_ref, n_ref, g_ref, down_ref, *refs):
@@ -501,7 +502,7 @@
 
 
 def sum_kernel(count, *refs):
-    outs = refs[3 * count + 1 :]
+    outs = refs[-count:]
     for at in range(count):
         own, near, relayed = refs[3 * at : 3 * at + 3]
         total = own[...].astype(F32) + near[...].astype(F32) + relayed[...].astype(F32)
@@ -512,19 +513,21 @@
     vmem = pl.BlockSpec(memory_space=pltpu.VMEM)
     return pl.pallas_call(
         functools.partial(sum_kernel, len(groups)),
-        in_specs=[vmem] * (3 * len(groups)) + [pl.BlockSpec(memory_space=pl.ANY)],
+        in_specs=[vmem] * (3 * len(groups)) + [pl.BlockSpec(memory_space=pl.ANY)] * len(after),
         out_shape=[jax.ShapeDtypeStruct(group[0].shape, dtype) for group in groups],
         compiler_params=pltpu.CompilerParams(vmem_limit_bytes=VMEM),
         cost_estimate=COST,
         name="sum_parts",
-    )(*[part for group in groups for part in group], after)
-
-
-def rope_tables(positions):
+    )(*[part for group in groups for part in group], *after)
+
+
+def row_tables(positions, docs):
     inverse = 10000.0 ** (-jnp.arange(0, HEAD_WIDTH, 2).astype(F32) / HEAD_WIDTH)
     angles = positions.astype(F32)[:, None] * inverse[None, :]
     cos, sin = jnp.cos(angles), jnp.sin(angles)
-    return jnp.concatenate([cos] * 4, 1), jnp.concatenate([-sin, sin] * 2, 1)
+    marks = jnp.stack([positions, docs], axis=1).astype(F32)
+    marks = jnp.pad(marks, ((0, 0), (0, 126)))
+    return jnp.concatenate([cos] * 4, 1), jnp.concatenate([-sin, sin] * 2, 1), marks
 
 
 def norm_back(upstream, values, gain):
@@ -678,10 +681,10 @@
     raw_far, raw_near = layout.start_four(raw, "raw")
     x = layout.in_order(blocks)
     x_team = layout.team_gather(x)
-    cos, sin = rope_tables(positions)
+    cos, sin, marks = row_tables(positions, docs)
     dealt = deal(places, w_gate, w_up)
-    raw_far, raw_near, w_out, down_sent, cotangent, cos, sin, positions, docs, dealt = tie(
-        (raw_far, raw_near, w_out, w_down, cotangent, cos, sin, positions, docs, dealt)
+    raw_far, raw_near, w_out, cotangent, cos, sin, marks, dealt = tie(
+        (raw_far, raw_near, w_out, cotangent, cos, sin, marks, dealt)
     )
     raw_corner = layout.corner_four(raw_far, "raw")
     out_part = layout.cross(w_out)
@@ -689,10 +692,10 @@
     dealt_attn = deal_attn(
         bits, order, kv_of, query_width, query_width + padding, (raw, raw_far, raw_near, raw_corner)
     )
-    dealt_attn, out_part, down_sent, *g_blocks = tie((dealt_attn, out_part, down_sent, *g_blocks))
+    dealt_attn, out_part, w_down, *g_blocks = tie((dealt_attn, out_part, w_down, *g_blocks))
     dealt_attn = layout.exchange(dealt_attn)
+    down_own = lax.all_gather(w_down, (layout.high, layout.low), axis=0, tiled=True)
     out_far, out_near = layout.start_four(out_part, "out")
-    down_far, down_near = layout.start_four(down_sent, "down")
     g_rows = layout.in_order(g_blocks)
     g = layout.team_gather(g_rows)
     dealt_attn, out_far, out_near, dealt = tie((dealt_attn, out_far, out_near, dealt))
@@ -701,10 +704,8 @@
 
     normed_attn, q, k, v, kt, vt, gains, w_attn = project(places, x_team, dealt_attn, cos, sin)
     gain_attn, gain_mlp = gains[:1], gains[1:2]
-    q, out_corner, down_far, down_near = tie((q, out_corner, down_far, down_near))
-    down_corner = layout.corner_four(down_far, "down")
-    attended, lse = attend_forward(heads, q, k, vt, positions, docs)
-    attended, dealt, down_corner = tie((attended, dealt, down_corner))
+    attended, lse = attend_forward(heads, q, k, vt, marks)
+    attended, out_corner, dealt = tie((attended, out_corner, dealt))
     dealt = dealt.reshape(places, 2 * weight_rows, -1)
     chunk = lambda a, at: a[at * places // 2 : (at + 1) * places // 2]
     gu_parts = [chunk(dealt, 0), chunk(dealt, 1)]
@@ -712,9 +713,6 @@
     gu_far[0], gu_near[0] = layout.start_four(gu_parts[0], "gate_up_0")
     out_own = layout.join_four(layout.low, layout.high, out_part, out_near, out_far, out_corner)
     out_own = out_own.reshape(query_width, width)
-    down_own = layout.join_four(
-        layout.high, layout.low, w_down, down_far, down_near, down_corner
-    ).reshape(-1, width)
     attended = attended[:, :query_width]
 
     half = x_team.shape[0] // 2
@@ -730,9 +728,8 @@
         gu_far[1], gu_near[1] = layout.start_four(gu_parts[1], "gate_up_1")
         return parts
 
-    branch = layout.scatter_rows(
-        lambda core: dot(part(attended, core), out_own), (None, same, weights_on)
-    )
+    branch = layout.scatter_rows(lambda core: dot(part(attended, core), out_own))
+    (branch,) = weights_on((branch,))
     x_wide = x.astype(F32)
     middle = x_wide + branch
     scale_mlp = lax.rsqrt(jnp.mean(middle * middle, axis=-1, keepdims=True) + EPSILON)
@@ -752,21 +749,16 @@
     )
     w_gu = w_gu.reshape(width, -1)
 
-    down_parts = outer_quarters(False, bits, activated, g)
-    grad_gu, activated, down_parts = tie((grad_gu, activated, down_parts))
-    down_far = swap(down_parts[3], layout.low, "grad_down_far")
-
     def gu_terms(parts):
         *parts, right = tie((*parts, grad_gu))
         late["theirs"], late["far"] = outer_rows((1,), 2, places, bits, normed_mlp, right)
         return parts
 
     def gu_others(parts):
-        *parts, late["far"], late["theirs"], right, late["down_far"] = tie(
-            (*parts, late["far"], late["theirs"], grad_gu, down_far)
+        *parts, late["far"], late["theirs"], right = tie(
+            (*parts, late["far"], late["theirs"], grad_gu)
         )
         late["far"][0] = swap(late["far"][0], layout.low, "grad_gate_up_far_0")
-        late["down_relay"] = layout.relay_sum(down_parts[2], late["down_far"], "grad_down")
         late["own"], late["near"] = outer_rows((0,), 2, places, bits, normed_mlp, right)
         return parts
 
@@ -774,29 +766,32 @@
         lambda core: dot(part(grad_gu, core), w_gu, NT), (None, gu_terms, gu_others)
     )
     gu_theirs, gu_far, gu_own, gu_near = (late[key] for key in ("theirs", "far", "own", "near"))
-    down_relay = late["down_relay"]
-    grad_normed_mlp, gu_own, gu_near = tie((grad_normed_mlp, gu_own, gu_near))
+    grad_normed_mlp, gu_own, gu_near, gu_far[0] = tie((grad_normed_mlp, gu_own, gu_near, gu_far[0]))
     grad_middle = g_rows.astype(F32) + norm_back(grad_normed_mlp, middle, gain_mlp)
     grad_branch = grad_middle.astype(BF16)
     branch_team = layout.team_gather(grad_branch)
     gu_far[0], act, grad_branch, sent = tie((gu_far[0], activated, grad_branch, gu_far[1]))
+    gu_relay = [layout.relay_sum(gu_theirs[0], gu_far[0], "grad_gate_up_0")]
     gu_far[1] = swap(sent, layout.low, "grad_gate_up_far_1")
-    gu_relay = [layout.relay_sum(gu_theirs[0], gu_far[0], "grad_gate_up_0")]
+    grad_down = dot(act, g, TN).astype(BF16)
+    act, grad_down = tie((act, grad_down))
     final = layout.scatter_cores(lambda core: dot(part(act, core), down_own))
-    branch_team, gu_far[1], down_sent, near_sent, *final = tie(
-        (branch_team, gu_far[1], down_parts[1], gu_near[0], *final)
+    branch_team, grad_down, gu_far[1], gu_relay[0], gu_near, *final = tie(
+        (branch_team, grad_down, gu_far[1], gu_relay[0], gu_near, *final)
     )
     gu_relay.append(layout.relay_sum(gu_theirs[1], gu_far[1], "grad_gate_up_1"))
-    down_near = swap(down_sent, layout.low, "grad_down_near")
+    gu_near = [swap(near, layout.low, f"grad_gate_up_near_{at}") for at, near in enumerate(gu_near)]
+    grad_down = lax.psum_scatter(
+        grad_down, (layout.high, layout.low), scatter_dimension=0, tiled=True
+    ).astype(F32)
     final = layout.scatter_send(final, 0)
     grad_attended = dot(branch_team, out_own, NT).astype(BF16)
     if padding:
         grad_attended = jnp.pad(grad_attended, ((0, 0), (0, padding)))
 
-    gq, gkv = attend_backward(heads, q, grad_attended, k, v, kt, positions, docs, lse, cos, sin)
+    gq, gkv = attend_backward(heads, q, grad_attended, k, v, kt, marks, lse, cos, sin)
     grad_qkv = jnp.concatenate([gq, gkv], axis=1)
-    grad_qkv, final, down_near, near_sent = tie((grad_qkv, final, down_near, near_sent))
-    gu_near[0] = swap(near_sent, layout.low, "grad_gate_up_near_0")
+    grad_qkv, final, gu_near, gu_relay[1] = tie((grad_qkv, final, gu_near, gu_relay[1]))
     for count in range(1, len(layout.mid)):
         final = layout.scatter_send(layout.scatter_add(final), count)
 
@@ -814,39 +809,39 @@
         late["out"] = outer_quarters(True, bits, attended, right)
         return parts
 
-    def relays_on(parts):
-        *parts, late["attn_far"], late["out"], gu_near[0], sent, gu_relay[0] = tie(
-            (*parts, late["attn_far"], late["out"], gu_near[0], gu_near[1], gu_relay[0])
+    def sums_on(parts):
+        *parts, late["attn_far"], late["out"], total, own, near, relayed = tie(
+            (*parts, late["attn_far"], late["out"], late["final"], gu_own, gu_near, gu_relay)
         )
-        gu_near[1] = swap(sent, layout.low, "grad_gate_up_near_1")
+        late["total"] = (middle + layout.scatter_add(total)).astype(BF16)
+        late["attn_relay"] = layout.relay_sum(late["attn"][0], late["attn_far"], "grad_attn")
         late["out_far"] = swap(late["out"][3], layout.low, "grad_out_far")
+        late["gate_up"] = sum_parts(BF16, (parts[0],), *zip(own, near, relayed))
         return parts
 
     grad_normed_attn = layout.scatter_rows(
-        lambda core: dot(part(grad_qkv, core), w_attn_own, NT), (attn_terms, out_terms, relays_on)
+        lambda core: dot(part(grad_qkv, core), w_attn_own, NT), (attn_terms, out_terms, sums_on)
     )
     attn_parts, out_parts = late["attn"], late["out"]
-    grad_normed_attn, final, out_far, attn_far, attn_sent = tie(
-        (grad_normed_attn, late["final"], late["out_far"], late["attn_far"], attn_parts[3])
-    )
-    attn_relay = layout.relay_sum(attn_parts[0], attn_far, "grad_attn")
+    grad_normed_attn, out_far, attn_sent, gu_sums = tie(
+        (grad_normed_attn, late["out_far"], attn_parts[3], late["gate_up"])
+    )
+    grad_normed_attn, grad_down = tie((grad_normed_attn, grad_down))
+    attn_relay = late["attn_relay"]
     attn_near = swap(attn_sent, layout.low, "grad_attn_near")
-    final = layout.scatter_add(final)
-    block_out = layout.from_team((middle + final).astype(BF16), "block_out")
     out_relay = layout.relay_sum(out_parts[2], out_far, "grad_out")
     out_near = swap(out_parts[1], layout.low, "grad_out_near")
     grad_input = grad_middle + norm_back(grad_normed_attn, x_wide, gain_attn)
-    grad_rows = grad_input.astype(BF16)
-    grad_input = layout.from_team(grad_rows, "grad_input").astype(F32)
+    grad_rows, attn_relay = tie((grad_input.astype(BF16), attn_relay))
+    home = layout.from_team(jnp.concatenate([late["total"], grad_rows], axis=1), "rows_home")
+    block_out, grad_input = home[..., :width], home[..., width:].astype(F32)
 
     by_member = lambda a: a.reshape(members, weight_rows, -1)
-    dealt = sum_parts(BF16, grad_rows, *zip(gu_own, gu_near, gu_relay))
-    dealt = layout.exchange(by_member(jnp.concatenate(dealt)))
-    (grad_attn,) = sum_parts(BF16, grad_rows, (attn_parts[2], attn_near, attn_relay))
+    dealt = layout.exchange(by_member(jnp.concatenate(gu_sums)))
+    (grad_attn,) = sum_parts(BF16, (grad_rows, dealt), (attn_parts[2], attn_near, attn_relay))
     grad_attn = layout.rows_in(layout.exchange(by_member(grad_attn))).astype(F32)
-    (grad_out,) = sum_parts(BF16, grad_rows, (out_parts[0], out_near, out_relay))
+    (grad_out,) = sum_parts(BF16, (grad_rows,), (out_parts[0], out_near, out_relay))
     grad_out = layout.cross(grad_out).astype(F32)
-    (grad_down,) = sum_parts(F32, grad_rows, (down_parts[0], down_near, down_relay))
     grad_gate, grad_up = collect(places, dealt)
 
     def sum_kv(array):

time: 634 us -> 571 us (0.901)
  Pallas kernels: 122 us -> 78.3 us
  waiting for transfers between devices: 286 us -> 252 us
  local copies, waits for them, and re-layouts: 27.4 us -> 47.4 us
  starting transfers between devices: 107 us -> 98.2 us
  matrix products: 28.1 us -> 35.2 us
    ppermute x50 -> x44, waiting for transfers between devices: 266 us -> 218 us  [swap(): return lax.ppermute(array, axis, SWAP)]
    unnamed x133 -> x225, local copies, waits for them, and re-layouts: 4.93 us -> 32.1 us
    pallas_call x2 -> x1, Pallas kernels: 13.7 us -> 3.81 us  [outer_quarters(): pl.pallas_call(functools.partial(quarters_kernel, flip), grid_spec=pltpu....]
    pallas_call x3, Pallas kernels: 23.7 us -> 14.7 us  [outer_rows(): pl.pallas_call(functools.partial(rows_kernel, sides, chunks), grid_spec=p...]
    ppermute x50 -> x44, starting transfers between devices: 60.3 us -> 51.4 us  [swap(): return lax.ppermute(array, axis, SWAP)]
    reduce_scatter x0 -> x1, waiting for transfers between devices: none -> 8.77 us  [shards(): lax.psum_scatter(grad_down, (layout.high, layout.low), scatter_dimension=...]
    pallas_call x4 -> x3, Pallas kernels: 10.5 us -> 2.71 us  [sum_parts(): pl.pallas_call(functools.partial(sum_kernel, len(groups)), in_specs=[vmem...]
    dot_general x9 -> x10, matrix products: 28.1 us -> 35.2 us  [dot(): return lax.dot_general(left, right, dims, preferred_element_type=F32)]
  transfers between devices with their start and end apart: 69 -> 63, of which waited for: 35 -> 32; matrix products, arithmetic and copies ran while one was open for 12% -> 12% of each run, Pallas kernels for 15% -> 11%
where the time goes in v2:
time: 571 us; the launch traced here: 565 us
  waiting for transfers between devices  252 us (44%)
  starting transfers between devices  98.2 us (17%)
  Pallas kernels  78.3 us (14%)
  local copies, waits for them, and re-layouts  47.4 us (8%)
  other arithmetic  37.2 us (7%)
  matrix products  35.2 us (6%)
  between operations  16 us (3%)
    ppermute x44, waiting for transfers between devices, swap(): return lax.ppermute(array, axis, SWAP)  218 us
    ppermute x44, starting transfers between devices, swap(): return lax.ppermute(array, axis, SWAP)  51.4 us
    dot_general x10, matrix products, dot(): return lax.dot_general(left, right, dims, preferred_element_type=F32)  35.2 us
    unnamed x225, local copies, waits for them, and re-layouts  32.1 us
    all_to_all x4, starting transfers between devices, exchange(): return lax.all_to_all(array, self.mid + ('core',), 0, 0, tiled=True)  31.2 us
    pallas_call x1, Pallas kernels, attend_backward(): pl.pallas_call(functools.partial(backward_kernel, heads), grid=(rows // b...  18.7 us
    pallas_call x1, Pallas kernels, feed_forward(): pl.pallas_call(feed_kernel, grid=(rows // block,), in_specs=[pl.BlockSpec...  16.6 us
    pallas_call x3, Pallas kernels, outer_rows(): pl.pallas_call(functools.partial(rows_kernel, sides, chunks), grid_spec=p...  14.7 us
  transfers between devices with their start and end apart: 63, of which 32 were waited for; matrix products, arithmetic and copies ran while one was open for 12% of the time, Pallas kernels for 11%

profile of v2, /device:TPU:0, one launch (start us, length us, event | category | flops | bytes accessed | tf_op | source)
XLA Modules:
  0.0 564.6 jit_solution(16050800299917959775)
XLA Ops:
  9.1 3.0 collective-permute-start.1
  12.1 4.3 collective-permute-done.1
  19.8 9.7 %collective-permute-start.2 = (bf16[64,2688]{1,0:T(8,128)(2,1)S(1)}, bf16[64,2688]{1,0:T(8,128)(2,1)S(1)}, u32[]{:S(2)}, u32[]{:S(2)}) collective-permute-start(bf16[64,2688]{1,0:T(8,128)(2,1)S(1)} %fusion.21.own), channel_id=1, source_target_pairs={{0,16},{16,0},{1,17},{17,1},{2,18},{18,2},{3,19},{19,3},{4,20},{20... | collective-permute-start | bytes 1032200 | tf_op jit(solution)/shard_map/raw_far/ppermute | solution.py:43
  35.1 8.7 %collective-permute-done.2.far = bf16[64,2688]{1,0:T(8,128)(2,1)S(1)} collective-permute-done((bf16[64,2688]{1,0:T(8,128)(2,1)S(1)}, bf16[64,2688]{1,0:T(8,128)(2,1)S(1)}, u32[]{:S(2)}, u32[]{:S(2)}) %collective-permute-start.2) | collective-permute-done | bytes 344096 | tf_op jit(solution)/shard_map/raw_far/ppermute | solution.py:43
  50.1 3.1 collective-permute-done.5.corner
  55.4 5.7 %collective-permute-done.8 = bf16[64,2048]{1,0:T(8,128)(2,1)S(1)} collective-permute-done((bf16[64,2048]{1,0:T(8,128)(2,1)S(1)}, bf16[64,2048]{1,0:T(8,128)(2,1)S(1)}, u32[]{:S(2)}, u32[]{:S(2)}) %collective-permute-start.8) | collective-permute-done | bytes 262176 | tf_op jit(solution)/shard_map/cotangent/ppermute | solution.py:564
  61.8 11.1 %all-to-all-start = ((bf16[8,272,384]{2,1,0:T(8,128)(2,1)}), bf16[8,272,384]{2,1,0:T(8,128)(2,1)S(1)}, u32[]{:S(2)}, u32[]{:S(2)}) async-start(bf16[8,272,384]{2,1,0:T(8,128)(2,1)} %copy-done.4), calls=%async_computation | async-start | bytes 3342336 | tf_op jit(solution)/shard_map/all_to_all | solution.py:620
  76.2 6.3 %collective-permute-done.10 = bf16[64,2048]{1,0:T(8,128)(2,1)S(1)} collective-permute-done((bf16[64,2048]{1,0:T(8,128)(2,1)S(1)}, bf16[64,2048]{1,0:T(8,128)(2,1)S(1)}, u32[]{:S(2)}, u32[]{:S(2)}) %collective-permute-start.10) | collective-permute-done | bytes 262176 | tf_op jit(solution)/shard_map/out_near/ppermute | solution.py:43
  83.2 22.2 %collective-permute-done.9 = bf16[64,2048]{1,0:T(8,128)(2,1)} collective-permute-done((bf16[64,2048]{1,0:T(8,128)(2,1)S(1)}, bf16[64,2048]{1,0:T(8,128)(2,1)}, u32[]{:S(2)}, u32[]{:S(2)}) %collective-permute-start.9) | collective-permute-done | bytes 262176 | tf_op jit(solution)/shard_map/out_far/ppermute | solution.py:43
  106.9 4.3 all-to-all-start.1
  118.5 5.4 project.1
  127.2 12.2 %attend_forward.1 = (bf16[1024,256]{1,0:T(8,128)(2,1)S(1)}, f32[8,1024]{1,0:T(8,128)S(1)}) custom-call(bf16[1024,256]{1,0:T(8,128)(2,1)S(1)} %get-tuple-element.154.q_ref, bf16[1024,256]{1,0:T(8,128)(2,1)S(1)} %get-tuple-element.155.k_ref, bf16[256,1024]{1,0:T(8,128)(2,1)S(1)} %get-tuple-element.156.vt_ref, f32[1024,128]{1,0:T(8,128)S(1)} %pad.9.marks_ref.marks_all_ref, ...), custom_call_target="tpu_custom_call" | custom-call | flops 1 | bytes 1 | tf_op jit(solution)/shard_map/attend_forward/pallas_call | solution.py:212
  140.2 4.5 all-to-all-done.1
  148.1 4.5 collective-permute-done.12
  160.7 14.8 %collective-permute-done.15 = bf16[2,128,1024]{2,1,0:T(8,128)(2,1)S(1)} collective-permute-done((bf16[2,128,1024]{2,1,0:T(8,128)(2,1)S(1)}, bf16[2,128,1024]{2,1,0:T(8,128)(2,1)S(1)}, u32[]{:S(2)}, u32[]{:S(2)}) %collective-permute-start.15) | collective-permute-done | bytes 524320 | tf_op jit(solution)/shard_map/sum_places_0/ppermute | solution.py:43
  175.8 5.3 collective-permute-start.16
  181.1 17.1 %collective-permute-done.13 = bf16[2,128,1024]{2,1,0:T(8,128)(2,1)S(1)} collective-permute-done((bf16[2,128,1024]{2,1,0:T(8,128)(2,1)S(1)}, bf16[2,128,1024]{2,1,0:T(8,128)(2,1)S(1)}, u32[]{:S(2)}, u32[]{:S(2)}) %collective-permute-start.13) | collective-permute-done | bytes 524320 | tf_op jit(solution)/shard_map/sum_places_0/ppermute | solution.py:43
  198.7 9.1 %collective-permute-done.16 = bf16[128,1024]{1,0:T(8,128)(2,1)S(1)} collective-permute-done((bf16[128,1024]{1,0:T(8,128)(2,1)S(1)}, bf16[128,1024]{1,0:T(8,128)(2,1)S(1)}, u32[]{:S(2)}, u32[]{:S(2)}) %collective-permute-start.16) | collective-permute-done | bytes 262176 | tf_op jit(solution)/shard_map/sum_places_1/ppermute | solution.py:43
  216.3 29.9 %collective-permute-done.20.refs_5_ = bf16[2,128,1408]{2,1,0:T(8,128)(2,1)} collective-permute-done((bf16[2,128,1408]{2,1,0:T(8,128)(2,1)S(1)}, bf16[2,128,1408]{2,1,0:T(8,128)(2,1)}, u32[]{:S(2)}, u32[]{:S(2)}) %collective-permute-start.20) | collective-permute-done | bytes 720928 | tf_op jit(solution)/shard_map/gate_up_1_far/ppermute | solution.py:43
  247.3 17.1 %collective-permute-done.22.refs_7_ = bf16[2,128,1408]{2,1,0:T(8,128)(2,1)} collective-permute-done((bf16[2,128,1408]{2,1,0:T(8,128)(2,1)}, bf16[2,128,1408]{2,1,0:T(8,128)(2,1)}, u32[]{:S(2)}, u32[]{:S(2)}) %collective-permute-start.22) | collective-permute-done | bytes 720928 | tf_op jit(solution)/shard_map/gate_up_1_corner/ppermute | solution.py:43
  272.9 16.6 %feed_forward.1 = (bf16[1024,704]{1,0:T(8,128)(2,1)S(1)}, bf16[1024,1408]{1,0:T(8,128)(2,1)S(1)}, bf16[2,4,2,128,1408]{4,3,2,1,0:T(8,128)(2,1)}) custom-call(s32[3]{0:T(128)S(1)} %pad_add_fusion.bits_ref, bf16[1024,2048]{1,0:T(8,128)(2,1)S(1)} %copy-done.2, bf16[1024,2048]{1,0:T(8,128)(2,1)S(1)} %copy-done.8, bf16[704,2048]{1,0:T(8,128)(2,1)S(1)} %copy-done.14, ...), custom_call_target="tpu_custom_call" | custom-call | flops 1 | bytes 1 | tf_op jit(solution)/shard_map/feed_forward/pallas_call | solution.py:338
  289.5 6.9 %convolution_convert_fusion.4 = bf16[512,2048]{1,0:T(8,128)(2,1)S(1)} fusion(bf16[2048,1408]{1,0:T(8,128)(2,1)} %bitcast.214, bf16[1024,1408]{1,0:T(8,128)(2,1)S(1)} %get-tuple-element.184.right_ref, s32[]{:T(128)S(6)} %select_n.182), kind=kOutput, calls=%fused_computation.8 | convolution fusion | flops 2953838592 | bytes 9306116 | tf_op jit(solution)/shard_map/dot_general | solution.py:30
  296.5 4.1 collective-permute-done.23
  300.7 3.7 add_convert_fusion.2
  306.7 4.6 outer_rows.3
  311.4 7.3 %collective-permute-done.25 = bf16[2,128,1024]{2,1,0:T(8,128)(2,1)S(1)} collective-permute-done((bf16[2,128,1024]{2,1,0:T(8,128)(2,1)S(1)}, bf16[2,128,1024]{2,1,0:T(8,128)(2,1)S(1)}, u32[]{:S(2)}, u32[]{:S(2)}) %collective-permute-start.25) | collective-permute-done | bytes 524320 | tf_op jit(solution)/shard_map/sum_places_0/ppermute | solution.py:43
  321.5 5.7 %outer_rows.4 = (bf16[2,128,1408]{2,1,0:T(8,128)(2,1)S(1)}, bf16[2,128,1408]{2,1,0:T(8,128)(2,1)S(1)}, bf16[2,128,1408]{2,1,0:T(8,128)(2,1)}, bf16[2,128,1408]{2,1,0:T(8,128)(2,1)}) custom-call(s32[3]{0:T(128)S(1)} %pad_add_fusion.bits_ref, bf16[1024,2048]{1,0:T(8,128)(2,1)S(1)} %copy-done.3, bf16[1024,1408]{1,0:T(8,128)(2,1)S(1)} %get-tuple-element.184.right_ref), custom_call_target="tpu_custom_call" | custom-call | flops 1 | bytes 1 | tf_op jit(solution)/shard_map/outer_rows/pallas_call | solution.py:388
  328.3 9.7 %collective-permute-done.28 = bf16[2,128,1408]{2,1,0:T(8,128)(2,1)S(1)} collective-permute-done((bf16[2,128,1408]{2,1,0:T(8,128)(2,1)S(1)}, bf16[2,128,1408]{2,1,0:T(8,128)(2,1)S(1)}, u32[]{:S(2)}, u32[]{:S(2)}) %collective-permute-start.28) | collective-permute-done | bytes 720928 | tf_op jit(solution)/shard_map/grad_gate_up_far_0/ppermute | solution.py:43
  340.2 7.4 %convolution_convert_fusion = bf16[704,2048]{1,0:T(8,128)(2,1)} fusion(bf16[1024,704]{1,0:T(8,128)(2,1)} %copy-done.51, bf16[1024,2048]{1,0:T(8,128)(2,1)} %all-gather.10.cloned.1.call-done.g_ref), kind=kOutput, calls=%fused_computation.4 | convolution fusion | flops 2954231808 | bytes 8519680 | tf_op jit(solution)/shard_map/dot_general | solution.py:30
  347.6 4.0 convolution_convert_fusion.3
  359.6 27.3 %collective-permute-done.30.refs_2_ = bf16[2,128,1408]{2,1,0:T(8,128)(2,1)S(1)} collective-permute-done((bf16[2,128,1408]{2,1,0:T(8,128)(2,1)S(1)}, bf16[2,128,1408]{2,1,0:T(8,128)(2,1)S(1)}, u32[]{:S(2)}, u32[]{:S(2)}) %collective-permute-start.30) | collective-permute-done | bytes 720928 | tf_op jit(solution)/shard_map/grad_gate_up_0_relay/ppermute | solution.py:43
  396.8 18.7 %attend_backward.1 = (bf16[1024,256]{1,0:T(8,128)(2,1)S(1)}, bf16[1024,128]{1,0:T(8,128)(2,1)S(1)}) custom-call(bf16[1024,256]{1,0:T(8,128)(2,1)S(1)} %copy-done.23, bf16[1024,256]{1,0:T(8,128)(2,1)S(1)} %convolution_convert_fusion.5.g_ref, bf16[1024,256]{1,0:T(8,128)(2,1)S(1)} %copy-done.25, bf16[1024,256]{1,0:T(8,128)(2,1)S(1)} %copy-done.44, ...), custom_call_target="tpu_custom_call" | custom-call | flops 1 | bytes 1 | tf_op jit(solution)/shard_map/attend_backward/pallas_call | solution.py:281
  417.2 4.0 collective-permute-done.35.refs_4_
  423.1 2.6 convolution_convert_fusion.2
  430.9 4.4 outer_rows.5
  435.3 3.2 add_convert_fusion
  438.9 5.4 collective-permute-done.39
  450.9 3.8 outer_quarters.1
  454.7 3.6 collective-permute-done.41
  459.6 9.9 %collective-permute-done.40 = bf16[2,128,1024]{2,1,0:T(8,128)(2,1)} collective-permute-done((bf16[2,128,1024]{2,1,0:T(8,128)(2,1)}, bf16[2,128,1024]{2,1,0:T(8,128)(2,1)}, u32[]{:S(2)}, u32[]{:S(2)}) %collective-permute-start.40) | collective-permute-done | bytes 524320 | tf_op jit(solution)/shard_map/sum_places_0/ppermute | solution.py:43
  475.3 2.9 collective-permute-start.46
  480.6 4.0 collective-permute-done.44
  488.1 3.8 all-to-all-start.2
  495.6 8.8 %reduce-scatter.2.cloned.1.call-done = bf16[176,2048]{1,0:T(8,128)(2,1)} async-done(((bf16[704,2048]{1,0:T(8,128)(2,1)}), bf16[176,2048]{1,0:T(8,128)(2,1)}) %reduce-scatter.2.cloned.1.call-update) | async-done | bytes 720912 | tf_op jit(solution)/shard_map/reduce_scatter | solution.py:784
  509.6 4.7 collective-permute-done.51.refs_2_
  517.5 5.4 collective-permute-start.47
  523.7 5.9 %all-to-all-done.2.refs_4_.in_ref = bf16[8,64,1408]{2,1,0:T(8,128)(2,1)S(1)} async-done(((bf16[8,64,1408]{2,1,0:T(8,128)(2,1)}), bf16[8,64,1408]{2,1,0:T(8,128)(2,1)S(1)}, u32[]{:S(2)}, u32[]{:S(2)}) %all-to-all-start.2) | async-done | bytes 1441824 | tf_op jit(solution)/shard_map/all_to_all | solution.py:620
  532.5 11.9 %all-to-all-start.3 = ((bf16[8,64,384]{2,1,0:T(8,128)(2,1)}), bf16[8,64,384]{2,1,0:T(8,128)(2,1)S(1)}, u32[]{:S(2)}, u32[]{:S(2)}) async-start(bf16[8,64,384]{2,1,0:T(8,128)(2,1)} %bitcast.186), calls=%async_computation.4 | async-start | bytes 786432 | tf_op jit(solution)/shard_map/all_to_all | solution.py:620
  (441 shorter events, 149.9 us)
Async XLA Ops:
  7.3 109.0 %all-gather.6.cloned.1.call-start = ((), (), s32[]{:S(2)}) async-start(), calls=%async_computation.5 | async-start | bytes 4718592 | tf_op jit(solution)/shard_map/all_gather | solution.py:584
  17.7 17.4 %collective-permute-start.3 = (bf16[64,2688]{1,0:T(8,128)(2,1)S(1)}, bf16[64,2688]{1,0:T(8,128)(2,1)S(1)}, u32[]{:S(2)}, u32[]{:S(2)}) collective-permute-start(bf16[64,2688]{1,0:T(8,128)(2,1)S(1)} %fusion.21.own), channel_id=1, source_target_pairs={{0,2},{2,0},{1,3},{3,1},{4,6},{6,4},{5,7},{7,5},{8,10},{10,8},{9,1... | collective-permute-start | bytes 1032200 | tf_op jit(solution)/shard_map/raw_near/ppermute | solution.py:43
  19.8 24.0 %collective-permute-start.2 = (bf16[64,2688]{1,0:T(8,128)(2,1)S(1)}, bf16[64,2688]{1,0:T(8,128)(2,1)S(1)}, u32[]{:S(2)}, u32[]{:S(2)}) collective-permute-start(bf16[64,2688]{1,0:T(8,128)(2,1)S(1)} %fusion.21.own), channel_id=1, source_target_pairs={{0,16},{16,0},{1,17},{17,1},{2,18},{18,2},{3,19},{19,3},{4,20},{20... | collective-permute-start | bytes 1032200 | tf_op jit(solution)/shard_map/raw_far/ppermute | solution.py:43
  46.0 15.1 %collective-permute-start.8 = (bf16[64,2048]{1,0:T(8,128)(2,1)S(1)}, bf16[64,2048]{1,0:T(8,128)(2,1)S(1)}, u32[]{:S(2)}, u32[]{:S(2)}) collective-permute-start(bf16[64,2048]{1,0:T(8,128)(2,1)S(1)} %get-tuple-element.313), channel_id=1, source_target_pairs={{0,2},{1,18},{2,0},{3,16},{16,3},{17,19},{18,1},{19,17},{4,6},{5,2... | collective-permute-start | bytes 786440 | tf_op jit(solution)/shard_map/cotangent/ppermute | solution.py:564
  47.7 14.1 %collective-permute-start.7 = (bf16[64,2048]{1,0:T(8,128)(2,1)S(1)}, bf16[64,2048]{1,0:T(8,128)(2,1)}, u32[]{:S(2)}, u32[]{:S(2)}) collective-permute-start(bf16[64,2048]{1,0:T(8,128)(2,1)S(1)} %get-tuple-element.314), channel_id=1, source_target_pairs={{0,0},{1,16},{2,2},{3,18},{16,1},{17,17},{18,3},{19,19},{4,4},{5,2... | collective-permute-start | bytes 786440 | tf_op jit(solution)/shard_map/cotangent/ppermute | solution.py:564
  61.8 45.1 %all-to-all-start = ((bf16[8,272,384]{2,1,0:T(8,128)(2,1)}), bf16[8,272,384]{2,1,0:T(8,128)(2,1)S(1)}, u32[]{:S(2)}, u32[]{:S(2)}) async-start(bf16[8,272,384]{2,1,0:T(8,128)(2,1)} %copy-done.4), calls=%async_computation | async-start | bytes 3342336 | tf_op jit(solution)/shard_map/all_to_all | solution.py:620
  72.9 173.2 %all-gather.12.cloned.1.call-start = ((), (), s32[]{:S(2)}) async-start(), calls=%async_computation.8 | async-start | bytes 3604480 | tf_op jit(solution)/shard_map/all_gather | solution.py:697
  74.3 31.1 %collective-permute-start.9 = (bf16[64,2048]{1,0:T(8,128)(2,1)S(1)}, bf16[64,2048]{1,0:T(8,128)(2,1)}, u32[]{:S(2)}, u32[]{:S(2)}) collective-permute-start(bf16[64,2048]{1,0:T(8,128)(2,1)S(1)} %broadcast_select_fusion.2), channel_id=1, source_target_pairs={{0,16},{16,0},{1,17},{17,1},{2,18},{18,2},{3,19},{19,3},{4,20},{20... | collective-permute-start | bytes 786440 | tf_op jit(solution)/shard_map/out_far/ppermute | solution.py:43
  106.9 37.8 %all-to-all-start.1 = ((bf16[8,64,1408]{2,1,0:T(8,128)(2,1)}), bf16[8,64,1408]{2,1,0:T(8,128)(2,1)}, u32[]{:S(2)}, u32[]{:S(2)}) async-start(bf16[8,64,1408]{2,1,0:T(8,128)(2,1)} %copy-done.7), calls=%async_computation.1 | async-start | bytes 2883584 | tf_op jit(solution)/shard_map/all_to_all | solution.py:620
  111.2 135.0 %all-gather.10.cloned.1.call-start = ((), (), s32[]{:S(2)}) async-start(), calls=%async_computation.7 | async-start | bytes 4718592 | tf_op jit(solution)/shard_map/all_gather | solution.py:584
  113.2 151.3 %all-gather.8.cloned.1.call-start = ((), (), s32[]{:S(2)}) async-start(), calls=%async_computation.6 | async-start | bytes 4718592 | tf_op jit(solution)/shard_map/all_gather | solution.py:584
  113.5 26.7 %collective-permute-start.11 = (bf16[64,2048]{1,0:T(8,128)(2,1)}, bf16[64,2048]{1,0:T(8,128)(2,1)}, u32[]{:S(2)}, u32[]{:S(2)}) collective-permute-start(bf16[64,2048]{1,0:T(8,128)(2,1)} %collective-permute-done.9), channel_id=1, source_target_pairs={{0,2},{2,0},{1,3},{3,1},{4,6},{6,4},{5,7},{7,5},{8,10},{10,8},{9,1... | collective-permute-start | bytes 786440 | tf_op jit(solution)/shard_map/out_corner/ppermute | solution.py:43
  155.2 20.4 %collective-permute-start.15 = (bf16[2,128,1024]{2,1,0:T(8,128)(2,1)S(1)}, bf16[2,128,1024]{2,1,0:T(8,128)(2,1)S(1)}, u32[]{:S(2)}, u32[]{:S(2)}) collective-permute-start(bf16[2,128,1024]{2,1,0:T(8,128)(2,1)S(1)} %dynamic-slice_bitcast_fusion.10), channel_id=1, source_target_pairs={{0,4},{4,0},{1,5},{5,1},{2,6},{6,2},{3,7},{7,3},{8,12},{12,8},{9,1... | collective-permute-start | bytes 1572872 | tf_op jit(solution)/shard_map/sum_places_0/ppermute | solution.py:43
  156.8 41.4 %collective-permute-start.13 = (bf16[2,128,1024]{2,1,0:T(8,128)(2,1)S(1)}, bf16[2,128,1024]{2,1,0:T(8,128)(2,1)S(1)}, u32[]{:S(2)}, u32[]{:S(2)}) collective-permute-start(bf16[2,128,1024]{2,1,0:T(8,128)(2,1)S(1)} %dynamic-slice_bitcast_fusion.11), channel_id=1, source_target_pairs={{0,8},{8,0},{1,9},{9,1},{2,10},{10,2},{3,11},{11,3},{4,12},{12,4},... | collective-permute-start | bytes 1572872 | tf_op jit(solution)/shard_map/sum_places_0/ppermute | solution.py:43
  159.4 48.7 %collective-permute-start.18 = (bf16[2,128,1408]{2,1,0:T(8,128)(2,1)S(1)}, bf16[2,128,1408]{2,1,0:T(8,128)(2,1)S(1)}, u32[]{:S(2)}, u32[]{:S(2)}) collective-permute-start(bf16[2,128,1408]{2,1,0:T(8,128)(2,1)S(1)} %bitcast.183), channel_id=1, source_target_pairs={{0,2},{2,0},{1,3},{3,1},{4,6},{6,4},{5,7},{7,5},{8,10},{10,8},{9,1... | collective-permute-start | bytes 2162696 | tf_op jit(solution)/shard_map/gate_up_0_near/ppermute | solution.py:43
  160.0 49.1 %collective-permute-start.17 = (bf16[2,128,1408]{2,1,0:T(8,128)(2,1)S(1)}, bf16[2,128,1408]{2,1,0:T(8,128)(2,1)S(1)}, u32[]{:S(2)}, u32[]{:S(2)}) collective-permute-start(bf16[2,128,1408]{2,1,0:T(8,128)(2,1)S(1)} %bitcast.184), channel_id=1, source_target_pairs={{0,16},{16,0},{1,17},{17,1},{2,18},{18,2},{3,19},{19,3},{4,20},{20... | collective-permute-start | bytes 2162696 | tf_op jit(solution)/shard_map/gate_up_0_far/ppermute | solution.py:43
  175.8 32.0 %collective-permute-start.16 = (bf16[128,1024]{1,0:T(8,128)(2,1)S(1)}, bf16[128,1024]{1,0:T(8,128)(2,1)S(1)}, u32[]{:S(2)}, u32[]{:S(2)}) collective-permute-start(bf16[128,1024]{1,0:T(8,128)(2,1)S(1)} %dynamic-slice_bitcast_fusion.20), channel_id=1, source_target_pairs={{0,8},{8,0},{1,9},{9,1},{2,10},{10,2},{3,11},{11,3},{4,12},{12,4},... | collective-permute-start | bytes 786440 | tf_op jit(solution)/shard_map/sum_places_1/ppermute | solution.py:43
  211.2 176.6 %all-gather.14.cloned.1.call-start = ((), (), s32[]{:S(2)}) async-start(), calls=%async_computation.9 | async-start | bytes 4718592 | tf_op jit(solution)/shard_map/all_gather | solution.py:584
  211.8 34.4 %collective-permute-start.20 = (bf16[2,128,1408]{2,1,0:T(8,128)(2,1)S(1)}, bf16[2,128,1408]{2,1,0:T(8,128)(2,1)}, u32[]{:S(2)}, u32[]{:S(2)}) collective-permute-start(bf16[2,128,1408]{2,1,0:T(8,128)(2,1)S(1)} %bitcast.180), channel_id=1, source_target_pairs={{0,16},{16,0},{1,17},{17,1},{2,18},{18,2},{3,19},{19,3},{4,20},{20... | collective-permute-start | bytes 2162696 | tf_op jit(solution)/shard_map/gate_up_1_far/ppermute | solution.py:43
  214.2 33.1 %collective-permute-start.21 = (bf16[2,128,1408]{2,1,0:T(8,128)(2,1)S(1)}, bf16[2,128,1408]{2,1,0:T(8,128)(2,1)}, u32[]{:S(2)}, u32[]{:S(2)}) collective-permute-start(bf16[2,128,1408]{2,1,0:T(8,128)(2,1)S(1)} %bitcast.181), channel_id=1, source_target_pairs={{0,2},{2,0},{1,3},{3,1},{4,6},{6,4},{5,7},{7,5},{8,10},{10,8},{9,1... | collective-permute-start | bytes 2162696 | tf_op jit(solution)/shard_map/gate_up_1_near/ppermute | solution.py:43
  214.2 33.1 %collective-permute-start.19 = (bf16[2,128,1408]{2,1,0:T(8,128)(2,1)}, bf16[2,128,1408]{2,1,0:T(8,128)(2,1)}, u32[]{:S(2)}, u32[]{:S(2)}) collective-permute-start(bf16[2,128,1408]{2,1,0:T(8,128)(2,1)} %copy-done.29), channel_id=1, source_target_pairs={{0,2},{2,0},{1,3},{3,1},{4,6},{6,4},{5,7},{7,5},{8,10},{10,8},{9,1... | collective-permute-start | bytes 2162696 | tf_op jit(solution)/shard_map/gate_up_0_corner/ppermute | solution.py:43
  246.1 18.3 %collective-permute-start.22 = (bf16[2,128,1408]{2,1,0:T(8,128)(2,1)}, bf16[2,128,1408]{2,1,0:T(8,128)(2,1)}, u32[]{:S(2)}, u32[]{:S(2)}) collective-permute-start(bf16[2,128,1408]{2,1,0:T(8,128)(2,1)} %collective-permute-done.20.refs_5_), channel_id=1, source_target_pairs={{0,2},{2,0},{1,3},{3,1},{4,6},{6,4},{5,7},{7,5},{8,10},{10,8},{9,1... | collective-permute-start | bytes 2162696 | tf_op jit(solution)/shard_map/gate_up_1_corner/ppermute | solution.py:43
  304.7 14.0 %collective-permute-start.25 = (bf16[2,128,1024]{2,1,0:T(8,128)(2,1)S(1)}, bf16[2,128,1024]{2,1,0:T(8,128)(2,1)S(1)}, u32[]{:S(2)}, u32[]{:S(2)}) collective-permute-start(bf16[2,128,1024]{2,1,0:T(8,128)(2,1)S(1)} %dynamic-slice_bitcast_fusion.8), channel_id=1, source_target_pairs={{0,4},{4,0},{1,5},{5,1},{2,6},{6,2},{3,7},{7,3},{8,12},{12,8},{9,1... | collective-permute-start | bytes 1572872 | tf_op jit(solution)/shard_map/sum_places_0/ppermute | solution.py:43
  304.8 14.1 %collective-permute-start.24 = (bf16[2,128,1024]{2,1,0:T(8,128)(2,1)S(1)}, bf16[2,128,1024]{2,1,0:T(8,128)(2,1)S(1)}, u32[]{:S(2)}, u32[]{:S(2)}) collective-permute-start(bf16[2,128,1024]{2,1,0:T(8,128)(2,1)S(1)} %dynamic-slice_bitcast_fusion.9), channel_id=1, source_target_pairs={{0,8},{8,0},{1,9},{9,1},{2,10},{10,2},{3,11},{11,3},{4,12},{12,4},... | collective-permute-start | bytes 1572872 | tf_op jit(solution)/shard_map/sum_places_0/ppermute | solution.py:43
  321.2 16.8 %collective-permute-start.28 = (bf16[2,128,1408]{2,1,0:T(8,128)(2,1)S(1)}, bf16[2,128,1408]{2,1,0:T(8,128)(2,1)S(1)}, u32[]{:S(2)}, u32[]{:S(2)}) collective-permute-start(bf16[2,128,1408]{2,1,0:T(8,128)(2,1)S(1)} %get-tuple-element.189), channel_id=1, source_target_pairs={{0,2},{2,0},{1,3},{3,1},{4,6},{6,4},{5,7},{7,5},{8,10},{10,8},{9,1... | collective-permute-start | bytes 2162696 | tf_op jit(solution)/shard_map/grad_gate_up_far_0/ppermute | solution.py:43
  340.0 164.4 %reduce-scatter.2.cloned.1.call-start = ((), (), s32[]{:S(2)}) async-start(), calls=%async_computation.10 | async-start | bytes 3604480 | tf_op jit(solution)/shard_map/reduce_scatter | solution.py:784
  351.9 34.9 %collective-permute-start.30 = (bf16[2,128,1408]{2,1,0:T(8,128)(2,1)S(1)}, bf16[2,128,1408]{2,1,0:T(8,128)(2,1)S(1)}, u32[]{:S(2)}, u32[]{:S(2)}) collective-permute-start(bf16[2,128,1408]{2,1,0:T(8,128)(2,1)S(1)} %add_convert_fusion.5), channel_id=1, source_target_pairs={{0,16},{16,0},{1,17},{17,1},{2,18},{18,2},{3,19},{19,3},{4,20},{20... | collective-permute-start | bytes 2162696 | tf_op jit(solution)/shard_map/grad_gate_up_0_relay/ppermute | solution.py:43
  352.5 35.2 %collective-permute-start.29 = (bf16[2,128,1408]{2,1,0:T(8,128)(2,1)S(1)}, bf16[2,128,1408]{2,1,0:T(8,128)(2,1)S(1)}, u32[]{:S(2)}, u32[]{:S(2)}) collective-permute-start(bf16[2,128,1408]{2,1,0:T(8,128)(2,1)S(1)} %copy-done.54), channel_id=1, source_target_pairs={{0,2},{2,0},{1,3},{3,1},{4,6},{6,4},{5,7},{7,5},{8,10},{10,8},{9,1... | collective-permute-start | bytes 2162696 | tf_op jit(solution)/shard_map/grad_gate_up_far_1/ppermute | solution.py:43
  387.8 28.6 %collective-permute-start.34 = (bf16[2,128,1408]{2,1,0:T(8,128)(2,1)}, bf16[2,128,1408]{2,1,0:T(8,128)(2,1)S(1)}, u32[]{:S(2)}, u32[]{:S(2)}) collective-permute-start(bf16[2,128,1408]{2,1,0:T(8,128)(2,1)} %get-tuple-element.210), channel_id=1, source_target_pairs={{0,2},{2,0},{1,3},{3,1},{4,6},{6,4},{5,7},{7,5},{8,10},{10,8},{9,1... | collective-permute-start | bytes 2162696 | tf_op jit(solution)/shard_map/grad_gate_up_near_0/ppermute | solution.py:43
  388.0 33.1 %collective-permute-start.35 = (bf16[2,128,1408]{2,1,0:T(8,128)(2,1)}, bf16[2,128,1408]{2,1,0:T(8,128)(2,1)S(1)}, u32[]{:S(2)}, u32[]{:S(2)}) collective-permute-start(bf16[2,128,1408]{2,1,0:T(8,128)(2,1)} %get-tuple-element.211), channel_id=1, source_target_pairs={{0,2},{2,0},{1,3},{3,1},{4,6},{6,4},{5,7},{7,5},{8,10},{10,8},{9,1... | collective-permute-start | bytes 2162696 | tf_op jit(solution)/shard_map/grad_gate_up_near_1/ppermute | solution.py:43
  390.0 32.3 %collective-permute-start.36 = (bf16[2,128,1408]{2,1,0:T(8,128)(2,1)S(1)}, bf16[2,128,1408]{2,1,0:T(8,128)(2,1)S(1)}, u32[]{:S(2)}, u32[]{:S(2)}) collective-permute-start(bf16[2,128,1408]{2,1,0:T(8,128)(2,1)S(1)} %add_convert_fusion.4), channel_id=1, source_target_pairs={{0,16},{16,0},{1,17},{17,1},{2,18},{18,2},{3,19},{19,3},{4,20},{20... | collective-permute-start | bytes 2162696 | tf_op jit(solution)/shard_map/grad_gate_up_1_relay/ppermute | solution.py:43
  392.3 24.0 %collective-permute-start.32 = (bf16[2,128,1024]{2,1,0:T(8,128)(2,1)S(1)}, bf16[2,128,1024]{2,1,0:T(8,128)(2,1)S(1)}, u32[]{:S(2)}, u32[]{:S(2)}) collective-permute-start(bf16[2,128,1024]{2,1,0:T(8,128)(2,1)S(1)} %get-tuple-element.297), channel_id=1, source_target_pairs={{0,8},{8,0},{1,9},{9,1},{2,10},{10,2},{3,11},{11,3},{4,12},{12,4},... | collective-permute-start | bytes 1572872 | tf_op jit(solution)/shard_map/sum_places_0/ppermute | solution.py:43
  394.7 21.6 %collective-permute-start.33 = (bf16[2,128,1024]{2,1,0:T(8,128)(2,1)S(1)}, bf16[2,128,1024]{2,1,0:T(8,128)(2,1)S(1)}, u32[]{:S(2)}, u32[]{:S(2)}) collective-permute-start(bf16[2,128,1024]{2,1,0:T(8,128)(2,1)S(1)} %get-tuple-element.295), channel_id=1, source_target_pairs={{0,4},{4,0},{1,5},{5,1},{2,6},{6,2},{3,7},{7,3},{8,12},{12,8},{9,1... | collective-permute-start | bytes 1572872 | tf_op jit(solution)/shard_map/sum_places_0/ppermute | solution.py:43
  425.7 9.6 %collective-permute-start.37 = (bf16[512,2048]{1,0:T(8,128)(2,1)}, bf16[512,2048]{1,0:T(8,128)(2,1)}, u32[]{:S(2)}, u32[]{:S(2)}) collective-permute-start(bf16[512,2048]{1,0:T(8,128)(2,1)} %convolution_convert_fusion.2), channel_id=1, source_target_pairs={{0,1},{1,0},{2,3},{3,2},{4,5},{5,4},{6,7},{7,6},{8,9},{9,8},{10,11... | collective-permute-start | bytes 6291464 | tf_op jit(solution)/shard_map/sum_cores/ppermute | solution.py:43
  430.9 13.3 %collective-permute-start.39 = (bf16[128,1024]{1,0:T(8,128)(2,1)S(1)}, bf16[128,1024]{1,0:T(8,128)(2,1)S(1)}, u32[]{:S(2)}, u32[]{:S(2)}) collective-permute-start(bf16[128,1024]{1,0:T(8,128)(2,1)S(1)} %get-tuple-element.303), channel_id=1, source_target_pairs={{0,8},{8,0},{1,9},{9,1},{2,10},{10,2},{3,11},{11,3},{4,12},{12,4},... | collective-permute-start | bytes 786440 | tf_op jit(solution)/shard_map/sum_places_1/ppermute | solution.py:43
  445.1 13.2 %collective-permute-start.41 = (bf16[2,128,1024]{2,1,0:T(8,128)(2,1)}, bf16[2,128,1024]{2,1,0:T(8,128)(2,1)}, u32[]{:S(2)}, u32[]{:S(2)}) collective-permute-start(bf16[2,128,1024]{2,1,0:T(8,128)(2,1)} %dynamic-slice_bitcast_fusion.2), channel_id=1, source_target_pairs={{0,4},{4,0},{1,5},{5,1},{2,6},{6,2},{3,7},{7,3},{8,12},{12,8},{9,1... | collective-permute-start | bytes 1572872 | tf_op jit(solution)/shard_map/sum_places_0/ppermute | solution.py:43
  447.0 22.5 %collective-permute-start.40 = (bf16[2,128,1024]{2,1,0:T(8,128)(2,1)}, bf16[2,128,1024]{2,1,0:T(8,128)(2,1)}, u32[]{:S(2)}, u32[]{:S(2)}) collective-permute-start(bf16[2,128,1024]{2,1,0:T(8,128)(2,1)} %dynamic-slice_bitcast_fusion.3), channel_id=1, source_target_pairs={{0,8},{8,0},{1,9},{9,1},{2,10},{10,2},{3,11},{11,3},{4,12},{12,4},... | collective-permute-start | bytes 1572872 | tf_op jit(solution)/shard_map/sum_places_0/ppermute | solution.py:43
  448.1 22.8 %collective-permute-start.42 = (bf16[4,128,384]{2,1,0:T(8,128)(2,1)}, bf16[4,128,384]{2,1,0:T(8,128)(2,1)S(1)}, u32[]{:S(2)}, u32[]{:S(2)}) collective-permute-start(bf16[4,128,384]{2,1,0:T(8,128)(2,1)} %get-tuple-element.219), channel_id=1, source_target_pairs={{0,2},{2,0},{1,3},{3,1},{4,6},{6,4},{5,7},{7,5},{8,10},{10,8},{9,1... | collective-permute-start | bytes 1179656 | tf_op jit(solution)/shard_map/grad_attn_far/ppermute | solution.py:43
  472.3 12.3 %collective-permute-start.44 = (bf16[128,1024]{1,0:T(8,128)(2,1)S(1)}, bf16[128,1024]{1,0:T(8,128)(2,1)S(1)}, u32[]{:S(2)}, u32[]{:S(2)}) collective-permute-start(bf16[128,1024]{1,0:T(8,128)(2,1)S(1)} %dynamic-slice_bitcast_fusion.12), channel_id=1, source_target_pairs={{0,8},{8,0},{1,9},{9,1},{2,10},{10,2},{3,11},{11,3},{4,12},{12,4},... | collective-permute-start | bytes 786440 | tf_op jit(solution)/shard_map/sum_places_1/ppermute | solution.py:43
  472.3 14.6 %collective-permute-start.45 = (bf16[64,2048]{1,0:T(8,128)(2,1)S(1)}, bf16[64,2048]{1,0:T(8,128)(2,1)S(1)}, u32[]{:S(2)}, u32[]{:S(2)}) collective-permute-start(bf16[64,2048]{1,0:T(8,128)(2,1)S(1)} %get-tuple-element.249), channel_id=1, source_target_pairs={{0,2},{2,0},{1,3},{3,1},{4,6},{6,4},{5,7},{7,5},{8,10},{10,8},{9,1... | collective-permute-start | bytes 786440 | tf_op jit(solution)/shard_map/grad_out_far/ppermute | solution.py:43
  472.4 37.2 %collective-permute-start.50 = (bf16[64,2048]{1,0:T(8,128)(2,1)}, bf16[64,2048]{1,0:T(8,128)(2,1)S(1)}, u32[]{:S(2)}, u32[]{:S(2)}) collective-permute-start(bf16[64,2048]{1,0:T(8,128)(2,1)} %get-tuple-element.271), channel_id=1, source_target_pairs={{0,2},{2,0},{1,3},{3,1},{4,6},{6,4},{5,7},{7,5},{8,10},{10,8},{9,1... | collective-permute-start | bytes 786440 | tf_op jit(solution)/shard_map/grad_out_near/ppermute | solution.py:43
  475.3 34.3 %collective-permute-start.46 = (bf16[4,128,384]{2,1,0:T(8,128)(2,1)}, bf16[4,128,384]{2,1,0:T(8,128)(2,1)S(1)}, u32[]{:S(2)}, u32[]{:S(2)}) collective-permute-start(bf16[4,128,384]{2,1,0:T(8,128)(2,1)} %add_convert_fusion.8), channel_id=1, source_target_pairs={{0,16},{16,0},{1,17},{17,1},{2,18},{18,2},{3,19},{19,3},{4,20},{20... | collective-permute-start | bytes 1179656 | tf_op jit(solution)/shard_map/grad_attn_relay/ppermute | solution.py:43
  488.1 41.5 %all-to-all-start.2 = ((bf16[8,64,1408]{2,1,0:T(8,128)(2,1)}), bf16[8,64,1408]{2,1,0:T(8,128)(2,1)S(1)}, u32[]{:S(2)}, u32[]{:S(2)}) async-start(bf16[8,64,1408]{2,1,0:T(8,128)(2,1)} %bitcast.193), calls=%async_computation.3 | async-start | bytes 2883584 | tf_op jit(solution)/shard_map/all_to_all | solution.py:620
  492.8 21.5 %collective-permute-start.51 = (bf16[64,2048]{1,0:T(8,128)(2,1)}, bf16[64,2048]{1,0:T(8,128)(2,1)}, u32[]{:S(2)}, u32[]{:S(2)}) collective-permute-start(bf16[64,2048]{1,0:T(8,128)(2,1)} %add_convert_fusion.9), channel_id=1, source_target_pairs={{0,16},{16,0},{1,17},{17,1},{2,18},{18,2},{3,19},{19,3},{4,20},{20... | collective-permute-start | bytes 786440 | tf_op jit(solution)/shard_map/grad_out_relay/ppermute | solution.py:43
  495.2 28.6 %collective-permute-start.49 = (bf16[4,128,384]{2,1,0:T(8,128)(2,1)}, bf16[4,128,384]{2,1,0:T(8,128)(2,1)}, u32[]{:S(2)}, u32[]{:S(2)}) collective-permute-start(bf16[4,128,384]{2,1,0:T(8,128)(2,1)} %copy-done.55), channel_id=1, source_target_pairs={{0,2},{2,0},{1,3},{3,1},{4,6},{6,4},{5,7},{7,5},{8,10},{10,8},{9,1... | collective-permute-start | bytes 1179656 | tf_op jit(solution)/shard_map/grad_attn_near/ppermute | solution.py:43
  517.2 32.3 %collective-permute-start.48 = (bf16[64,4096]{1,0:T(8,128)(2,1)}, bf16[64,4096]{1,0:T(8,128)(2,1)}, u32[]{:S(2)}, u32[]{:S(2)}) collective-permute-start(bf16[64,4096]{1,0:T(8,128)(2,1)} %get-tuple-element.293), channel_id=1, source_target_pairs={{0,2},{1,18},{2,0},{3,16},{16,3},{17,19},{18,1},{19,17},{4,6},{5,2... | collective-permute-start | bytes 1572872 | tf_op jit(solution)/shard_map/rows_home/ppermute | solution.py:564
  517.5 32.0 %collective-permute-start.47 = (bf16[64,4096]{1,0:T(8,128)(2,1)}, bf16[64,4096]{1,0:T(8,128)(2,1)}, u32[]{:S(2)}, u32[]{:S(2)}) collective-permute-start(bf16[64,4096]{1,0:T(8,128)(2,1)} %get-tuple-element.294), channel_id=1, source_target_pairs={{0,0},{1,16},{2,2},{3,18},{16,1},{17,17},{18,3},{19,19},{4,4},{5,2... | collective-permute-start | bytes 1572872 | tf_op jit(solution)/shard_map/rows_home/ppermute | solution.py:564
  532.5 22.0 %all-to-all-start.3 = ((bf16[8,64,384]{2,1,0:T(8,128)(2,1)}), bf16[8,64,384]{2,1,0:T(8,128)(2,1)S(1)}, u32[]{:S(2)}, u32[]{:S(2)}) async-start(bf16[8,64,384]{2,1,0:T(8,128)(2,1)} %bitcast.186), calls=%async_computation.4 | async-start | bytes 786432 | tf_op jit(solution)/shard_map/all_to_all | solution.py:620
  (127 other events, 865.7 us)
Sparse Core Ops, SparseCore 0:
  17.6 54.1 all-gather.5
  75.6 71.3 all-gather.11
  149.2 59.7 all-gather.9
  211.3 42.6 all-gather.7
  340.1 36.0 all-gather.13
  425.9 78.4 reduce-scatter.1

commit v3 on v2

--- a/solution.py
+++ b/solution.py
@@ -18,7 +18,7 @@
 CROSS = ((1, 2), (2, 1))
 BF16 = jnp.bfloat16
 F32 = jnp.float32
-VMEM = 32 * 1024 * 1024
+VMEM = 22 * 1024 * 1024
 COST = pl.CostEstimate(flops=1, bytes_accessed=1, transcendentals=0)
 
 NT = (((1,), (1,)), ((), ()))
@@ -832,7 +832,7 @@
     out_relay = layout.relay_sum(out_parts[2], out_far, "grad_out")
     out_near = swap(out_parts[1], layout.low, "grad_out_near")
     grad_input = grad_middle + norm_back(grad_normed_attn, x_wide, gain_attn)
-    grad_rows, attn_relay = tie((grad_input.astype(BF16), attn_relay))
+    grad_rows = grad_input.astype(BF16)
     home = layout.from_team(jnp.concatenate([late["total"], grad_rows], axis=1), "rows_home")
     block_out, grad_input = home[..., :width], home[..., width:].astype(F32)
 

time: 571 us -> 564 us (0.988)
    unnamed x225 -> x219, local copies, waits for them, and re-layouts: 32.1 us -> 31 us
where the time goes in v3:
time: 564 us; the launch traced here: 558 us
  waiting for transfers between devices  256 us (45%)
  starting transfers between devices  96.5 us (17%)
  Pallas kernels  74.4 us (13%)
  local copies, waits for them, and re-layouts  46.3 us (8%)
  other arithmetic  36.7 us (7%)
  matrix products  32.1 us (6%)
  between operations  16 us (3%)
    ppermute x44, waiting for transfers between devices, swap(): return lax.ppermute(array, axis, SWAP)  220 us
    ppermute x44, starting transfers between devices, swap(): return lax.ppermute(array, axis, SWAP)  50.6 us
    dot_general x10, matrix products, dot(): return lax.dot_general(left, right, dims, preferred_element_type=F32)  32.1 us
    unnamed x219, local copies, waits for them, and re-layouts  31 us
    all_to_all x4, starting transfers between devices, exchange(): return lax.all_to_all(array, self.mid + ('core',), 0, 0, tiled=True)  30.3 us
    pallas_call x1, Pallas kernels, attend_backward(): pl.pallas_call(functools.partial(backward_kernel, heads), grid=(rows // b...  18.7 us
    all_to_all x4, waiting for transfers between devices, exchange(): return lax.all_to_all(array, self.mid + ('core',), 0, 0, tiled=True)  16.2 us
    pallas_call x3, Pallas kernels, outer_rows(): pl.pallas_call(functools.partial(rows_kernel, sides, chunks), grid_spec=p...  14.6 us
  transfers between devices with their start and end apart: 63, of which 32 were waited for; matrix products, arithmetic and copies ran while one was open for 12% of the time, Pallas kernels for 11%

profile of v3, /device:TPU:0, one launch (start us, length us, event | category | flops | bytes accessed | tf_op | source)
XLA Modules:
  0.0 558.1 jit_solution(15251877067564330587)
XLA Ops:
  9.1 3.0 collective-permute-start.1
  12.1 4.3 collective-permute-done.1
  19.8 9.7 %collective-permute-start.2 = (bf16[64,2688]{1,0:T(8,128)(2,1)S(1)}, bf16[64,2688]{1,0:T(8,128)(2,1)S(1)}, u32[]{:S(2)}, u32[]{:S(2)}) collective-permute-start(bf16[64,2688]{1,0:T(8,128)(2,1)S(1)} %fusion.21.own), channel_id=1, source_target_pairs={{0,16},{16,0},{1,17},{17,1},{2,18},{18,2},{3,19},{19,3},{4,20},{20... | collective-permute-start | bytes 1032200 | tf_op jit(solution)/shard_map/raw_far/ppermute | solution.py:43
  35.1 8.7 %collective-permute-done.2.far = bf16[64,2688]{1,0:T(8,128)(2,1)S(1)} collective-permute-done((bf16[64,2688]{1,0:T(8,128)(2,1)S(1)}, bf16[64,2688]{1,0:T(8,128)(2,1)S(1)}, u32[]{:S(2)}, u32[]{:S(2)}) %collective-permute-start.2) | collective-permute-done | bytes 344096 | tf_op jit(solution)/shard_map/raw_far/ppermute | solution.py:43
  50.0 3.1 collective-permute-done.5.corner
  55.4 5.7 %collective-permute-done.8 = bf16[64,2048]{1,0:T(8,128)(2,1)S(1)} collective-permute-done((bf16[64,2048]{1,0:T(8,128)(2,1)S(1)}, bf16[64,2048]{1,0:T(8,128)(2,1)S(1)}, u32[]{:S(2)}, u32[]{:S(2)}) %collective-permute-start.8) | collective-permute-done | bytes 262176 | tf_op jit(solution)/shard_map/cotangent/ppermute | solution.py:564
  61.8 11.1 %all-to-all-start = ((bf16[8,272,384]{2,1,0:T(8,128)(2,1)}), bf16[8,272,384]{2,1,0:T(8,128)(2,1)S(1)}, u32[]{:S(2)}, u32[]{:S(2)}) async-start(bf16[8,272,384]{2,1,0:T(8,128)(2,1)} %copy-done.4), calls=%async_computation | async-start | bytes 3342336 | tf_op jit(solution)/shard_map/all_to_all | solution.py:620
  76.2 6.3 %collective-permute-done.10 = bf16[64,2048]{1,0:T(8,128)(2,1)S(1)} collective-permute-done((bf16[64,2048]{1,0:T(8,128)(2,1)S(1)}, bf16[64,2048]{1,0:T(8,128)(2,1)S(1)}, u32[]{:S(2)}, u32[]{:S(2)}) %collective-permute-start.10) | collective-permute-done | bytes 262176 | tf_op jit(solution)/shard_map/out_near/ppermute | solution.py:43
  83.1 22.2 %collective-permute-done.9 = bf16[64,2048]{1,0:T(8,128)(2,1)} collective-permute-done((bf16[64,2048]{1,0:T(8,128)(2,1)S(1)}, bf16[64,2048]{1,0:T(8,128)(2,1)}, u32[]{:S(2)}, u32[]{:S(2)}) %collective-permute-start.9) | collective-permute-done | bytes 262176 | tf_op jit(solution)/shard_map/out_far/ppermute | solution.py:43
  106.9 4.3 all-to-all-start.1
  118.4 5.4 project.1
  127.1 12.2 %attend_forward.1 = (bf16[1024,256]{1,0:T(8,128)(2,1)S(1)}, f32[8,1024]{1,0:T(8,128)S(1)}) custom-call(bf16[1024,256]{1,0:T(8,128)(2,1)S(1)} %get-tuple-element.152.q_ref, bf16[1024,256]{1,0:T(8,128)(2,1)S(1)} %get-tuple-element.153.k_ref, bf16[256,1024]{1,0:T(8,128)(2,1)S(1)} %get-tuple-element.154.vt_ref, f32[1024,128]{1,0:T(8,128)S(1)} %pad.9.marks_ref.marks_all_ref, ...), custom_call_target="tpu_custom_call" | custom-call | flops 1 | bytes 1 | tf_op jit(solution)/shard_map/attend_forward/pallas_call | solution.py:212
  140.1 4.5 all-to-all-done.1
  148.0 4.5 collective-permute-done.12
  160.7 14.8 %collective-permute-done.15 = bf16[2,128,1024]{2,1,0:T(8,128)(2,1)S(1)} collective-permute-done((bf16[2,128,1024]{2,1,0:T(8,128)(2,1)S(1)}, bf16[2,128,1024]{2,1,0:T(8,128)(2,1)S(1)}, u32[]{:S(2)}, u32[]{:S(2)}) %collective-permute-start.15) | collective-permute-done | bytes 524320 | tf_op jit(solution)/shard_map/sum_places_0/ppermute | solution.py:43
  175.7 5.3 collective-permute-start.16
  181.0 17.1 %collective-permute-done.13 = bf16[2,128,1024]{2,1,0:T(8,128)(2,1)S(1)} collective-permute-done((bf16[2,128,1024]{2,1,0:T(8,128)(2,1)S(1)}, bf16[2,128,1024]{2,1,0:T(8,128)(2,1)S(1)}, u32[]{:S(2)}, u32[]{:S(2)}) %collective-permute-start.13) | collective-permute-done | bytes 524320 | tf_op jit(solution)/shard_map/sum_places_0/ppermute | solution.py:43
  198.7 9.1 %collective-permute-done.16 = bf16[128,1024]{1,0:T(8,128)(2,1)S(1)} collective-permute-done((bf16[128,1024]{1,0:T(8,128)(2,1)S(1)}, bf16[128,1024]{1,0:T(8,128)(2,1)S(1)}, u32[]{:S(2)}, u32[]{:S(2)}) %collective-permute-start.16) | collective-permute-done | bytes 262176 | tf_op jit(solution)/shard_map/sum_places_1/ppermute | solution.py:43
  216.2 29.9 %collective-permute-done.20.refs_5_ = bf16[2,128,1408]{2,1,0:T(8,128)(2,1)} collective-permute-done((bf16[2,128,1408]{2,1,0:T(8,128)(2,1)S(1)}, bf16[2,128,1408]{2,1,0:T(8,128)(2,1)}, u32[]{:S(2)}, u32[]{:S(2)}) %collective-permute-start.20) | collective-permute-done | bytes 720928 | tf_op jit(solution)/shard_map/gate_up_1_far/ppermute | solution.py:43
  247.3 17.1 %collective-permute-done.22.refs_7_ = bf16[2,128,1408]{2,1,0:T(8,128)(2,1)} collective-permute-done((bf16[2,128,1408]{2,1,0:T(8,128)(2,1)}, bf16[2,128,1408]{2,1,0:T(8,128)(2,1)}, u32[]{:S(2)}, u32[]{:S(2)}) %collective-permute-start.22) | collective-permute-done | bytes 720928 | tf_op jit(solution)/shard_map/gate_up_1_corner/ppermute | solution.py:43
  272.8 14.2 %feed_forward.1 = (bf16[1024,704]{1,0:T(8,128)(2,1)S(1)}, bf16[1024,1408]{1,0:T(8,128)(2,1)S(1)}, bf16[2,4,2,128,1408]{4,3,2,1,0:T(8,128)(2,1)S(1)}) custom-call(s32[3]{0:T(128)S(1)} %pad_add_fusion.bits_ref, bf16[1024,2048]{1,0:T(8,128)(2,1)S(1)} %copy-done.2, bf16[1024,2048]{1,0:T(8,128)(2,1)S(1)} %copy-done.8, bf16[704,2048]{1,0:T(8,128)(2,1)S(1)} %copy-done.14, ...), custom_call_target="tpu_custom_call" | custom-call | flops 1 | bytes 1 | tf_op jit(solution)/shard_map/feed_forward/pallas_call | solution.py:338
  287.0 3.7 convolution_convert_fusion.4
  290.8 4.1 collective-permute-done.23
  295.0 3.7 add_convert_fusion.2
  301.0 4.6 outer_rows.3
  305.6 7.3 %collective-permute-done.25 = bf16[2,128,1024]{2,1,0:T(8,128)(2,1)S(1)} collective-permute-done((bf16[2,128,1024]{2,1,0:T(8,128)(2,1)S(1)}, bf16[2,128,1024]{2,1,0:T(8,128)(2,1)S(1)}, u32[]{:S(2)}, u32[]{:S(2)}) %collective-permute-start.25) | collective-permute-done | bytes 524320 | tf_op jit(solution)/shard_map/sum_places_0/ppermute | solution.py:43
  315.8 5.7 %outer_rows.4 = (bf16[2,128,1408]{2,1,0:T(8,128)(2,1)S(1)}, bf16[2,128,1408]{2,1,0:T(8,128)(2,1)S(1)}, bf16[2,128,1408]{2,1,0:T(8,128)(2,1)}, bf16[2,128,1408]{2,1,0:T(8,128)(2,1)}) custom-call(s32[3]{0:T(128)S(1)} %pad_add_fusion.bits_ref, bf16[1024,2048]{1,0:T(8,128)(2,1)S(1)} %copy-done.3, bf16[1024,1408]{1,0:T(8,128)(2,1)S(1)} %get-tuple-element.182.right_ref), custom_call_target="tpu_custom_call" | custom-call | flops 1 | bytes 1 | tf_op jit(solution)/shard_map/outer_rows/pallas_call | solution.py:388
  322.7 9.6 %collective-permute-done.28 = bf16[2,128,1408]{2,1,0:T(8,128)(2,1)S(1)} collective-permute-done((bf16[2,128,1408]{2,1,0:T(8,128)(2,1)S(1)}, bf16[2,128,1408]{2,1,0:T(8,128)(2,1)S(1)}, u32[]{:S(2)}, u32[]{:S(2)}) %collective-permute-start.28) | collective-permute-done | bytes 720928 | tf_op jit(solution)/shard_map/grad_gate_up_far_0/ppermute | solution.py:43
  334.6 7.4 %convolution_convert_fusion = bf16[704,2048]{1,0:T(8,128)(2,1)} fusion(bf16[1024,704]{1,0:T(8,128)(2,1)} %copy-done.49, bf16[1024,2048]{1,0:T(8,128)(2,1)} %all-gather.10.cloned.1.call-done.g_ref), kind=kOutput, calls=%fused_computation.4 | convolution fusion | flops 2954231808 | bytes 8519680 | tf_op jit(solution)/shard_map/dot_general | solution.py:30
  342.0 4.0 convolution_convert_fusion.3
  353.9 27.4 %collective-permute-done.30.refs_2_ = bf16[2,128,1408]{2,1,0:T(8,128)(2,1)S(1)} collective-permute-done((bf16[2,128,1408]{2,1,0:T(8,128)(2,1)S(1)}, bf16[2,128,1408]{2,1,0:T(8,128)(2,1)S(1)}, u32[]{:S(2)}, u32[]{:S(2)}) %collective-permute-start.30) | collective-permute-done | bytes 720928 | tf_op jit(solution)/shard_map/grad_gate_up_0_relay/ppermute | solution.py:43
  391.2 18.7 %attend_backward.1 = (bf16[1024,256]{1,0:T(8,128)(2,1)S(1)}, bf16[1024,128]{1,0:T(8,128)(2,1)S(1)}) custom-call(bf16[1024,256]{1,0:T(8,128)(2,1)S(1)} %copy-done.23, bf16[1024,256]{1,0:T(8,128)(2,1)S(1)} %convolution_convert_fusion.5.g_ref, bf16[1024,256]{1,0:T(8,128)(2,1)S(1)} %copy-done.25, bf16[1024,256]{1,0:T(8,128)(2,1)S(1)} %copy-done.44, ...), custom_call_target="tpu_custom_call" | custom-call | flops 1 | bytes 1 | tf_op jit(solution)/shard_map/attend_backward/pallas_call | solution.py:281
  411.6 3.9 collective-permute-done.35.refs_4_
  417.6 2.7 convolution_convert_fusion.2
  425.5 4.3 outer_rows.5
  429.8 3.2 add_convert_fusion
  433.3 5.5 collective-permute-done.39
  445.8 3.2 outer_quarters.1
  449.0 3.9 collective-permute-done.41
  453.1 11.1 %collective-permute-done.40 = bf16[2,128,1024]{2,1,0:T(8,128)(2,1)} collective-permute-done((bf16[2,128,1024]{2,1,0:T(8,128)(2,1)}, bf16[2,128,1024]{2,1,0:T(8,128)(2,1)}, u32[]{:S(2)}, u32[]{:S(2)}) %collective-permute-start.40) | collective-permute-done | bytes 524320 | tf_op jit(solution)/shard_map/sum_places_0/ppermute | solution.py:43
  474.9 4.1 collective-permute-done.44
  482.6 4.0 all-to-all-start.2
  490.1 8.7 %reduce-scatter.2.cloned.1.call-done = bf16[176,2048]{1,0:T(8,128)(2,1)} async-done(((bf16[704,2048]{1,0:T(8,128)(2,1)}), bf16[176,2048]{1,0:T(8,128)(2,1)}) %reduce-scatter.2.cloned.1.call-update) | async-done | bytes 720912 | tf_op jit(solution)/shard_map/reduce_scatter | solution.py:784
  503.9 4.9 collective-permute-done.51.refs_2_
  511.1 5.3 collective-permute-start.46
  517.3 6.9 %all-to-all-done.2.refs_4_.in_ref = bf16[8,64,1408]{2,1,0:T(8,128)(2,1)S(1)} async-done(((bf16[8,64,1408]{2,1,0:T(8,128)(2,1)}), bf16[8,64,1408]{2,1,0:T(8,128)(2,1)S(1)}, u32[]{:S(2)}, u32[]{:S(2)}) %all-to-all-start.2) | async-done | bytes 1441824 | tf_op jit(solution)/shard_map/all_to_all | solution.py:620
  526.2 10.9 %all-to-all-start.3 = ((bf16[8,64,384]{2,1,0:T(8,128)(2,1)}), bf16[8,64,384]{2,1,0:T(8,128)(2,1)S(1)}, u32[]{:S(2)}, u32[]{:S(2)}) async-start(bf16[8,64,384]{2,1,0:T(8,128)(2,1)} %bitcast.186), calls=%async_computation.4 | async-start | bytes 786432 | tf_op jit(solution)/shard_map/all_to_all | solution.py:620
  544.8 3.2 all-to-all-done.3
  (435 shorter events, 147.3 us)
Async XLA Ops:
  7.3 109.0 %all-gather.6.cloned.1.call-start = ((), (), s32[]{:S(2)}) async-start(), calls=%async_computation.5 | async-start | bytes 4718592 | tf_op jit(solution)/shard_map/all_gather | solution.py:584
  17.7 17.4 %collective-permute-start.3 = (bf16[64,2688]{1,0:T(8,128)(2,1)S(1)}, bf16[64,2688]{1,0:T(8,128)(2,1)S(1)}, u32[]{:S(2)}, u32[]{:S(2)}) collective-permute-start(bf16[64,2688]{1,0:T(8,128)(2,1)S(1)} %fusion.21.own), channel_id=1, source_target_pairs={{0,2},{2,0},{1,3},{3,1},{4,6},{6,4},{5,7},{7,5},{8,10},{10,8},{9,1... | collective-permute-start | bytes 1032200 | tf_op jit(solution)/shard_map/raw_near/ppermute | solution.py:43
  19.8 24.0 %collective-permute-start.2 = (bf16[64,2688]{1,0:T(8,128)(2,1)S(1)}, bf16[64,2688]{1,0:T(8,128)(2,1)S(1)}, u32[]{:S(2)}, u32[]{:S(2)}) collective-permute-start(bf16[64,2688]{1,0:T(8,128)(2,1)S(1)} %fusion.21.own), channel_id=1, source_target_pairs={{0,16},{16,0},{1,17},{17,1},{2,18},{18,2},{3,19},{19,3},{4,20},{20... | collective-permute-start | bytes 1032200 | tf_op jit(solution)/shard_map/raw_far/ppermute | solution.py:43
  46.0 15.1 %collective-permute-start.8 = (bf16[64,2048]{1,0:T(8,128)(2,1)S(1)}, bf16[64,2048]{1,0:T(8,128)(2,1)S(1)}, u32[]{:S(2)}, u32[]{:S(2)}) collective-permute-start(bf16[64,2048]{1,0:T(8,128)(2,1)S(1)} %get-tuple-element.309), channel_id=1, source_target_pairs={{0,2},{1,18},{2,0},{3,16},{16,3},{17,19},{18,1},{19,17},{4,6},{5,2... | collective-permute-start | bytes 786440 | tf_op jit(solution)/shard_map/cotangent/ppermute | solution.py:564
  47.7 14.1 %collective-permute-start.7 = (bf16[64,2048]{1,0:T(8,128)(2,1)S(1)}, bf16[64,2048]{1,0:T(8,128)(2,1)}, u32[]{:S(2)}, u32[]{:S(2)}) collective-permute-start(bf16[64,2048]{1,0:T(8,128)(2,1)S(1)} %get-tuple-element.310), channel_id=1, source_target_pairs={{0,0},{1,16},{2,2},{3,18},{16,1},{17,17},{18,3},{19,19},{4,4},{5,2... | collective-permute-start | bytes 786440 | tf_op jit(solution)/shard_map/cotangent/ppermute | solution.py:564
  61.8 45.1 %all-to-all-start = ((bf16[8,272,384]{2,1,0:T(8,128)(2,1)}), bf16[8,272,384]{2,1,0:T(8,128)(2,1)S(1)}, u32[]{:S(2)}, u32[]{:S(2)}) async-start(bf16[8,272,384]{2,1,0:T(8,128)(2,1)} %copy-done.4), calls=%async_computation | async-start | bytes 3342336 | tf_op jit(solution)/shard_map/all_to_all | solution.py:620
  72.9 173.2 %all-gather.12.cloned.1.call-start = ((), (), s32[]{:S(2)}) async-start(), calls=%async_computation.8 | async-start | bytes 3604480 | tf_op jit(solution)/shard_map/all_gather | solution.py:697
  74.3 31.1 %collective-permute-start.9 = (bf16[64,2048]{1,0:T(8,128)(2,1)S(1)}, bf16[64,2048]{1,0:T(8,128)(2,1)}, u32[]{:S(2)}, u32[]{:S(2)}) collective-permute-start(bf16[64,2048]{1,0:T(8,128)(2,1)S(1)} %broadcast_select_fusion.2), channel_id=1, source_target_pairs={{0,16},{16,0},{1,17},{17,1},{2,18},{18,2},{3,19},{19,3},{4,20},{20... | collective-permute-start | bytes 786440 | tf_op jit(solution)/shard_map/out_far/ppermute | solution.py:43
  106.9 37.8 %all-to-all-start.1 = ((bf16[8,64,1408]{2,1,0:T(8,128)(2,1)}), bf16[8,64,1408]{2,1,0:T(8,128)(2,1)}, u32[]{:S(2)}, u32[]{:S(2)}) async-start(bf16[8,64,1408]{2,1,0:T(8,128)(2,1)} %copy-done.7), calls=%async_computation.1 | async-start | bytes 2883584 | tf_op jit(solution)/shard_map/all_to_all | solution.py:620
  111.2 134.9 %all-gather.10.cloned.1.call-start = ((), (), s32[]{:S(2)}) async-start(), calls=%async_computation.7 | async-start | bytes 4718592 | tf_op jit(solution)/shard_map/all_gather | solution.py:584
  113.2 151.2 %all-gather.8.cloned.1.call-start = ((), (), s32[]{:S(2)}) async-start(), calls=%async_computation.6 | async-start | bytes 4718592 | tf_op jit(solution)/shard_map/all_gather | solution.py:584
  113.5 26.6 %collective-permute-start.11 = (bf16[64,2048]{1,0:T(8,128)(2,1)}, bf16[64,2048]{1,0:T(8,128)(2,1)}, u32[]{:S(2)}, u32[]{:S(2)}) collective-permute-start(bf16[64,2048]{1,0:T(8,128)(2,1)} %collective-permute-done.9), channel_id=1, source_target_pairs={{0,2},{2,0},{1,3},{3,1},{4,6},{6,4},{5,7},{7,5},{8,10},{10,8},{9,1... | collective-permute-start | bytes 786440 | tf_op jit(solution)/shard_map/out_corner/ppermute | solution.py:43
  155.1 20.4 %collective-permute-start.15 = (bf16[2,128,1024]{2,1,0:T(8,128)(2,1)S(1)}, bf16[2,128,1024]{2,1,0:T(8,128)(2,1)S(1)}, u32[]{:S(2)}, u32[]{:S(2)}) collective-permute-start(bf16[2,128,1024]{2,1,0:T(8,128)(2,1)S(1)} %dynamic-slice_bitcast_fusion.10), channel_id=1, source_target_pairs={{0,4},{4,0},{1,5},{5,1},{2,6},{6,2},{3,7},{7,3},{8,12},{12,8},{9,1... | collective-permute-start | bytes 1572872 | tf_op jit(solution)/shard_map/sum_places_0/ppermute | solution.py:43
  156.7 41.4 %collective-permute-start.13 = (bf16[2,128,1024]{2,1,0:T(8,128)(2,1)S(1)}, bf16[2,128,1024]{2,1,0:T(8,128)(2,1)S(1)}, u32[]{:S(2)}, u32[]{:S(2)}) collective-permute-start(bf16[2,128,1024]{2,1,0:T(8,128)(2,1)S(1)} %dynamic-slice_bitcast_fusion.11), channel_id=1, source_target_pairs={{0,8},{8,0},{1,9},{9,1},{2,10},{10,2},{3,11},{11,3},{4,12},{12,4},... | collective-permute-start | bytes 1572872 | tf_op jit(solution)/shard_map/sum_places_0/ppermute | solution.py:43
  159.4 48.7 %collective-permute-start.18 = (bf16[2,128,1408]{2,1,0:T(8,128)(2,1)S(1)}, bf16[2,128,1408]{2,1,0:T(8,128)(2,1)S(1)}, u32[]{:S(2)}, u32[]{:S(2)}) collective-permute-start(bf16[2,128,1408]{2,1,0:T(8,128)(2,1)S(1)} %bitcast.183), channel_id=1, source_target_pairs={{0,2},{2,0},{1,3},{3,1},{4,6},{6,4},{5,7},{7,5},{8,10},{10,8},{9,1... | collective-permute-start | bytes 2162696 | tf_op jit(solution)/shard_map/gate_up_0_near/ppermute | solution.py:43
  159.9 49.1 %collective-permute-start.17 = (bf16[2,128,1408]{2,1,0:T(8,128)(2,1)S(1)}, bf16[2,128,1408]{2,1,0:T(8,128)(2,1)S(1)}, u32[]{:S(2)}, u32[]{:S(2)}) collective-permute-start(bf16[2,128,1408]{2,1,0:T(8,128)(2,1)S(1)} %bitcast.184), channel_id=1, source_target_pairs={{0,16},{16,0},{1,17},{17,1},{2,18},{18,2},{3,19},{19,3},{4,20},{20... | collective-permute-start | bytes 2162696 | tf_op jit(solution)/shard_map/gate_up_0_far/ppermute | solution.py:43
  175.7 32.1 %collective-permute-start.16 = (bf16[128,1024]{1,0:T(8,128)(2,1)S(1)}, bf16[128,1024]{1,0:T(8,128)(2,1)S(1)}, u32[]{:S(2)}, u32[]{:S(2)}) collective-permute-start(bf16[128,1024]{1,0:T(8,128)(2,1)S(1)} %dynamic-slice_bitcast_fusion.20), channel_id=1, source_target_pairs={{0,8},{8,0},{1,9},{9,1},{2,10},{10,2},{3,11},{11,3},{4,12},{12,4},... | collective-permute-start | bytes 786440 | tf_op jit(solution)/shard_map/sum_places_1/ppermute | solution.py:43
  198.3 9.5 %collective-permute-start.14 = (bf16[128,1024]{1,0:T(8,128)(2,1)S(1)}, bf16[128,1024]{1,0:T(8,128)(2,1)S(1)}, u32[]{:S(2)}, u32[]{:S(2)}) collective-permute-start(bf16[128,1024]{1,0:T(8,128)(2,1)S(1)} %dynamic-slice_bitcast_fusion.21), channel_id=1, source_target_pairs={{0,4},{4,0},{1,5},{5,1},{2,6},{6,2},{3,7},{7,3},{8,12},{12,8},{9,1... | collective-permute-start | bytes 786440 | tf_op jit(solution)/shard_map/sum_places_1/ppermute | solution.py:43
  211.1 171.0 %all-gather.14.cloned.1.call-start = ((), (), s32[]{:S(2)}) async-start(), calls=%async_computation.9 | async-start | bytes 4718592 | tf_op jit(solution)/shard_map/all_gather | solution.py:584
  211.7 34.4 %collective-permute-start.20 = (bf16[2,128,1408]{2,1,0:T(8,128)(2,1)S(1)}, bf16[2,128,1408]{2,1,0:T(8,128)(2,1)}, u32[]{:S(2)}, u32[]{:S(2)}) collective-permute-start(bf16[2,128,1408]{2,1,0:T(8,128)(2,1)S(1)} %bitcast.180), channel_id=1, source_target_pairs={{0,16},{16,0},{1,17},{17,1},{2,18},{18,2},{3,19},{19,3},{4,20},{20... | collective-permute-start | bytes 2162696 | tf_op jit(solution)/shard_map/gate_up_1_far/ppermute | solution.py:43
  214.2 33.1 %collective-permute-start.21 = (bf16[2,128,1408]{2,1,0:T(8,128)(2,1)S(1)}, bf16[2,128,1408]{2,1,0:T(8,128)(2,1)}, u32[]{:S(2)}, u32[]{:S(2)}) collective-permute-start(bf16[2,128,1408]{2,1,0:T(8,128)(2,1)S(1)} %bitcast.181), channel_id=1, source_target_pairs={{0,2},{2,0},{1,3},{3,1},{4,6},{6,4},{5,7},{7,5},{8,10},{10,8},{9,1... | collective-permute-start | bytes 2162696 | tf_op jit(solution)/shard_map/gate_up_1_near/ppermute | solution.py:43
  214.2 33.1 %collective-permute-start.19 = (bf16[2,128,1408]{2,1,0:T(8,128)(2,1)}, bf16[2,128,1408]{2,1,0:T(8,128)(2,1)}, u32[]{:S(2)}, u32[]{:S(2)}) collective-permute-start(bf16[2,128,1408]{2,1,0:T(8,128)(2,1)} %copy-done.29), channel_id=1, source_target_pairs={{0,2},{2,0},{1,3},{3,1},{4,6},{6,4},{5,7},{7,5},{8,10},{10,8},{9,1... | collective-permute-start | bytes 2162696 | tf_op jit(solution)/shard_map/gate_up_0_corner/ppermute | solution.py:43
  246.1 18.3 %collective-permute-start.22 = (bf16[2,128,1408]{2,1,0:T(8,128)(2,1)}, bf16[2,128,1408]{2,1,0:T(8,128)(2,1)}, u32[]{:S(2)}, u32[]{:S(2)}) collective-permute-start(bf16[2,128,1408]{2,1,0:T(8,128)(2,1)} %collective-permute-done.20.refs_5_), channel_id=1, source_target_pairs={{0,2},{2,0},{1,3},{3,1},{4,6},{6,4},{5,7},{7,5},{8,10},{10,8},{9,1... | collective-permute-start | bytes 2162696 | tf_op jit(solution)/shard_map/gate_up_1_corner/ppermute | solution.py:43
  298.9 14.0 %collective-permute-start.25 = (bf16[2,128,1024]{2,1,0:T(8,128)(2,1)S(1)}, bf16[2,128,1024]{2,1,0:T(8,128)(2,1)S(1)}, u32[]{:S(2)}, u32[]{:S(2)}) collective-permute-start(bf16[2,128,1024]{2,1,0:T(8,128)(2,1)S(1)} %dynamic-slice_bitcast_fusion.8), channel_id=1, source_target_pairs={{0,4},{4,0},{1,5},{5,1},{2,6},{6,2},{3,7},{7,3},{8,12},{12,8},{9,1... | collective-permute-start | bytes 1572872 | tf_op jit(solution)/shard_map/sum_places_0/ppermute | solution.py:43
  299.1 14.1 %collective-permute-start.24 = (bf16[2,128,1024]{2,1,0:T(8,128)(2,1)S(1)}, bf16[2,128,1024]{2,1,0:T(8,128)(2,1)S(1)}, u32[]{:S(2)}, u32[]{:S(2)}) collective-permute-start(bf16[2,128,1024]{2,1,0:T(8,128)(2,1)S(1)} %dynamic-slice_bitcast_fusion.9), channel_id=1, source_target_pairs={{0,8},{8,0},{1,9},{9,1},{2,10},{10,2},{3,11},{11,3},{4,12},{12,4},... | collective-permute-start | bytes 1572872 | tf_op jit(solution)/shard_map/sum_places_0/ppermute | solution.py:43
  315.5 16.8 %collective-permute-start.28 = (bf16[2,128,1408]{2,1,0:T(8,128)(2,1)S(1)}, bf16[2,128,1408]{2,1,0:T(8,128)(2,1)S(1)}, u32[]{:S(2)}, u32[]{:S(2)}) collective-permute-start(bf16[2,128,1408]{2,1,0:T(8,128)(2,1)S(1)} %get-tuple-element.187), channel_id=1, source_target_pairs={{0,2},{2,0},{1,3},{3,1},{4,6},{6,4},{5,7},{7,5},{8,10},{10,8},{9,1... | collective-permute-start | bytes 2162696 | tf_op jit(solution)/shard_map/grad_gate_up_far_0/ppermute | solution.py:43
  334.3 164.4 %reduce-scatter.2.cloned.1.call-start = ((), (), s32[]{:S(2)}) async-start(), calls=%async_computation.10 | async-start | bytes 3604480 | tf_op jit(solution)/shard_map/reduce_scatter | solution.py:784
  346.3 34.9 %collective-permute-start.30 = (bf16[2,128,1408]{2,1,0:T(8,128)(2,1)S(1)}, bf16[2,128,1408]{2,1,0:T(8,128)(2,1)S(1)}, u32[]{:S(2)}, u32[]{:S(2)}) collective-permute-start(bf16[2,128,1408]{2,1,0:T(8,128)(2,1)S(1)} %add_convert_fusion.5), channel_id=1, source_target_pairs={{0,16},{16,0},{1,17},{17,1},{2,18},{18,2},{3,19},{19,3},{4,20},{20... | collective-permute-start | bytes 2162696 | tf_op jit(solution)/shard_map/grad_gate_up_0_relay/ppermute | solution.py:43
  346.6 35.5 %collective-permute-start.29 = (bf16[2,128,1408]{2,1,0:T(8,128)(2,1)S(1)}, bf16[2,128,1408]{2,1,0:T(8,128)(2,1)S(1)}, u32[]{:S(2)}, u32[]{:S(2)}) collective-permute-start(bf16[2,128,1408]{2,1,0:T(8,128)(2,1)S(1)} %copy-done.52), channel_id=1, source_target_pairs={{0,2},{2,0},{1,3},{3,1},{4,6},{6,4},{5,7},{7,5},{8,10},{10,8},{9,1... | collective-permute-start | bytes 2162696 | tf_op jit(solution)/shard_map/grad_gate_up_far_1/ppermute | solution.py:43
  382.1 28.6 %collective-permute-start.34 = (bf16[2,128,1408]{2,1,0:T(8,128)(2,1)}, bf16[2,128,1408]{2,1,0:T(8,128)(2,1)S(1)}, u32[]{:S(2)}, u32[]{:S(2)}) collective-permute-start(bf16[2,128,1408]{2,1,0:T(8,128)(2,1)} %get-tuple-element.208), channel_id=1, source_target_pairs={{0,2},{2,0},{1,3},{3,1},{4,6},{6,4},{5,7},{7,5},{8,10},{10,8},{9,1... | collective-permute-start | bytes 2162696 | tf_op jit(solution)/shard_map/grad_gate_up_near_0/ppermute | solution.py:43
  382.4 33.1 %collective-permute-start.35 = (bf16[2,128,1408]{2,1,0:T(8,128)(2,1)}, bf16[2,128,1408]{2,1,0:T(8,128)(2,1)S(1)}, u32[]{:S(2)}, u32[]{:S(2)}) collective-permute-start(bf16[2,128,1408]{2,1,0:T(8,128)(2,1)} %get-tuple-element.209), channel_id=1, source_target_pairs={{0,2},{2,0},{1,3},{3,1},{4,6},{6,4},{5,7},{7,5},{8,10},{10,8},{9,1... | collective-permute-start | bytes 2162696 | tf_op jit(solution)/shard_map/grad_gate_up_near_1/ppermute | solution.py:43
  384.3 32.4 %collective-permute-start.36 = (bf16[2,128,1408]{2,1,0:T(8,128)(2,1)S(1)}, bf16[2,128,1408]{2,1,0:T(8,128)(2,1)S(1)}, u32[]{:S(2)}, u32[]{:S(2)}) collective-permute-start(bf16[2,128,1408]{2,1,0:T(8,128)(2,1)S(1)} %add_convert_fusion.4), channel_id=1, source_target_pairs={{0,16},{16,0},{1,17},{17,1},{2,18},{18,2},{3,19},{19,3},{4,20},{20... | collective-permute-start | bytes 2162696 | tf_op jit(solution)/shard_map/grad_gate_up_1_relay/ppermute | solution.py:43
  386.6 24.0 %collective-permute-start.32 = (bf16[2,128,1024]{2,1,0:T(8,128)(2,1)S(1)}, bf16[2,128,1024]{2,1,0:T(8,128)(2,1)S(1)}, u32[]{:S(2)}, u32[]{:S(2)}) collective-permute-start(bf16[2,128,1024]{2,1,0:T(8,128)(2,1)S(1)} %get-tuple-element.293), channel_id=1, source_target_pairs={{0,8},{8,0},{1,9},{9,1},{2,10},{10,2},{3,11},{11,3},{4,12},{12,4},... | collective-permute-start | bytes 1572872 | tf_op jit(solution)/shard_map/sum_places_0/ppermute | solution.py:43
  389.1 21.6 %collective-permute-start.33 = (bf16[2,128,1024]{2,1,0:T(8,128)(2,1)S(1)}, bf16[2,128,1024]{2,1,0:T(8,128)(2,1)S(1)}, u32[]{:S(2)}, u32[]{:S(2)}) collective-permute-start(bf16[2,128,1024]{2,1,0:T(8,128)(2,1)S(1)} %get-tuple-element.291), channel_id=1, source_target_pairs={{0,4},{4,0},{1,5},{5,1},{2,6},{6,2},{3,7},{7,3},{8,12},{12,8},{9,1... | collective-permute-start | bytes 1572872 | tf_op jit(solution)/shard_map/sum_places_0/ppermute | solution.py:43
  425.5 13.3 %collective-permute-start.39 = (bf16[128,1024]{1,0:T(8,128)(2,1)S(1)}, bf16[128,1024]{1,0:T(8,128)(2,1)S(1)}, u32[]{:S(2)}, u32[]{:S(2)}) collective-permute-start(bf16[128,1024]{1,0:T(8,128)(2,1)S(1)} %get-tuple-element.299), channel_id=1, source_target_pairs={{0,8},{8,0},{1,9},{9,1},{2,10},{10,2},{3,11},{11,3},{4,12},{12,4},... | collective-permute-start | bytes 786440 | tf_op jit(solution)/shard_map/sum_places_1/ppermute | solution.py:43
  439.7 13.2 %collective-permute-start.41 = (bf16[2,128,1024]{2,1,0:T(8,128)(2,1)}, bf16[2,128,1024]{2,1,0:T(8,128)(2,1)S(1)}, u32[]{:S(2)}, u32[]{:S(2)}) collective-permute-start(bf16[2,128,1024]{2,1,0:T(8,128)(2,1)} %dynamic-slice_bitcast_fusion.2), channel_id=1, source_target_pairs={{0,4},{4,0},{1,5},{5,1},{2,6},{6,2},{3,7},{7,3},{8,12},{12,8},{9,1... | collective-permute-start | bytes 1572872 | tf_op jit(solution)/shard_map/sum_places_0/ppermute | solution.py:43
  441.6 22.6 %collective-permute-start.40 = (bf16[2,128,1024]{2,1,0:T(8,128)(2,1)}, bf16[2,128,1024]{2,1,0:T(8,128)(2,1)}, u32[]{:S(2)}, u32[]{:S(2)}) collective-permute-start(bf16[2,128,1024]{2,1,0:T(8,128)(2,1)} %dynamic-slice_bitcast_fusion.3), channel_id=1, source_target_pairs={{0,8},{8,0},{1,9},{9,1},{2,10},{10,2},{3,11},{11,3},{4,12},{12,4},... | collective-permute-start | bytes 1572872 | tf_op jit(solution)/shard_map/sum_places_0/ppermute | solution.py:43
  443.2 22.4 %collective-permute-start.42 = (bf16[4,128,384]{2,1,0:T(8,128)(2,1)}, bf16[4,128,384]{2,1,0:T(8,128)(2,1)S(1)}, u32[]{:S(2)}, u32[]{:S(2)}) collective-permute-start(bf16[4,128,384]{2,1,0:T(8,128)(2,1)} %get-tuple-element.217), channel_id=1, source_target_pairs={{0,2},{2,0},{1,3},{3,1},{4,6},{6,4},{5,7},{7,5},{8,10},{10,8},{9,1... | collective-permute-start | bytes 1179656 | tf_op jit(solution)/shard_map/grad_attn_far/ppermute | solution.py:43
  466.9 12.2 %collective-permute-start.44 = (bf16[128,1024]{1,0:T(8,128)(2,1)S(1)}, bf16[128,1024]{1,0:T(8,128)(2,1)S(1)}, u32[]{:S(2)}, u32[]{:S(2)}) collective-permute-start(bf16[128,1024]{1,0:T(8,128)(2,1)S(1)} %dynamic-slice_bitcast_fusion.12), channel_id=1, source_target_pairs={{0,8},{8,0},{1,9},{9,1},{2,10},{10,2},{3,11},{11,3},{4,12},{12,4},... | collective-permute-start | bytes 786440 | tf_op jit(solution)/shard_map/sum_places_1/ppermute | solution.py:43
  466.9 14.4 %collective-permute-start.45 = (bf16[64,2048]{1,0:T(8,128)(2,1)S(1)}, bf16[64,2048]{1,0:T(8,128)(2,1)S(1)}, u32[]{:S(2)}, u32[]{:S(2)}) collective-permute-start(bf16[64,2048]{1,0:T(8,128)(2,1)S(1)} %get-tuple-element.247), channel_id=1, source_target_pairs={{0,2},{2,0},{1,3},{3,1},{4,6},{6,4},{5,7},{7,5},{8,10},{10,8},{9,1... | collective-permute-start | bytes 786440 | tf_op jit(solution)/shard_map/grad_out_far/ppermute | solution.py:43
  467.0 36.9 %collective-permute-start.50 = (bf16[64,2048]{1,0:T(8,128)(2,1)S(1)}, bf16[64,2048]{1,0:T(8,128)(2,1)S(1)}, u32[]{:S(2)}, u32[]{:S(2)}) collective-permute-start(bf16[64,2048]{1,0:T(8,128)(2,1)S(1)} %get-tuple-element.267), channel_id=1, source_target_pairs={{0,2},{2,0},{1,3},{3,1},{4,6},{6,4},{5,7},{7,5},{8,10},{10,8},{9,1... | collective-permute-start | bytes 786440 | tf_op jit(solution)/shard_map/grad_out_near/ppermute | solution.py:43
  469.9 47.4 %collective-permute-start.49 = (bf16[4,128,384]{2,1,0:T(8,128)(2,1)}, bf16[4,128,384]{2,1,0:T(8,128)(2,1)}, u32[]{:S(2)}, u32[]{:S(2)}) collective-permute-start(bf16[4,128,384]{2,1,0:T(8,128)(2,1)} %add_convert_fusion.8), channel_id=1, source_target_pairs={{0,16},{16,0},{1,17},{17,1},{2,18},{18,2},{3,19},{19,3},{4,20},{20... | collective-permute-start | bytes 1179656 | tf_op jit(solution)/shard_map/grad_attn_relay/ppermute | solution.py:43
  482.6 41.6 %all-to-all-start.2 = ((bf16[8,64,1408]{2,1,0:T(8,128)(2,1)}), bf16[8,64,1408]{2,1,0:T(8,128)(2,1)S(1)}, u32[]{:S(2)}, u32[]{:S(2)}) async-start(bf16[8,64,1408]{2,1,0:T(8,128)(2,1)} %bitcast.195), calls=%async_computation.3 | async-start | bytes 2883584 | tf_op jit(solution)/shard_map/all_to_all | solution.py:620
  487.3 21.6 %collective-permute-start.51 = (bf16[64,2048]{1,0:T(8,128)(2,1)}, bf16[64,2048]{1,0:T(8,128)(2,1)S(1)}, u32[]{:S(2)}, u32[]{:S(2)}) collective-permute-start(bf16[64,2048]{1,0:T(8,128)(2,1)} %add_convert_fusion.9), channel_id=1, source_target_pairs={{0,16},{16,0},{1,17},{17,1},{2,18},{18,2},{3,19},{19,3},{4,20},{20... | collective-permute-start | bytes 786440 | tf_op jit(solution)/shard_map/grad_out_relay/ppermute | solution.py:43
  489.6 27.6 %collective-permute-start.48 = (bf16[4,128,384]{2,1,0:T(8,128)(2,1)}, bf16[4,128,384]{2,1,0:T(8,128)(2,1)}, u32[]{:S(2)}, u32[]{:S(2)}) collective-permute-start(bf16[4,128,384]{2,1,0:T(8,128)(2,1)} %copy-done.53), channel_id=1, source_target_pairs={{0,2},{2,0},{1,3},{3,1},{4,6},{6,4},{5,7},{7,5},{8,10},{10,8},{9,1... | collective-permute-start | bytes 1179656 | tf_op jit(solution)/shard_map/grad_attn_near/ppermute | solution.py:43
  510.8 31.5 %collective-permute-start.47 = (bf16[64,4096]{1,0:T(8,128)(2,1)}, bf16[64,4096]{1,0:T(8,128)(2,1)}, u32[]{:S(2)}, u32[]{:S(2)}) collective-permute-start(bf16[64,4096]{1,0:T(8,128)(2,1)} %get-tuple-element.289), channel_id=1, source_target_pairs={{0,2},{1,18},{2,0},{3,16},{16,3},{17,19},{18,1},{19,17},{4,6},{5,2... | collective-permute-start | bytes 1572872 | tf_op jit(solution)/shard_map/rows_home/ppermute | solution.py:564
  511.1 31.2 %collective-permute-start.46 = (bf16[64,4096]{1,0:T(8,128)(2,1)}, bf16[64,4096]{1,0:T(8,128)(2,1)}, u32[]{:S(2)}, u32[]{:S(2)}) collective-permute-start(bf16[64,4096]{1,0:T(8,128)(2,1)} %get-tuple-element.290), channel_id=1, source_target_pairs={{0,0},{1,16},{2,2},{3,18},{16,1},{17,17},{18,3},{19,19},{4,4},{5,2... | collective-permute-start | bytes 1572872 | tf_op jit(solution)/shard_map/rows_home/ppermute | solution.py:564
  526.2 21.8 %all-to-all-start.3 = ((bf16[8,64,384]{2,1,0:T(8,128)(2,1)}), bf16[8,64,384]{2,1,0:T(8,128)(2,1)S(1)}, u32[]{:S(2)}, u32[]{:S(2)}) async-start(bf16[8,64,384]{2,1,0:T(8,128)(2,1)} %bitcast.186), calls=%async_computation.4 | async-start | bytes 786432 | tf_op jit(solution)/shard_map/all_to_all | solution.py:620
  (124 other events, 828.9 us)
Sparse Core Ops, SparseCore 0:
  17.6 54.1 all-gather.5
  75.6 71.3 all-gather.11
  149.2 59.7 all-gather.9
  211.2 42.5 all-gather.7
  334.5 35.9 all-gather.13
  420.5 78.2 reduce-scatter.1

commit v4 on v3

--- a/solution.py
+++ b/solution.py
@@ -776,15 +776,17 @@
     grad_down = dot(act, g, TN).astype(BF16)
     act, grad_down = tie((act, grad_down))
     final = layout.scatter_cores(lambda core: dot(part(act, core), down_own))
-    branch_team, grad_down, gu_far[1], gu_relay[0], gu_near, *final = tie(
-        (branch_team, grad_down, gu_far[1], gu_relay[0], gu_near, *final)
+    final = layout.scatter_send(final, 0)
+    branch_team, grad_down, gu_far[1], gu_relay[0], gu_near, final = tie(
+        (branch_team, grad_down, gu_far[1], gu_relay[0], gu_near, final)
     )
     gu_relay.append(layout.relay_sum(gu_theirs[1], gu_far[1], "grad_gate_up_1"))
     gu_near = [swap(near, layout.low, f"grad_gate_up_near_{at}") for at, near in enumerate(gu_near)]
     grad_down = lax.psum_scatter(
         grad_down, (layout.high, layout.low), scatter_dimension=0, tiled=True
     ).astype(F32)
-    final = layout.scatter_send(final, 0)
+    for count in range(1, len(layout.mid)):
+        final = layout.scatter_send(layout.scatter_add(final), count)
     grad_attended = dot(branch_team, out_own, NT).astype(BF16)
     if padding:
         grad_attended = jnp.pad(grad_attended, ((0, 0), (0, padding)))
@@ -792,9 +794,6 @@
     gq, gkv = attend_backward(heads, q, grad_attended, k, v, kt, marks, lse, cos, sin)
     grad_qkv = jnp.concatenate([gq, gkv], axis=1)
     grad_qkv, final, gu_near, gu_relay[1] = tie((grad_qkv, final, gu_near, gu_relay[1]))
-    for count in range(1, len(layout.mid)):
-        final = layout.scatter_send(layout.scatter_add(final), count)
-
     w_attn_own = w_attn.reshape(width, -1)[:, : grad_qkv.shape[1]]
 
     def attn_terms(sent):

time: 564 us -> 575 us (1.020)
  starting transfers between devices: 96.5 us -> 109 us
    all_to_all x4, waiting for transfers between devices: 16.2 us -> 9.08 us  [exchange(): return lax.all_to_all(array, self.mid + ('core',), 0, 0, tiled=True)]
    ppermute x44, starting transfers between devices: 50.6 us -> 57.3 us  [swap(): return lax.ppermute(array, axis, SWAP)]
    unnamed x219 -> x215, local copies, waits for them, and re-layouts: 31 us -> 33.3 us
  transfers between devices with their start and end apart: 63 -> 63, of which waited for: 32 -> 31; matrix products, arithmetic and copies ran while one was open for 12% -> 11% of each run, Pallas kernels for 11% -> 11%
where the time goes in v4:
time: 575 us; the launch traced here: 569 us
  waiting for transfers between devices  255 us (44%)
  starting transfers between devices  109 us (19%)
  Pallas kernels  74.1 us (13%)
  local copies, waits for them, and re-layouts  45.9 us (8%)
  other arithmetic  37.6 us (7%)
  matrix products  32.1 us (6%)
  between operations  16 us (3%)
    ppermute x44, waiting for transfers between devices, swap(): return lax.ppermute(array, axis, SWAP)  225 us
    ppermute x44, starting transfers between devices, swap(): return lax.ppermute(array, axis, SWAP)  57.3 us
    all_to_all x4, starting transfers between devices, exchange(): return lax.all_to_all(array, self.mid + ('core',), 0, 0, tiled=True)  34.5 us
    unnamed x215, local copies, waits for them, and re-layouts  33.3 us
    dot_general x10, matrix products, dot(): return lax.dot_general(left, right, dims, preferred_element_type=F32)  32.1 us
    pallas_call x1, Pallas kernels, attend_backward(): pl.pallas_call(functools.partial(backward_kernel, heads), grid=(rows // b...  18.7 us
    pallas_call x3, Pallas kernels, outer_rows(): pl.pallas_call(functools.partial(rows_kernel, sides, chunks), grid_spec=p...  14.6 us
    pallas_call x1, Pallas kernels, feed_forward(): pl.pallas_call(feed_kernel, grid=(rows // block,), in_specs=[pl.BlockSpec...  14.2 us
  transfers between devices with their start and end apart: 63, of which 31 were waited for; matrix products, arithmetic and copies ran while one was open for 11% of the time, Pallas kernels for 11%

profile of v4, /device:TPU:0, one launch (start us, length us, event | category | flops | bytes accessed | tf_op | source)
XLA Modules:
  0.0 568.8 jit_solution(10355306772660070247)
XLA Ops:
  9.1 3.0 collective-permute-start.1
  12.1 4.3 collective-permute-done.1
  19.8 9.7 %collective-permute-start.2 = (bf16[64,2688]{1,0:T(8,128)(2,1)S(1)}, bf16[64,2688]{1,0:T(8,128)(2,1)S(1)}, u32[]{:S(2)}, u32[]{:S(2)}) collective-permute-start(bf16[64,2688]{1,0:T(8,128)(2,1)S(1)} %fusion.21.own), channel_id=1, source_target_pairs={{0,16},{16,0},{1,17},{17,1},{2,18},{18,2},{3,19},{19,3},{4,20},{20... | collective-permute-start | bytes 1032200 | tf_op jit(solution)/shard_map/raw_far/ppermute | solution.py:43
  35.1 8.7 %collective-permute-done.2.far = bf16[64,2688]{1,0:T(8,128)(2,1)S(1)} collective-permute-done((bf16[64,2688]{1,0:T(8,128)(2,1)S(1)}, bf16[64,2688]{1,0:T(8,128)(2,1)S(1)}, u32[]{:S(2)}, u32[]{:S(2)}) %collective-permute-start.2) | collective-permute-done | bytes 344096 | tf_op jit(solution)/shard_map/raw_far/ppermute | solution.py:43
  50.1 3.1 collective-permute-done.5.corner
  55.4 5.7 %collective-permute-done.8 = bf16[64,2048]{1,0:T(8,128)(2,1)S(1)} collective-permute-done((bf16[64,2048]{1,0:T(8,128)(2,1)S(1)}, bf16[64,2048]{1,0:T(8,128)(2,1)S(1)}, u32[]{:S(2)}, u32[]{:S(2)}) %collective-permute-start.8) | collective-permute-done | bytes 262176 | tf_op jit(solution)/shard_map/cotangent/ppermute | solution.py:564
  61.8 11.1 %all-to-all-start = ((bf16[8,272,384]{2,1,0:T(8,128)(2,1)}), bf16[8,272,384]{2,1,0:T(8,128)(2,1)S(1)}, u32[]{:S(2)}, u32[]{:S(2)}) async-start(bf16[8,272,384]{2,1,0:T(8,128)(2,1)} %copy-done.4), calls=%async_computation | async-start | bytes 3342336 | tf_op jit(solution)/shard_map/all_to_all | solution.py:620
  76.2 6.3 %collective-permute-done.10 = bf16[64,2048]{1,0:T(8,128)(2,1)S(1)} collective-permute-done((bf16[64,2048]{1,0:T(8,128)(2,1)S(1)}, bf16[64,2048]{1,0:T(8,128)(2,1)S(1)}, u32[]{:S(2)}, u32[]{:S(2)}) %collective-permute-start.10) | collective-permute-done | bytes 262176 | tf_op jit(solution)/shard_map/out_near/ppermute | solution.py:43
  83.1 22.2 %collective-permute-done.9 = bf16[64,2048]{1,0:T(8,128)(2,1)} collective-permute-done((bf16[64,2048]{1,0:T(8,128)(2,1)S(1)}, bf16[64,2048]{1,0:T(8,128)(2,1)}, u32[]{:S(2)}, u32[]{:S(2)}) %collective-permute-start.9) | collective-permute-done | bytes 262176 | tf_op jit(solution)/shard_map/out_far/ppermute | solution.py:43
  106.9 4.3 all-to-all-start.1
  118.4 5.4 project.1
  127.1 12.2 %attend_forward.1 = (bf16[1024,256]{1,0:T(8,128)(2,1)S(1)}, f32[8,1024]{1,0:T(8,128)S(1)}) custom-call(bf16[1024,256]{1,0:T(8,128)(2,1)S(1)} %get-tuple-element.154.q_ref, bf16[1024,256]{1,0:T(8,128)(2,1)S(1)} %get-tuple-element.155.k_ref, bf16[256,1024]{1,0:T(8,128)(2,1)S(1)} %get-tuple-element.156.vt_ref, f32[1024,128]{1,0:T(8,128)S(1)} %pad.9.marks_ref.marks_all_ref, ...), custom_call_target="tpu_custom_call" | custom-call | flops 1 | bytes 1 | tf_op jit(solution)/shard_map/attend_forward/pallas_call | solution.py:212
  140.2 4.5 all-to-all-done.1
  148.1 4.5 collective-permute-done.12
  160.7 14.8 %collective-permute-done.15 = bf16[2,128,1024]{2,1,0:T(8,128)(2,1)S(1)} collective-permute-done((bf16[2,128,1024]{2,1,0:T(8,128)(2,1)S(1)}, bf16[2,128,1024]{2,1,0:T(8,128)(2,1)S(1)}, u32[]{:S(2)}, u32[]{:S(2)}) %collective-permute-start.15) | collective-permute-done | bytes 524320 | tf_op jit(solution)/shard_map/sum_places_0/ppermute | solution.py:43
  175.8 5.3 collective-permute-start.16
  181.0 17.1 %collective-permute-done.13 = bf16[2,128,1024]{2,1,0:T(8,128)(2,1)S(1)} collective-permute-done((bf16[2,128,1024]{2,1,0:T(8,128)(2,1)S(1)}, bf16[2,128,1024]{2,1,0:T(8,128)(2,1)S(1)}, u32[]{:S(2)}, u32[]{:S(2)}) %collective-permute-start.13) | collective-permute-done | bytes 524320 | tf_op jit(solution)/shard_map/sum_places_0/ppermute | solution.py:43
  198.7 9.1 %collective-permute-done.16 = bf16[128,1024]{1,0:T(8,128)(2,1)S(1)} collective-permute-done((bf16[128,1024]{1,0:T(8,128)(2,1)S(1)}, bf16[128,1024]{1,0:T(8,128)(2,1)S(1)}, u32[]{:S(2)}, u32[]{:S(2)}) %collective-permute-start.16) | collective-permute-done | bytes 262176 | tf_op jit(solution)/shard_map/sum_places_1/ppermute | solution.py:43
  216.2 29.9 %collective-permute-done.20.refs_5_ = bf16[2,128,1408]{2,1,0:T(8,128)(2,1)} collective-permute-done((bf16[2,128,1408]{2,1,0:T(8,128)(2,1)S(1)}, bf16[2,128,1408]{2,1,0:T(8,128)(2,1)}, u32[]{:S(2)}, u32[]{:S(2)}) %collective-permute-start.20) | collective-permute-done | bytes 720928 | tf_op jit(solution)/shard_map/gate_up_1_far/ppermute | solution.py:43
  247.3 17.1 %collective-permute-done.22.refs_7_ = bf16[2,128,1408]{2,1,0:T(8,128)(2,1)} collective-permute-done((bf16[2,128,1408]{2,1,0:T(8,128)(2,1)}, bf16[2,128,1408]{2,1,0:T(8,128)(2,1)}, u32[]{:S(2)}, u32[]{:S(2)}) %collective-permute-start.22) | collective-permute-done | bytes 720928 | tf_op jit(solution)/shard_map/gate_up_1_corner/ppermute | solution.py:43
  272.8 14.2 %feed_forward.1 = (bf16[1024,704]{1,0:T(8,128)(2,1)S(1)}, bf16[1024,1408]{1,0:T(8,128)(2,1)S(1)}, bf16[2,4,2,128,1408]{4,3,2,1,0:T(8,128)(2,1)S(1)}) custom-call(s32[3]{0:T(128)S(1)} %pad_add_fusion.bits_ref, bf16[1024,2048]{1,0:T(8,128)(2,1)S(1)} %copy-done.2, bf16[1024,2048]{1,0:T(8,128)(2,1)S(1)} %copy-done.8, bf16[704,2048]{1,0:T(8,128)(2,1)S(1)} %copy-done.14, ...), custom_call_target="tpu_custom_call" | custom-call | flops 1 | bytes 1 | tf_op jit(solution)/shard_map/feed_forward/pallas_call | solution.py:338
  287.0 3.7 convolution_convert_fusion.4
  290.8 4.1 collective-permute-done.23
  295.0 3.7 add_convert_fusion.2
  301.0 4.6 outer_rows.3
  305.6 7.3 %collective-permute-done.25 = bf16[2,128,1024]{2,1,0:T(8,128)(2,1)S(1)} collective-permute-done((bf16[2,128,1024]{2,1,0:T(8,128)(2,1)S(1)}, bf16[2,128,1024]{2,1,0:T(8,128)(2,1)S(1)}, u32[]{:S(2)}, u32[]{:S(2)}) %collective-permute-start.25) | collective-permute-done | bytes 524320 | tf_op jit(solution)/shard_map/sum_places_0/ppermute | solution.py:43
  315.8 5.7 %outer_rows.4 = (bf16[2,128,1408]{2,1,0:T(8,128)(2,1)S(1)}, bf16[2,128,1408]{2,1,0:T(8,128)(2,1)S(1)}, bf16[2,128,1408]{2,1,0:T(8,128)(2,1)}, bf16[2,128,1408]{2,1,0:T(8,128)(2,1)}) custom-call(s32[3]{0:T(128)S(1)} %pad_add_fusion.bits_ref, bf16[1024,2048]{1,0:T(8,128)(2,1)S(1)} %copy-done.3, bf16[1024,1408]{1,0:T(8,128)(2,1)S(1)} %get-tuple-element.184.right_ref), custom_call_target="tpu_custom_call" | custom-call | flops 1 | bytes 1 | tf_op jit(solution)/shard_map/outer_rows/pallas_call | solution.py:388
  322.7 9.6 %collective-permute-done.28 = bf16[2,128,1408]{2,1,0:T(8,128)(2,1)S(1)} collective-permute-done((bf16[2,128,1408]{2,1,0:T(8,128)(2,1)S(1)}, bf16[2,128,1408]{2,1,0:T(8,128)(2,1)S(1)}, u32[]{:S(2)}, u32[]{:S(2)}) %collective-permute-start.28) | collective-permute-done | bytes 720928 | tf_op jit(solution)/shard_map/grad_gate_up_far_0/ppermute | solution.py:43
  334.6 7.4 %convolution_convert_fusion = bf16[704,2048]{1,0:T(8,128)(2,1)} fusion(bf16[1024,704]{1,0:T(8,128)(2,1)} %copy-done.49, bf16[1024,2048]{1,0:T(8,128)(2,1)} %all-gather.10.cloned.1.call-done.g_ref), kind=kOutput, calls=%fused_computation.4 | convolution fusion | flops 2954231808 | bytes 8519680 | tf_op jit(solution)/shard_map/dot_general | solution.py:30
  342.0 4.0 convolution_convert_fusion.3
  356.3 25.1 %collective-permute-done.30.refs_2_ = bf16[2,128,1408]{2,1,0:T(8,128)(2,1)S(1)} collective-permute-done((bf16[2,128,1408]{2,1,0:T(8,128)(2,1)S(1)}, bf16[2,128,1408]{2,1,0:T(8,128)(2,1)S(1)}, u32[]{:S(2)}, u32[]{:S(2)}) %collective-permute-start.30) | collective-permute-done | bytes 720928 | tf_op jit(solution)/shard_map/grad_gate_up_0_relay/ppermute | solution.py:43
  382.3 3.6 collective-permute-done.32
  398.3 18.7 %attend_backward.1 = (bf16[1024,256]{1,0:T(8,128)(2,1)S(1)}, bf16[1024,128]{1,0:T(8,128)(2,1)S(1)}) custom-call(bf16[1024,256]{1,0:T(8,128)(2,1)S(1)} %copy-done.23, bf16[1024,256]{1,0:T(8,128)(2,1)S(1)} %convolution_convert_fusion.5.g_ref, bf16[1024,256]{1,0:T(8,128)(2,1)S(1)} %copy-done.25, bf16[1024,256]{1,0:T(8,128)(2,1)S(1)} %copy-done.44, ...), custom_call_target="tpu_custom_call" | custom-call | flops 1 | bytes 1 | tf_op jit(solution)/shard_map/attend_backward/pallas_call | solution.py:281
  418.1 5.2 collective-permute-done.37.refs_4_
  426.3 2.7 convolution_convert_fusion.2
  432.4 4.3 outer_rows.5
  436.8 3.2 add_convert_fusion
  447.0 3.0 outer_quarters.1
  450.0 5.2 collective-permute-done.41
  455.4 15.3 %collective-permute-done.40 = bf16[2,128,1024]{2,1,0:T(8,128)(2,1)} collective-permute-done((bf16[2,128,1024]{2,1,0:T(8,128)(2,1)}, bf16[2,128,1024]{2,1,0:T(8,128)(2,1)}, u32[]{:S(2)}, u32[]{:S(2)}) %collective-permute-start.40) | collective-permute-done | bytes 524320 | tf_op jit(solution)/shard_map/sum_places_0/ppermute | solution.py:43
  476.7 3.3 collective-permute-start.49
  482.4 3.5 collective-permute-done.44
  489.4 4.1 all-to-all-start.2
  494.2 3.5 collective-permute-start.51
  499.4 10.0 %reduce-scatter.2.cloned.1.call-done = bf16[176,2048]{1,0:T(8,128)(2,1)} async-done(((bf16[704,2048]{1,0:T(8,128)(2,1)}), bf16[176,2048]{1,0:T(8,128)(2,1)}) %reduce-scatter.2.cloned.1.call-update) | async-done | bytes 720912 | tf_op jit(solution)/shard_map/reduce_scatter | solution.py:785
  514.6 6.9 %collective-permute-done.51.refs_2_ = bf16[64,2048]{1,0:T(8,128)(2,1)S(1)} collective-permute-done((bf16[64,2048]{1,0:T(8,128)(2,1)}, bf16[64,2048]{1,0:T(8,128)(2,1)S(1)}, u32[]{:S(2)}, u32[]{:S(2)}) %collective-permute-start.51) | collective-permute-done | bytes 262176 | tf_op jit(solution)/shard_map/grad_out_relay/ppermute | solution.py:43
  524.9 5.4 collective-permute-start.46
  533.6 15.0 %all-to-all-start.3 = ((bf16[8,64,384]{2,1,0:T(8,128)(2,1)}), bf16[8,64,384]{2,1,0:T(8,128)(2,1)S(1)}, u32[]{:S(2)}, u32[]{:S(2)}) async-start(bf16[8,64,384]{2,1,0:T(8,128)(2,1)} %bitcast.186), calls=%async_computation.4 | async-start | bytes 786432 | tf_op jit(solution)/shard_map/all_to_all | solution.py:620
  (431 shorter events, 152.1 us)
Async XLA Ops:
  7.3 109.0 %all-gather.6.cloned.1.call-start = ((), (), s32[]{:S(2)}) async-start(), calls=%async_computation.5 | async-start | bytes 4718592 | tf_op jit(solution)/shard_map/all_gather | solution.py:584
  17.7 17.4 %collective-permute-start.3 = (bf16[64,2688]{1,0:T(8,128)(2,1)S(1)}, bf16[64,2688]{1,0:T(8,128)(2,1)S(1)}, u32[]{:S(2)}, u32[]{:S(2)}) collective-permute-start(bf16[64,2688]{1,0:T(8,128)(2,1)S(1)} %fusion.21.own), channel_id=1, source_target_pairs={{0,2},{2,0},{1,3},{3,1},{4,6},{6,4},{5,7},{7,5},{8,10},{10,8},{9,1... | collective-permute-start | bytes 1032200 | tf_op jit(solution)/shard_map/raw_near/ppermute | solution.py:43
  19.8 24.0 %collective-permute-start.2 = (bf16[64,2688]{1,0:T(8,128)(2,1)S(1)}, bf16[64,2688]{1,0:T(8,128)(2,1)S(1)}, u32[]{:S(2)}, u32[]{:S(2)}) collective-permute-start(bf16[64,2688]{1,0:T(8,128)(2,1)S(1)} %fusion.21.own), channel_id=1, source_target_pairs={{0,16},{16,0},{1,17},{17,1},{2,18},{18,2},{3,19},{19,3},{4,20},{20... | collective-permute-start | bytes 1032200 | tf_op jit(solution)/shard_map/raw_far/ppermute | solution.py:43
  46.0 15.1 %collective-permute-start.8 = (bf16[64,2048]{1,0:T(8,128)(2,1)S(1)}, bf16[64,2048]{1,0:T(8,128)(2,1)S(1)}, u32[]{:S(2)}, u32[]{:S(2)}) collective-permute-start(bf16[64,2048]{1,0:T(8,128)(2,1)S(1)} %get-tuple-element.313), channel_id=1, source_target_pairs={{0,2},{1,18},{2,0},{3,16},{16,3},{17,19},{18,1},{19,17},{4,6},{5,2... | collective-permute-start | bytes 786440 | tf_op jit(solution)/shard_map/cotangent/ppermute | solution.py:564
  47.7 14.1 %collective-permute-start.7 = (bf16[64,2048]{1,0:T(8,128)(2,1)S(1)}, bf16[64,2048]{1,0:T(8,128)(2,1)}, u32[]{:S(2)}, u32[]{:S(2)}) collective-permute-start(bf16[64,2048]{1,0:T(8,128)(2,1)S(1)} %get-tuple-element.314), channel_id=1, source_target_pairs={{0,0},{1,16},{2,2},{3,18},{16,1},{17,17},{18,3},{19,19},{4,4},{5,2... | collective-permute-start | bytes 786440 | tf_op jit(solution)/shard_map/cotangent/ppermute | solution.py:564
  61.8 45.1 %all-to-all-start = ((bf16[8,272,384]{2,1,0:T(8,128)(2,1)}), bf16[8,272,384]{2,1,0:T(8,128)(2,1)S(1)}, u32[]{:S(2)}, u32[]{:S(2)}) async-start(bf16[8,272,384]{2,1,0:T(8,128)(2,1)} %copy-done.4), calls=%async_computation | async-start | bytes 3342336 | tf_op jit(solution)/shard_map/all_to_all | solution.py:620
  72.9 173.2 %all-gather.12.cloned.1.call-start = ((), (), s32[]{:S(2)}) async-start(), calls=%async_computation.8 | async-start | bytes 3604480 | tf_op jit(solution)/shard_map/all_gather | solution.py:697
  74.3 31.1 %collective-permute-start.9 = (bf16[64,2048]{1,0:T(8,128)(2,1)S(1)}, bf16[64,2048]{1,0:T(8,128)(2,1)}, u32[]{:S(2)}, u32[]{:S(2)}) collective-permute-start(bf16[64,2048]{1,0:T(8,128)(2,1)S(1)} %broadcast_select_fusion.2), channel_id=1, source_target_pairs={{0,16},{16,0},{1,17},{17,1},{2,18},{18,2},{3,19},{19,3},{4,20},{20... | collective-permute-start | bytes 786440 | tf_op jit(solution)/shard_map/out_far/ppermute | solution.py:43
  106.9 37.8 %all-to-all-start.1 = ((bf16[8,64,1408]{2,1,0:T(8,128)(2,1)}), bf16[8,64,1408]{2,1,0:T(8,128)(2,1)}, u32[]{:S(2)}, u32[]{:S(2)}) async-start(bf16[8,64,1408]{2,1,0:T(8,128)(2,1)} %copy-done.7), calls=%async_computation.1 | async-start | bytes 2883584 | tf_op jit(solution)/shard_map/all_to_all | solution.py:620
  111.2 134.9 %all-gather.10.cloned.1.call-start = ((), (), s32[]{:S(2)}) async-start(), calls=%async_computation.7 | async-start | bytes 4718592 | tf_op jit(solution)/shard_map/all_gather | solution.py:584
  113.2 151.2 %all-gather.8.cloned.1.call-start = ((), (), s32[]{:S(2)}) async-start(), calls=%async_computation.6 | async-start | bytes 4718592 | tf_op jit(solution)/shard_map/all_gather | solution.py:584
  113.5 26.6 %collective-permute-start.11 = (bf16[64,2048]{1,0:T(8,128)(2,1)}, bf16[64,2048]{1,0:T(8,128)(2,1)}, u32[]{:S(2)}, u32[]{:S(2)}) collective-permute-start(bf16[64,2048]{1,0:T(8,128)(2,1)} %collective-permute-done.9), channel_id=1, source_target_pairs={{0,2},{2,0},{1,3},{3,1},{4,6},{6,4},{5,7},{7,5},{8,10},{10,8},{9,1... | collective-permute-start | bytes 786440 | tf_op jit(solution)/shard_map/out_corner/ppermute | solution.py:43
  155.2 20.4 %collective-permute-start.15 = (bf16[2,128,1024]{2,1,0:T(8,128)(2,1)S(1)}, bf16[2,128,1024]{2,1,0:T(8,128)(2,1)S(1)}, u32[]{:S(2)}, u32[]{:S(2)}) collective-permute-start(bf16[2,128,1024]{2,1,0:T(8,128)(2,1)S(1)} %dynamic-slice_bitcast_fusion.10), channel_id=1, source_target_pairs={{0,4},{4,0},{1,5},{5,1},{2,6},{6,2},{3,7},{7,3},{8,12},{12,8},{9,1... | collective-permute-start | bytes 1572872 | tf_op jit(solution)/shard_map/sum_places_0/ppermute | solution.py:43
  156.7 41.4 %collective-permute-start.13 = (bf16[2,128,1024]{2,1,0:T(8,128)(2,1)S(1)}, bf16[2,128,1024]{2,1,0:T(8,128)(2,1)S(1)}, u32[]{:S(2)}, u32[]{:S(2)}) collective-permute-start(bf16[2,128,1024]{2,1,0:T(8,128)(2,1)S(1)} %dynamic-slice_bitcast_fusion.11), channel_id=1, source_target_pairs={{0,8},{8,0},{1,9},{9,1},{2,10},{10,2},{3,11},{11,3},{4,12},{12,4},... | collective-permute-start | bytes 1572872 | tf_op jit(solution)/shard_map/sum_places_0/ppermute | solution.py:43
  159.4 48.7 %collective-permute-start.18 = (bf16[2,128,1408]{2,1,0:T(8,128)(2,1)S(1)}, bf16[2,128,1408]{2,1,0:T(8,128)(2,1)S(1)}, u32[]{:S(2)}, u32[]{:S(2)}) collective-permute-start(bf16[2,128,1408]{2,1,0:T(8,128)(2,1)S(1)} %bitcast.183), channel_id=1, source_target_pairs={{0,2},{2,0},{1,3},{3,1},{4,6},{6,4},{5,7},{7,5},{8,10},{10,8},{9,1... | collective-permute-start | bytes 2162696 | tf_op jit(solution)/shard_map/gate_up_0_near/ppermute | solution.py:43
  159.9 49.1 %collective-permute-start.17 = (bf16[2,128,1408]{2,1,0:T(8,128)(2,1)S(1)}, bf16[2,128,1408]{2,1,0:T(8,128)(2,1)S(1)}, u32[]{:S(2)}, u32[]{:S(2)}) collective-permute-start(bf16[2,128,1408]{2,1,0:T(8,128)(2,1)S(1)} %bitcast.184), channel_id=1, source_target_pairs={{0,16},{16,0},{1,17},{17,1},{2,18},{18,2},{3,19},{19,3},{4,20},{20... | collective-permute-start | bytes 2162696 | tf_op jit(solution)/shard_map/gate_up_0_far/ppermute | solution.py:43
  175.8 32.0 %collective-permute-start.16 = (bf16[128,1024]{1,0:T(8,128)(2,1)S(1)}, bf16[128,1024]{1,0:T(8,128)(2,1)S(1)}, u32[]{:S(2)}, u32[]{:S(2)}) collective-permute-start(bf16[128,1024]{1,0:T(8,128)(2,1)S(1)} %dynamic-slice_bitcast_fusion.20), channel_id=1, source_target_pairs={{0,8},{8,0},{1,9},{9,1},{2,10},{10,2},{3,11},{11,3},{4,12},{12,4},... | collective-permute-start | bytes 786440 | tf_op jit(solution)/shard_map/sum_places_1/ppermute | solution.py:43
  211.1 174.8 %all-gather.14.cloned.1.call-start = ((), (), s32[]{:S(2)}) async-start(), calls=%async_computation.9 | async-start | bytes 4718592 | tf_op jit(solution)/shard_map/all_gather | solution.py:584
  211.7 34.4 %collective-permute-start.20 = (bf16[2,128,1408]{2,1,0:T(8,128)(2,1)S(1)}, bf16[2,128,1408]{2,1,0:T(8,128)(2,1)}, u32[]{:S(2)}, u32[]{:S(2)}) collective-permute-start(bf16[2,128,1408]{2,1,0:T(8,128)(2,1)S(1)} %bitcast.180), channel_id=1, source_target_pairs={{0,16},{16,0},{1,17},{17,1},{2,18},{18,2},{3,19},{19,3},{4,20},{20... | collective-permute-start | bytes 2162696 | tf_op jit(solution)/shard_map/gate_up_1_far/ppermute | solution.py:43
  214.2 33.1 %collective-permute-start.21 = (bf16[2,128,1408]{2,1,0:T(8,128)(2,1)S(1)}, bf16[2,128,1408]{2,1,0:T(8,128)(2,1)}, u32[]{:S(2)}, u32[]{:S(2)}) collective-permute-start(bf16[2,128,1408]{2,1,0:T(8,128)(2,1)S(1)} %bitcast.181), channel_id=1, source_target_pairs={{0,2},{2,0},{1,3},{3,1},{4,6},{6,4},{5,7},{7,5},{8,10},{10,8},{9,1... | collective-permute-start | bytes 2162696 | tf_op jit(solution)/shard_map/gate_up_1_near/ppermute | solution.py:43
  214.2 33.1 %collective-permute-start.19 = (bf16[2,128,1408]{2,1,0:T(8,128)(2,1)}, bf16[2,128,1408]{2,1,0:T(8,128)(2,1)}, u32[]{:S(2)}, u32[]{:S(2)}) collective-permute-start(bf16[2,128,1408]{2,1,0:T(8,128)(2,1)} %copy-done.29), channel_id=1, source_target_pairs={{0,2},{2,0},{1,3},{3,1},{4,6},{6,4},{5,7},{7,5},{8,10},{10,8},{9,1... | collective-permute-start | bytes 2162696 | tf_op jit(solution)/shard_map/gate_up_0_corner/ppermute | solution.py:43
  246.1 18.3 %collective-permute-start.22 = (bf16[2,128,1408]{2,1,0:T(8,128)(2,1)}, bf16[2,128,1408]{2,1,0:T(8,128)(2,1)}, u32[]{:S(2)}, u32[]{:S(2)}) collective-permute-start(bf16[2,128,1408]{2,1,0:T(8,128)(2,1)} %collective-permute-done.20.refs_5_), channel_id=1, source_target_pairs={{0,2},{2,0},{1,3},{3,1},{4,6},{6,4},{5,7},{7,5},{8,10},{10,8},{9,1... | collective-permute-start | bytes 2162696 | tf_op jit(solution)/shard_map/gate_up_1_corner/ppermute | solution.py:43
  298.9 14.0 %collective-permute-start.25 = (bf16[2,128,1024]{2,1,0:T(8,128)(2,1)S(1)}, bf16[2,128,1024]{2,1,0:T(8,128)(2,1)S(1)}, u32[]{:S(2)}, u32[]{:S(2)}) collective-permute-start(bf16[2,128,1024]{2,1,0:T(8,128)(2,1)S(1)} %dynamic-slice_bitcast_fusion.8), channel_id=1, source_target_pairs={{0,4},{4,0},{1,5},{5,1},{2,6},{6,2},{3,7},{7,3},{8,12},{12,8},{9,1... | collective-permute-start | bytes 1572872 | tf_op jit(solution)/shard_map/sum_places_0/ppermute | solution.py:43
  299.1 14.1 %collective-permute-start.24 = (bf16[2,128,1024]{2,1,0:T(8,128)(2,1)S(1)}, bf16[2,128,1024]{2,1,0:T(8,128)(2,1)S(1)}, u32[]{:S(2)}, u32[]{:S(2)}) collective-permute-start(bf16[2,128,1024]{2,1,0:T(8,128)(2,1)S(1)} %dynamic-slice_bitcast_fusion.9), channel_id=1, source_target_pairs={{0,8},{8,0},{1,9},{9,1},{2,10},{10,2},{3,11},{11,3},{4,12},{12,4},... | collective-permute-start | bytes 1572872 | tf_op jit(solution)/shard_map/sum_places_0/ppermute | solution.py:43
  315.5 16.8 %collective-permute-start.28 = (bf16[2,128,1408]{2,1,0:T(8,128)(2,1)S(1)}, bf16[2,128,1408]{2,1,0:T(8,128)(2,1)S(1)}, u32[]{:S(2)}, u32[]{:S(2)}) collective-permute-start(bf16[2,128,1408]{2,1,0:T(8,128)(2,1)S(1)} %get-tuple-element.189), channel_id=1, source_target_pairs={{0,2},{2,0},{1,3},{3,1},{4,6},{6,4},{5,7},{7,5},{8,10},{10,8},{9,1... | collective-permute-start | bytes 2162696 | tf_op jit(solution)/shard_map/grad_gate_up_far_0/ppermute | solution.py:43
  334.4 175.0 %reduce-scatter.2.cloned.1.call-start = ((), (), s32[]{:S(2)}) async-start(), calls=%async_computation.10 | async-start | bytes 3604480 | tf_op jit(solution)/shard_map/reduce_scatter | solution.py:785
  346.3 35.0 %collective-permute-start.30 = (bf16[2,128,1408]{2,1,0:T(8,128)(2,1)S(1)}, bf16[2,128,1408]{2,1,0:T(8,128)(2,1)S(1)}, u32[]{:S(2)}, u32[]{:S(2)}) collective-permute-start(bf16[2,128,1408]{2,1,0:T(8,128)(2,1)S(1)} %add_convert_fusion.5), channel_id=1, source_target_pairs={{0,16},{16,0},{1,17},{17,1},{2,18},{18,2},{3,19},{19,3},{4,20},{20... | collective-permute-start | bytes 2162696 | tf_op jit(solution)/shard_map/grad_gate_up_0_relay/ppermute | solution.py:43
  346.6 35.7 %collective-permute-start.29 = (bf16[2,128,1408]{2,1,0:T(8,128)(2,1)S(1)}, bf16[2,128,1408]{2,1,0:T(8,128)(2,1)S(1)}, u32[]{:S(2)}, u32[]{:S(2)}) collective-permute-start(bf16[2,128,1408]{2,1,0:T(8,128)(2,1)S(1)} %copy-done.52), channel_id=1, source_target_pairs={{0,2},{2,0},{1,3},{3,1},{4,6},{6,4},{5,7},{7,5},{8,10},{10,8},{9,1... | collective-permute-start | bytes 2162696 | tf_op jit(solution)/shard_map/grad_gate_up_far_1/ppermute | solution.py:43
  353.5 28.7 %collective-permute-start.33 = (bf16[2,128,1024]{2,1,0:T(8,128)(2,1)S(1)}, bf16[2,128,1024]{2,1,0:T(8,128)(2,1)}, u32[]{:S(2)}, u32[]{:S(2)}) collective-permute-start(bf16[2,128,1024]{2,1,0:T(8,128)(2,1)S(1)} %get-tuple-element.295), channel_id=1, source_target_pairs={{0,4},{4,0},{1,5},{5,1},{2,6},{6,2},{3,7},{7,3},{8,12},{12,8},{9,1... | collective-permute-start | bytes 1572872 | tf_op jit(solution)/shard_map/sum_places_0/ppermute | solution.py:43
  354.8 31.1 %collective-permute-start.32 = (bf16[2,128,1024]{2,1,0:T(8,128)(2,1)S(1)}, bf16[2,128,1024]{2,1,0:T(8,128)(2,1)}, u32[]{:S(2)}, u32[]{:S(2)}) collective-permute-start(bf16[2,128,1024]{2,1,0:T(8,128)(2,1)S(1)} %get-tuple-element.297), channel_id=1, source_target_pairs={{0,8},{8,0},{1,9},{9,1},{2,10},{10,2},{3,11},{11,3},{4,12},{12,4},... | collective-permute-start | bytes 1572872 | tf_op jit(solution)/shard_map/sum_places_0/ppermute | solution.py:43
  388.2 28.9 %collective-permute-start.34 = (bf16[128,1024]{1,0:T(8,128)(2,1)S(1)}, bf16[128,1024]{1,0:T(8,128)(2,1)S(1)}, u32[]{:S(2)}, u32[]{:S(2)}) collective-permute-start(bf16[128,1024]{1,0:T(8,128)(2,1)S(1)} %get-tuple-element.305), channel_id=1, source_target_pairs={{0,4},{4,0},{1,5},{5,1},{2,6},{6,2},{3,7},{7,3},{8,12},{12,8},{9,1... | collective-permute-start | bytes 786440 | tf_op jit(solution)/shard_map/sum_places_1/ppermute | solution.py:43
  390.0 27.2 %collective-permute-start.36 = (bf16[2,128,1408]{2,1,0:T(8,128)(2,1)}, bf16[2,128,1408]{2,1,0:T(8,128)(2,1)S(1)}, u32[]{:S(2)}, u32[]{:S(2)}) collective-permute-start(bf16[2,128,1408]{2,1,0:T(8,128)(2,1)} %get-tuple-element.212), channel_id=1, source_target_pairs={{0,2},{2,0},{1,3},{3,1},{4,6},{6,4},{5,7},{7,5},{8,10},{10,8},{9,1... | collective-permute-start | bytes 2162696 | tf_op jit(solution)/shard_map/grad_gate_up_near_0/ppermute | solution.py:43
  391.5 31.9 %collective-permute-start.37 = (bf16[2,128,1408]{2,1,0:T(8,128)(2,1)}, bf16[2,128,1408]{2,1,0:T(8,128)(2,1)S(1)}, u32[]{:S(2)}, u32[]{:S(2)}) collective-permute-start(bf16[2,128,1408]{2,1,0:T(8,128)(2,1)} %get-tuple-element.213), channel_id=1, source_target_pairs={{0,2},{2,0},{1,3},{3,1},{4,6},{6,4},{5,7},{7,5},{8,10},{10,8},{9,1... | collective-permute-start | bytes 2162696 | tf_op jit(solution)/shard_map/grad_gate_up_near_1/ppermute | solution.py:43
  392.2 33.3 %collective-permute-start.38 = (bf16[2,128,1408]{2,1,0:T(8,128)(2,1)S(1)}, bf16[2,128,1408]{2,1,0:T(8,128)(2,1)S(1)}, u32[]{:S(2)}, u32[]{:S(2)}) collective-permute-start(bf16[2,128,1408]{2,1,0:T(8,128)(2,1)S(1)} %add_convert_fusion.4), channel_id=1, source_target_pairs={{0,16},{16,0},{1,17},{17,1},{2,18},{18,2},{3,19},{19,3},{4,20},{20... | collective-permute-start | bytes 2162696 | tf_op jit(solution)/shard_map/grad_gate_up_1_relay/ppermute | solution.py:43
  396.7 20.5 %collective-permute-start.35 = (bf16[128,1024]{1,0:T(8,128)(2,1)S(1)}, bf16[128,1024]{1,0:T(8,128)(2,1)S(1)}, u32[]{:S(2)}, u32[]{:S(2)}) collective-permute-start(bf16[128,1024]{1,0:T(8,128)(2,1)S(1)} %get-tuple-element.303), channel_id=1, source_target_pairs={{0,8},{8,0},{1,9},{9,1},{2,10},{10,2},{3,11},{11,3},{4,12},{12,4},... | collective-permute-start | bytes 786440 | tf_op jit(solution)/shard_map/sum_places_1/ppermute | solution.py:43
  441.1 14.1 %collective-permute-start.41 = (bf16[2,128,1024]{2,1,0:T(8,128)(2,1)}, bf16[2,128,1024]{2,1,0:T(8,128)(2,1)S(1)}, u32[]{:S(2)}, u32[]{:S(2)}) collective-permute-start(bf16[2,128,1024]{2,1,0:T(8,128)(2,1)} %dynamic-slice_bitcast_fusion.2), channel_id=1, source_target_pairs={{0,4},{4,0},{1,5},{5,1},{2,6},{6,2},{3,7},{7,3},{8,12},{12,8},{9,1... | collective-permute-start | bytes 1572872 | tf_op jit(solution)/shard_map/sum_places_0/ppermute | solution.py:43
  442.5 28.2 %collective-permute-start.40 = (bf16[2,128,1024]{2,1,0:T(8,128)(2,1)}, bf16[2,128,1024]{2,1,0:T(8,128)(2,1)}, u32[]{:S(2)}, u32[]{:S(2)}) collective-permute-start(bf16[2,128,1024]{2,1,0:T(8,128)(2,1)} %dynamic-slice_bitcast_fusion.3), channel_id=1, source_target_pairs={{0,8},{8,0},{1,9},{9,1},{2,10},{10,2},{3,11},{11,3},{4,12},{12,4},... | collective-permute-start | bytes 1572872 | tf_op jit(solution)/shard_map/sum_places_0/ppermute | solution.py:43
  443.3 28.6 %collective-permute-start.42 = (bf16[4,128,384]{2,1,0:T(8,128)(2,1)}, bf16[4,128,384]{2,1,0:T(8,128)(2,1)S(1)}, u32[]{:S(2)}, u32[]{:S(2)}) collective-permute-start(bf16[4,128,384]{2,1,0:T(8,128)(2,1)} %get-tuple-element.221), channel_id=1, source_target_pairs={{0,2},{2,0},{1,3},{3,1},{4,6},{6,4},{5,7},{7,5},{8,10},{10,8},{9,1... | collective-permute-start | bytes 1179656 | tf_op jit(solution)/shard_map/grad_attn_far/ppermute | solution.py:43
  473.7 12.3 %collective-permute-start.44 = (bf16[128,1024]{1,0:T(8,128)(2,1)S(1)}, bf16[128,1024]{1,0:T(8,128)(2,1)S(1)}, u32[]{:S(2)}, u32[]{:S(2)}) collective-permute-start(bf16[128,1024]{1,0:T(8,128)(2,1)S(1)} %dynamic-slice_bitcast_fusion.12), channel_id=1, source_target_pairs={{0,8},{8,0},{1,9},{9,1},{2,10},{10,2},{3,11},{11,3},{4,12},{12,4},... | collective-permute-start | bytes 786440 | tf_op jit(solution)/shard_map/sum_places_1/ppermute | solution.py:43
  473.8 14.4 %collective-permute-start.45 = (bf16[64,2048]{1,0:T(8,128)(2,1)S(1)}, bf16[64,2048]{1,0:T(8,128)(2,1)S(1)}, u32[]{:S(2)}, u32[]{:S(2)}) collective-permute-start(bf16[64,2048]{1,0:T(8,128)(2,1)S(1)} %get-tuple-element.251), channel_id=1, source_target_pairs={{0,2},{2,0},{1,3},{3,1},{4,6},{6,4},{5,7},{7,5},{8,10},{10,8},{9,1... | collective-permute-start | bytes 786440 | tf_op jit(solution)/shard_map/grad_out_far/ppermute | solution.py:43
  475.3 39.3 %collective-permute-start.50 = (bf16[64,2048]{1,0:T(8,128)(2,1)S(1)}, bf16[64,2048]{1,0:T(8,128)(2,1)S(1)}, u32[]{:S(2)}, u32[]{:S(2)}) collective-permute-start(bf16[64,2048]{1,0:T(8,128)(2,1)S(1)} %get-tuple-element.271), channel_id=1, source_target_pairs={{0,2},{2,0},{1,3},{3,1},{4,6},{6,4},{5,7},{7,5},{8,10},{10,8},{9,1... | collective-permute-start | bytes 786440 | tf_op jit(solution)/shard_map/grad_out_near/ppermute | solution.py:43
  476.7 54.4 %collective-permute-start.49 = (bf16[4,128,384]{2,1,0:T(8,128)(2,1)}, bf16[4,128,384]{2,1,0:T(8,128)(2,1)}, u32[]{:S(2)}, u32[]{:S(2)}) collective-permute-start(bf16[4,128,384]{2,1,0:T(8,128)(2,1)} %add_convert_fusion.8), channel_id=1, source_target_pairs={{0,16},{16,0},{1,17},{17,1},{2,18},{18,2},{3,19},{19,3},{4,20},{20... | collective-permute-start | bytes 1179656 | tf_op jit(solution)/shard_map/grad_attn_relay/ppermute | solution.py:43
  489.4 42.2 %all-to-all-start.2 = ((bf16[8,64,1408]{2,1,0:T(8,128)(2,1)}), bf16[8,64,1408]{2,1,0:T(8,128)(2,1)S(1)}, u32[]{:S(2)}, u32[]{:S(2)}) async-start(bf16[8,64,1408]{2,1,0:T(8,128)(2,1)} %bitcast.195), calls=%async_computation.3 | async-start | bytes 2883584 | tf_op jit(solution)/shard_map/all_to_all | solution.py:620
  494.2 27.2 %collective-permute-start.51 = (bf16[64,2048]{1,0:T(8,128)(2,1)}, bf16[64,2048]{1,0:T(8,128)(2,1)S(1)}, u32[]{:S(2)}, u32[]{:S(2)}) collective-permute-start(bf16[64,2048]{1,0:T(8,128)(2,1)} %add_convert_fusion.9), channel_id=1, source_target_pairs={{0,16},{16,0},{1,17},{17,1},{2,18},{18,2},{3,19},{19,3},{4,20},{20... | collective-permute-start | bytes 786440 | tf_op jit(solution)/shard_map/grad_out_relay/ppermute | solution.py:43
  497.7 33.4 %collective-permute-start.48 = (bf16[4,128,384]{2,1,0:T(8,128)(2,1)}, bf16[4,128,384]{2,1,0:T(8,128)(2,1)}, u32[]{:S(2)}, u32[]{:S(2)}) collective-permute-start(bf16[4,128,384]{2,1,0:T(8,128)(2,1)} %copy-done.53), channel_id=1, source_target_pairs={{0,2},{2,0},{1,3},{3,1},{4,6},{6,4},{5,7},{7,5},{8,10},{10,8},{9,1... | collective-permute-start | bytes 1179656 | tf_op jit(solution)/shard_map/grad_attn_near/ppermute | solution.py:43
  523.4 30.3 %collective-permute-start.47 = (bf16[64,4096]{1,0:T(8,128)(2,1)}, bf16[64,4096]{1,0:T(8,128)(2,1)}, u32[]{:S(2)}, u32[]{:S(2)}) collective-permute-start(bf16[64,4096]{1,0:T(8,128)(2,1)} %get-tuple-element.293), channel_id=1, source_target_pairs={{0,2},{1,18},{2,0},{3,16},{16,3},{17,19},{18,1},{19,17},{4,6},{5,2... | collective-permute-start | bytes 1572872 | tf_op jit(solution)/shard_map/rows_home/ppermute | solution.py:564
  524.9 28.9 %collective-permute-start.46 = (bf16[64,4096]{1,0:T(8,128)(2,1)}, bf16[64,4096]{1,0:T(8,128)(2,1)}, u32[]{:S(2)}, u32[]{:S(2)}) collective-permute-start(bf16[64,4096]{1,0:T(8,128)(2,1)} %get-tuple-element.294), channel_id=1, source_target_pairs={{0,0},{1,16},{2,2},{3,18},{16,1},{17,17},{18,3},{19,19},{4,4},{5,2... | collective-permute-start | bytes 1572872 | tf_op jit(solution)/shard_map/rows_home/ppermute | solution.py:564
  533.6 25.1 %all-to-all-start.3 = ((bf16[8,64,384]{2,1,0:T(8,128)(2,1)}), bf16[8,64,384]{2,1,0:T(8,128)(2,1)S(1)}, u32[]{:S(2)}, u32[]{:S(2)}) async-start(bf16[8,64,384]{2,1,0:T(8,128)(2,1)} %bitcast.186), calls=%async_computation.4 | async-start | bytes 786432 | tf_op jit(solution)/shard_map/all_to_all | solution.py:620
  (122 other events, 864.7 us)
Sparse Core Ops, SparseCore 0:
  17.6 54.1 all-gather.5
  75.6 71.3 all-gather.11
  149.2 59.7 all-gather.9
  211.3 42.6 all-gather.7
  334.5 42.7 all-gather.13
  429.2 80.1 reduce-scatter.1
